TPU v7x, 256 devices: a whole 4x4x8 slice. The times are simulated.
256 devices in a mesh: blocks: 64 (over x, z, core), cat: 4 (over y).
Axes of the slice: x: 4, y: 4, z: 8, core: 2. Of those that a mesh axis runs over, the one named last changes fastest.
Arguments:
- velocity: float32 [2, 30, 30, 32768], P(None, None, None, ('blocks', 'cat')), may hold values from -6 to 6
- strength: float32 [30, 30, 32768], P(None, None, ('blocks', 'cat')), may hold values from 0.3 to 3
- mass: float32 [30, 30, 32768], P(None, None, ('blocks', 'cat')), may hold values from 0.5 to 2
- ice_cover: int32 [30, 30, 32768], P(None, None, ('blocks', 'cat')), may hold values 0 or 1
- neighbour: int32 [4, 32768], P(None, ('blocks', 'cat')), may hold values from 0 to 32767, as said below
- rotation: int32 [4, 32768], P(None, ('blocks', 'cat')), may hold values from 0 to 3
- concentration: float32 [4, 64, 256, 256], P('cat', 'blocks'), may hold values from 0.05 to 1
- air_wind: float32 [2, 64, 256, 256], P(None, 'blocks'), may hold values from -6 to 6
- ocean_current: float32 [2, 64, 256, 256], P(None, 'blocks'), may hold values from -5 to 5
- drag: float32 [2, 4], P(None, 'cat'), may hold values from 0.3 to 3
- slot_cell: int32 [64, 256, 256], P(None, ('blocks', 'cat')), may hold values from 0 to 115199
- slot_count: int32 [64, 256], P(None, ('blocks', 'cat')), may hold values from 0 to 256, as said below
Outputs:
- moving: float32 [2, 30, 30, 32768], P(None, None, None, ('blocks', 'cat'))
- stress: float32 [3, 30, 30, 32768], P(None, None, None, ('blocks', 'cat'))
Inputs may be any that keep to these rules, and one draw needn't show every extreme that they name: Each block's neighbour across every side lies on its own device or on one of the two adjacent devices in blocks+cat index order, the first and last device counting as adjacent; device d holds blocks d * 128 onward. `slot_count`: some ice device receives 256 live slots from every owner.
All inputs are finite; a program needn't handle non-finite values. No bound on the sum of `ice_cover` on one device may be relied on, other than what follows from the above.
Results may differ from a plain program's by a relative error of at most 0.0003.
Values sent between devices are 32-bit elements; how exact they have to be, the bound alone decides.
No kernel may reach another device: no remote copies, remote signals or barrier semaphores. Data moves between devices by JAX's collectives and lax.ppermute only.
A program may use at most 192 MiB of HBM per device.

v0:
```python
import functools

import jax
import jax.numpy as jnp
from jax import lax
from jax.experimental import pallas as pl
from jax.experimental.pallas import tpu as pltpu
from jax.sharding import PartitionSpec as P

F32 = jnp.float32
BF16 = jnp.bfloat16
I32 = jnp.int32

SIDE = 30
ROWS = 32
LANES = 128
OWNERS = 64
SLOTS = 256
EXTRA = 8
CHUNK = 8
BOTH = ("blocks", "cat")

PARAMS = pltpu.CompilerParams(vmem_limit_bytes=48 * 1024 * 1024)
VMEM = pl.BlockSpec(memory_space=pltpu.VMEM)
SMEM = pl.BlockSpec(memory_space=pltpu.SMEM)


def shape(*dims, dtype=F32):
    return jax.ShapeDtypeStruct(dims, dtype)


def partial_kernel(mine_ref, first_ref, second_ref, third_ref, air_ref, ocean_ref, out_ref):
    parts = (mine_ref, first_ref, second_ref, third_ref)
    air_weight = jnp.zeros((OWNERS, SLOTS), F32)
    ocean_weight = jnp.zeros((OWNERS, SLOTS), F32)
    for part in parts:
        fraction = part[0:OWNERS, :]
        air_weight += fraction * part[OWNERS : OWNERS + 1, :]
        ocean_weight += fraction * part[OWNERS + 1 : OWNERS + 2, :]
    air_east, air_north = air_ref[0], air_ref[1]
    ocean_east, ocean_north = ocean_ref[0], ocean_ref[1]
    air_weight *= jnp.sqrt(air_east * air_east + air_north * air_north)
    ocean_weight *= jnp.sqrt(ocean_east * ocean_east + ocean_north * ocean_north)
    out_ref[:, 0, :] = air_weight * air_east + ocean_weight * ocean_east
    out_ref[:, 1, :] = air_weight * air_north + ocean_weight * ocean_north


def split_lanes(lane_hits, value):
    high = value.astype(BF16).astype(F32)
    return (
        jnp.where(lane_hits, high, 0.0).astype(BF16),
        jnp.where(lane_hits, value - high, 0.0).astype(BF16),
    )


def spread_values(cell_ref, value_ref, count_ref, spread, index, group):
    block = lax.broadcasted_iota(I32, (LANES, SLOTS), 0)
    slot = lax.broadcasted_iota(I32, (1, SLOTS), 1)
    columns = pl.ds(index * SLOTS, SLOTS)
    lane_hits = block == lax.bitwise_and(cell_ref[group], LANES - 1)
    live = slot < count_ref[group]
    for member in range(2):
        value = jnp.where(live, value_ref[group, member : member + 1, :], 0.0)
        high, low = split_lanes(lane_hits, value)
        spread[pl.ds(member * 2 * LANES, LANES), columns] = high
        spread[pl.ds(member * 2 * LANES + LANES, LANES), columns] = low


def cell_place(cell):
    number = lax.shift_right_logical(cell, 7)
    east = lax.shift_right_logical(number * 2185, 16)
    return east, number - east * SIDE


def accumulate(total, hot, spread):
    total[...] += lax.dot_general(
        hot[...], spread[...], (((1,), (1,)), ((), ())), preferred_element_type=F32
    )


def row_kernel(first, last, cell_ref, value_ref, count_ref, out_ref, hot, spread, total):
    step = pl.program_id(0)

    @pl.when(step == 0)
    def _():
        total[...] = jnp.zeros_like(total)

    north_of = lax.broadcasted_iota(I32, (ROWS, SLOTS), 0)
    for index in range(CHUNK):
        east, north = cell_place(cell_ref[index])
        columns = pl.ds(index * SLOTS, SLOTS)
        north_hot = (north_of == north).astype(F32).astype(BF16)
        for i in range(first, last):
            hot[pl.ds((i - first) * ROWS, ROWS), columns] = jnp.where(
                east == i, north_hot, jnp.zeros_like(north_hot)
            )
        spread_values(cell_ref, value_ref, count_ref, spread, index, index)
    accumulate(total, hot, spread)

    @pl.when(step == pl.num_programs(0) - 1)
    def _():
        for member in range(2):
            at = member * 2 * LANES
            summed = total[:, at : at + LANES] + total[:, at + LANES : at + 2 * LANES]
            out_ref[member] = summed.reshape(last - first, ROWS, LANES)


def scatter_rows(cell, value, count, first, last):
    rows = (last - first) * ROWS
    width = CHUNK * SLOTS
    return pl.pallas_call(
        functools.partial(row_kernel, first, last),
        out_shape=shape(2, last - first, ROWS, LANES),
        grid=(OWNERS // CHUNK,),
        in_specs=[
            pl.BlockSpec((CHUNK, 1, SLOTS), lambda k: (k, 0, 0)),
            pl.BlockSpec((CHUNK, 2, SLOTS), lambda k: (k, 0, 0)),
            pl.BlockSpec((CHUNK, 1, 1), lambda k: (k, 0, 0)),
        ],
        out_specs=pl.BlockSpec((2, last - first, ROWS, LANES), lambda k: (0, 0, 0, 0)),
        scratch_shapes=[
            pltpu.VMEM((rows, width), BF16),
            pltpu.VMEM((4 * LANES, width), BF16),
            pltpu.VMEM((rows, 4 * LANES), F32),
        ],
        compiler_params=PARAMS,
        cost_estimate=pl.CostEstimate(
            flops=2 * rows * 4 * LANES * OWNERS * SLOTS, bytes_accessed=1 << 20, transcendentals=0
        ),
    )(cell, value, count)


def gather_rims(strips, place_ref, turn_ref, store):
    for side in range(4):
        place = place_ref[side : side + 1, :]
        turns = turn_ref[side : side + 1, :]
        source = lax.bitwise_and(turns + (side + 2), 3)
        holder = lax.shift_right_logical(place, 7)
        lane = jnp.broadcast_to(lax.bitwise_and(place, LANES - 1), (ROWS, LANES))
        rows = [jnp.zeros((ROWS, LANES), F32) for _ in range(2)]
        for where, ref in enumerate(strips):
            for edge in range(4):
                hits = jnp.broadcast_to((holder == where) & (source == edge), (ROWS, LANES))
                for member in range(2):
                    picked = jnp.take_along_axis(
                        ref[member, edge], lane, axis=1, mode="promise_in_bounds"
                    )
                    rows[member] = jnp.where(hits, picked, rows[member])
        store(side, turns, rows)


def turned_vector(turns, rows):
    cosine = (turns == 0).astype(F32) - (turns == 2).astype(F32)
    sine = (turns == 1).astype(F32) - (turns == 3).astype(F32)
    return cosine * rows[0] - sine * rows[1], sine * rows[0] + cosine * rows[1]


def turned_stress(turns, rows):
    parity = (1 - 2 * lax.bitwise_and(turns, 1)).astype(F32)
    return rows[0], parity * rows[1]


def store_rim(pad, member, side, rim):
    if side == 0 or side == 2:
        pad[member, 0 if side == 0 else SIDE + 1, 8 : 8 + SIDE, :] = rim[0:SIDE]
    else:
        column = 7 if side == 1 else 8 + SIDE
        for i in range(SIDE):
            pad[member, i + 1, column : column + 1, :] = rim[i : i + 1]


def store_strips(out_ref, member, cell_of):
    out_ref[member, :, SIDE:ROWS, :] = jnp.zeros((4, ROWS - SIDE, LANES), F32)
    out_ref[member, 0, 0:SIDE, :] = cell_of(0, slice(0, SIDE))
    out_ref[member, 2, 0:SIDE, :] = cell_of(SIDE - 1, slice(0, SIDE))
    for i in range(SIDE):
        out_ref[member, 1, i : i + 1, :] = cell_of(i, slice(0, 1))
        out_ref[member, 3, i : i + 1, :] = cell_of(i, slice(SIDE - 1, SIDE))


def first_strips_kernel(velocity_ref, cover_ref, out_ref):
    for member in range(2):
        store_strips(
            out_ref,
            member,
            lambda i, j: velocity_ref[member, i, j, :] * cover_ref[i, j, :].astype(F32),
        )


def derivatives(pad, member, i):
    middle = slice(8, 8 + SIDE)
    east = 0.5 * (pad[member, i + 2, middle, :] - pad[member, i, middle, :])
    north = 0.5 * (pad[member, i + 1, 9 : 9 + SIDE, :] - pad[member, i + 1, 7 : 7 + SIDE, :])
    return east, north


def stress_targets(pad, strength, i):
    east_e, east_n = derivatives(pad, 0, i)
    north_e, north_n = derivatives(pad, 1, i)
    divergence = east_e + north_n
    tension = east_e - north_n
    shearing = east_n + north_e
    inverse = lax.rsqrt(
        divergence * divergence + (tension * tension + shearing * shearing) * 0.25 + 0.25
    )
    scaled = strength * inverse
    return (
        divergence * scaled - strength,
        0.25 * (tension * scaled),
        0.125 * (shearing * scaled),
    )


def face_strips(stress_ref, out_ref):
    out_ref[:, :, SIDE:ROWS, :] = jnp.zeros((2, 4, ROWS - SIDE, LANES), F32)
    for side, i in ((0, 0), (2, SIDE - 1)):
        out_ref[0, side, 0:SIDE, :] = 0.5 * (stress_ref[0, i] + stress_ref[1, i])
        out_ref[1, side, 0:SIDE, :] = stress_ref[2, i]
    for side, j in ((1, 0), (3, SIDE - 1)):
        for i in range(SIDE):
            cell = pl.ds(j, 1)
            out_ref[0, side, i : i + 1, :] = 0.5 * (
                stress_ref[0, i, cell, :] - stress_ref[1, i, cell, :]
            )
            out_ref[1, side, i : i + 1, :] = stress_ref[2, i, cell, :]


def stress_kernel(
    first,
    before_ref,
    own_ref,
    after_ref,
    place_ref,
    turn_ref,
    velocity_ref,
    cover_ref,
    strength_ref,
    *rest,
):
    if first:
        stress_ref, out_strips_ref, pad = rest
    else:
        old_ref, stress_ref, out_strips_ref, pad = rest

    def fill(i, carry):
        covered = cover_ref[i].astype(F32) if first else 1.0
        for member in range(2):
            pad[member, i + 1, 8 : 8 + SIDE, :] = velocity_ref[member, i] * covered
        return carry

    lax.fori_loop(0, SIDE, fill, 0, unroll=True)

    def store(side, turns, rows):
        for member, rim in enumerate(turned_vector(turns, rows)):
            store_rim(pad, member, side, rim)

    gather_rims((before_ref, own_ref, after_ref), place_ref, turn_ref, store)
    for i in range(SIDE):
        targets = stress_targets(pad, strength_ref[i], i)
        for member in range(3):
            old = 0.0 if first else old_ref[member, i]
            stress_ref[member, i] = old + 0.5 * (targets[member] - old)
    face_strips(stress_ref, out_strips_ref)


def moving_kernel(
    first,
    before_ref,
    own_ref,
    after_ref,
    place_ref,
    turn_ref,
    velocity_ref,
    cover_ref,
    mass_ref,
    stress_ref,
    forcing_ref,
    *rest,
):
    if first:
        out_ref, out_strips_ref, pad = rest
    else:
        out_ref, pad = rest
    for i in range(SIDE):
        first_stress, second_stress = stress_ref[0, i], stress_ref[1, i]
        pad[0, i + 1, 8 : 8 + SIDE, :] = 0.5 * (first_stress + second_stress)
        pad[1, i + 1, 8 : 8 + SIDE, :] = stress_ref[2, i]
        pad[2, i + 1, 8 : 8 + SIDE, :] = 0.5 * (first_stress - second_stress)

    def store(side, turns, rows):
        normal, shear = turned_stress(turns, rows)
        store_rim(pad, 0 if side in (0, 2) else 2, side, normal)
        store_rim(pad, 1, side, shear)

    gather_rims((before_ref, own_ref, after_ref), place_ref, turn_ref, store)
    middle = slice(8, 8 + SIDE)
    upper, lower = slice(9, 9 + SIDE), slice(7, 7 + SIDE)
    for i in range(SIDE):
        shear_east, shear_north = derivatives(pad, 1, i)
        force_east = 0.5 * (pad[0, i + 2, middle, :] - pad[0, i, middle, :]) + shear_north
        force_north = shear_east + 0.5 * (pad[2, i + 1, upper, :] - pad[2, i + 1, lower, :])
        covered = cover_ref[i].astype(F32)
        eastward, northward = velocity_ref[0, i], velocity_ref[1, i]
        if first:
            eastward, northward = eastward * covered, northward * covered
        mass = mass_ref[i]
        weight = covered / (4.0 * mass + 1.0)
        out_ref[0, i] = weight * (
            mass * (4.0 * eastward + 0.5 * northward) + force_east + forcing_ref[0, i, 0:SIDE, :]
        )
        out_ref[1, i] = weight * (
            mass * (4.0 * northward - 0.5 * eastward) + force_north + forcing_ref[1, i, 0:SIDE, :]
        )
    if first:
        for member in range(2):
            store_strips(out_strips_ref, member, lambda i, j: out_ref[member, i, j, :])


def call(kernel, outs, *args, specs=None, scratch=(), work=1 << 22):
    return pl.pallas_call(
        kernel,
        out_shape=outs,
        in_specs=specs or [VMEM] * len(args),
        out_specs=jax.tree.map(lambda _: VMEM, outs),
        scratch_shapes=list(scratch),
        compiler_params=PARAMS,
        cost_estimate=pl.CostEstimate(flops=work, bytes_accessed=1 << 22, transcendentals=0),
    )(*args)


def shards(
    velocity,
    strength,
    mass,
    ice_cover,
    neighbour,
    rotation,
    concentration,
    air_wind,
    ocean_current,
    drag,
    slot_cell,
    slot_count,
):
    devices = lax.axis_size(BOTH)
    here = lax.axis_index(BOTH)
    cat = lax.axis_index("cat")
    ring = [(i, (i + 1) % devices) for i in range(devices)]
    back = [(j, i) for i, j in ring]

    def both_ways(strips):
        return lax.ppermute(strips, BOTH, ring), lax.ppermute(strips, BOTH, back)

    strip_shape = shape(2, 4, ROWS, LANES)
    block = (SIDE, SIDE, LANES)

    fractions = concentration.reshape(OWNERS, 4, SLOTS)
    coefficients = jnp.broadcast_to(jnp.tile(drag, (EXTRA // 2, 1)), (EXTRA, SLOTS))

    def share_of(receiver):
        return jnp.concatenate(
            [lax.dynamic_index_in_dim(fractions, receiver, 1, keepdims=False), coefficients]
        )

    parts = [share_of(cat)]
    for step in (1, 2, 3):
        parts.append(
            lax.ppermute(
                share_of(lax.rem(cat + step, 4)), "cat", [(i, (i + step) % 4) for i in range(4)]
            )
        )
    winds = [
        lax.dynamic_index_in_dim(q.reshape(2, OWNERS, 4, SLOTS), cat, 2, keepdims=False)
        for q in (air_wind, ocean_current)
    ]
    summed = call(partial_kernel, shape(OWNERS, 2, SLOTS), *parts, *winds)
    arrived = lax.all_to_all(summed, "blocks", split_axis=0, concat_axis=0, tiled=True)

    place = lax.bitwise_and(neighbour - (here - 1) * LANES, devices * LANES - 1)
    strips = call(first_strips_kernel, strip_shape, velocity, ice_cover)
    before, after = both_ways(strips)
    pad2 = [pltpu.VMEM((2, ROWS, 48, LANES), F32)]
    pad3 = [pltpu.VMEM((3, ROWS, 48, LANES), F32)]
    stress, faces = call(
        functools.partial(stress_kernel, True),
        (shape(3, *block), strip_shape),
        before, strips, after, place, rotation, velocity, ice_cover, strength,
        scratch=pad2,
    )
    before, after = both_ways(faces)

    forcing = scatter_rows(slot_cell, arrived, slot_count[:, :, None], 0, SIDE)

    moving, strips = call(
        functools.partial(moving_kernel, True),
        (shape(2, *block), strip_shape),
        before, faces, after, place, rotation, velocity, ice_cover, mass, stress, forcing,
        scratch=pad3,
    )
    before, after = both_ways(strips)
    stress, faces = call(
        functools.partial(stress_kernel, False),
        (shape(3, *block), strip_shape),
        before, strips, after, place, rotation, moving, ice_cover, strength, stress,
        scratch=pad2,
    )
    before, after = both_ways(faces)
    moving = call(
        functools.partial(moving_kernel, False),
        shape(2, *block),
        before, faces, after, place, rotation, moving, ice_cover, mass, stress, forcing,
        scratch=pad3,
    )
    return (moving, stress)


def solution(mesh):
    placed = (
        P(None, None, None, BOTH),
        P(None, None, BOTH),
        P(None, None, BOTH),
        P(None, None, BOTH),
        P(None, BOTH),
        P(None, BOTH),
        P("cat", "blocks", None, None),
        P(None, "blocks", None, None),
        P(None, "blocks", None, None),
        P(None, "cat"),
        P(None, BOTH, None),
        P(None, BOTH),
    )
    return jax.shard_map(
        shards,
        mesh=mesh,
        in_specs=placed,
        out_specs=(P(None, None, None, BOTH), P(None, None, None, BOTH)),
        check_vma=False,
    )
```

profile of v0, /device:TPU:0, one launch (start us, length us, event | category | flops | bytes accessed | tf_op | source)
XLA Modules:
  0.0 101.6 jit_solution(11886098376423954481)
XLA Ops:
  0.6 0.0 copy-start.13
  0.7 0.7 tile.12
  1.4 0.1 reshape.22
  1.5 1.0 %reshape.19 = f32[64,4,256]{2,1,0:T(4,128)S(1)} reshape(f32[1,1,256,256]{3,2,1,0:T(8,128)} %param.18) | data formatting | bytes 524288 | tf_op jit(solution)/shard_map/reshape | solution.py:357
  2.5 0.0 copy-start.14
  2.5 0.1 pad.7.clone
  2.6 0.2 constant_dynamic-slice_fusion.2
  2.9 0.1 pad_maximum_fusion.3
  3.0 1.4 %collective-permute-start.6 = (f32[72,256]{1,0:T(8,128)S(1)}, f32[72,256]{1,0:T(8,128)S(1)}, u32[]{:S(2)}, u32[]{:S(2)}) collective-permute-start(f32[72,256]{1,0:T(8,128)S(1)} %get-tuple-element.22), channel_id=1, source_target_pairs={{0,3},{1,0},{2,1},{3,2},{4,7},{5,4},{6,5},{7,6},{8,11},{9,8},{10,9... | collective-permute-start | bytes 221192 | tf_op jit(solution)/shard_map/ppermute | solution.py:368
  4.3 0.7 collective-permute-start.4
  5.1 1.5 %collective-permute-start.5 = (f32[72,256]{1,0:T(8,128)S(1)}, f32[72,256]{1,0:T(8,128)S(1)}, u32[]{:S(2)}, u32[]{:S(2)}) collective-permute-start(f32[72,256]{1,0:T(8,128)S(1)} %get-tuple-element.24), channel_id=1, source_target_pairs={{0,2},{1,3},{2,0},{3,1},{4,6},{5,7},{6,4},{7,5},{8,10},{9,11},{10,... | collective-permute-start | bytes 221192 | tf_op jit(solution)/shard_map/ppermute | solution.py:368
  6.5 0.0 copy-done.13
  6.5 0.1 reshape.20
  6.7 0.0 copy-done.14
  6.7 0.0 copy-start.12
  6.7 0.1 reshape.21
  6.8 0.3 constant_dynamic-slice_fusion
  7.2 0.0 copy-start
  7.2 0.2 collective-permute-done.6.third_ref
  7.4 2.7 %collective-permute-done.4.first_ref = f32[72,256]{1,0:T(8,128)S(1)} collective-permute-done((f32[72,256]{1,0:T(8,128)S(1)}, f32[72,256]{1,0:T(8,128)S(1)}, u32[]{:S(2)}, u32[]{:S(2)}) %collective-permute-start.4) | collective-permute-done | bytes 73760 | tf_op jit(solution)/shard_map/ppermute | solution.py:368
  10.1 0.9 collective-permute-done.5.second_ref
  10.9 0.8 shard_map.133
  11.7 12.1 %all-to-all-start = ((f32[64,2,256]{2,1,0:T(2,128)}), f32[64,2,256]{2,1,0:T(2,128)}, u32[]{:S(2)}, u32[]{:S(2)}) async-start(f32[64,2,256]{2,1,0:T(2,128)} %shard_map.133), calls=%async_computation | async-start | bytes 262144 | tf_op jit(solution)/shard_map/all_to_all | solution.py:377
  23.8 0.0 copy-done.12
  23.8 0.0 copy-start.16
  23.9 0.0 copy-start.15
  23.9 0.0 copy-start.1
  23.9 0.0 copy-start.10
  23.9 0.1 copy.25.velocity_ref
  24.0 0.0 copy-done
  24.0 0.0 copy-start.11
  24.1 0.1 shard_map.131.own_ref
  24.1 6.9 %collective-permute-start.1 = (f32[2,4,32,128]{3,2,1,0:T(8,128)S(1)}, f32[2,4,32,128]{3,2,1,0:T(8,128)S(1)}, u32[]{:S(2)}, u32[]{:S(2)}) collective-permute-start(f32[2,4,32,128]{3,2,1,0:T(8,128)S(1)} %shard_map.131.own_ref), channel_id=1, source_target_pairs={{1,0},{2,1},{3,2},{4,3},{5,4},{6,5},{7,6},{8,7},{9,8},{10,9},{11,1... | collective-permute-start | bytes 393224 | tf_op jit(solution)/shard_map/ppermute | solution.py:352
  31.1 0.0 collective-permute-start
  31.1 0.7 copy-done.4
  31.7 0.1 copy.33.count_ref
  31.8 1.8 %collective-permute-done.1.after_ref = f32[2,4,32,128]{3,2,1,0:T(8,128)S(1)} collective-permute-done((f32[2,4,32,128]{3,2,1,0:T(8,128)S(1)}, f32[2,4,32,128]{3,2,1,0:T(8,128)S(1)}, u32[]{:S(2)}, u32[]{:S(2)}) %collective-permute-start.1) | collective-permute-done | bytes 131104 | tf_op jit(solution)/shard_map/ppermute | solution.py:352
  33.6 0.7 copy-done.6
  34.3 6.6 %collective-permute-done.before_ref = f32[2,4,32,128]{3,2,1,0:T(8,128)S(1)} collective-permute-done((f32[2,4,32,128]{3,2,1,0:T(8,128)S(1)}, f32[2,4,32,128]{3,2,1,0:T(8,128)S(1)}, u32[]{:S(2)}, u32[]{:S(2)}) %collective-permute-start) | collective-permute-done | bytes 131104 | tf_op jit(solution)/shard_map/ppermute | solution.py:352
  40.9 0.7 copy-done.8
  41.6 0.0 copy-done.10
  41.6 0.9 copy-done.5
  42.5 0.9 copy-done.7
  43.4 0.9 copy-done.9
  44.3 1.7 %shard_map.132 = (f32[3,30,30,128]{3,2,1,0:T(8,128)S(1)}, f32[2,4,32,128]{3,2,1,0:T(8,128)}) custom-call(f32[2,4,32,128]{3,2,1,0:T(8,128)S(1)} %copy-done.9, f32[2,4,32,128]{3,2,1,0:T(8,128)S(1)} %copy-done.5, f32[2,4,32,128]{3,2,1,0:T(8,128)S(1)} %copy-done.7, s32[4,128]{1,0:T(4,128)S(1)} %subtract_and_fusion.place_ref, s32[4,128]{1,0:T(4,128)S(1)} %copy-done.10, ...), custom_call_target="tpu_custom_call" | custom-call | flops 4194304 | bytes 4194304 | tf_op jit(solution)/shard_map/pallas_call | solution.py:320
  46.0 0.7 collective-permute-start.3
  46.6 1.4 %collective-permute-start.2 = (f32[2,4,32,128]{3,2,1,0:T(8,128)}, f32[2,4,32,128]{3,2,1,0:T(8,128)}, u32[]{:S(2)}, u32[]{:S(2)}) collective-permute-start(f32[2,4,32,128]{3,2,1,0:T(8,128)} %get-tuple-element.8.own_ref), channel_id=1, source_target_pairs={{0,1},{1,2},{2,3},{3,4},{4,5},{5,6},{6,7},{7,8},{8,9},{9,10},{10,1... | collective-permute-start | bytes 393224 | tf_op jit(solution)/shard_map/ppermute | solution.py:352
  48.0 0.0 all-to-all-done.value_ref
  48.0 19.6 %shard_map.134.forcing_ref = f32[2,30,32,128]{3,2,1,0:T(8,128)S(1)} custom-call(s32[64,1,256]{2,1,0:T(1,128)S(1)} %copy-done.11, f32[64,2,256]{2,1,0:T(2,128)} %all-to-all-done.value_ref, s32[64,1,1]{2,1,0:T(1,128)S(1)} %copy.33.count_ref), custom_call_target="tpu_custom_call" | custom-call | flops 16106127360 | bytes 1048576 | tf_op jit(solution)/shard_map/pallas_call | solution.py:111
  67.6 0.0 collective-permute-done.3.after_ref
  67.6 0.0 collective-permute-done.2.before_ref
  67.6 2.1 %shard_map.135 = (f32[2,30,30,128]{3,2,1,0:T(8,128)S(1)}, f32[2,4,32,128]{3,2,1,0:T(8,128)S(1)}) custom-call(f32[2,4,32,128]{3,2,1,0:T(8,128)} %collective-permute-done.2.before_ref, f32[2,4,32,128]{3,2,1,0:T(8,128)} %get-tuple-element.8.own_ref, f32[2,4,32,128]{3,2,1,0:T(8,128)} %collective-permute-done.3.after_ref, ...), custom_call_target="tpu_custom_call" | custom-call | flops 4194304 | bytes 4194304 | tf_op jit(solution)/shard_map/pallas_call | solution.py:320
  69.7 5.9 %collective-permute-start.8 = (f32[2,4,32,128]{3,2,1,0:T(8,128)S(1)}, f32[2,4,32,128]{3,2,1,0:T(8,128)S(1)}, u32[]{:S(2)}, u32[]{:S(2)}) collective-permute-start(f32[2,4,32,128]{3,2,1,0:T(8,128)S(1)} %get-tuple-element.10.own_ref), channel_id=1, source_target_pairs={{1,0},{2,1},{3,2},{4,3},{5,4},{6,5},{7,6},{8,7},{9,8},{10,9},{11,1... | collective-permute-start | bytes 393224 | tf_op jit(solution)/shard_map/ppermute | solution.py:352
  75.6 0.0 collective-permute-start.7
  75.6 2.5 %collective-permute-done.8.after_ref = f32[2,4,32,128]{3,2,1,0:T(8,128)S(1)} collective-permute-done((f32[2,4,32,128]{3,2,1,0:T(8,128)S(1)}, f32[2,4,32,128]{3,2,1,0:T(8,128)S(1)}, u32[]{:S(2)}, u32[]{:S(2)}) %collective-permute-start.8) | collective-permute-done | bytes 131104 | tf_op jit(solution)/shard_map/ppermute | solution.py:352
  78.2 7.3 %collective-permute-done.7.before_ref = f32[2,4,32,128]{3,2,1,0:T(8,128)S(1)} collective-permute-done((f32[2,4,32,128]{3,2,1,0:T(8,128)S(1)}, f32[2,4,32,128]{3,2,1,0:T(8,128)S(1)}, u32[]{:S(2)}, u32[]{:S(2)}) %collective-permute-start.7) | collective-permute-done | bytes 131104 | tf_op jit(solution)/shard_map/ppermute | solution.py:352
  85.5 2.2 %shard_map.136 = (f32[3,30,30,128]{3,2,1,0:T(8,128)}, f32[2,4,32,128]{3,2,1,0:T(8,128)S(1)}) custom-call(f32[2,4,32,128]{3,2,1,0:T(8,128)S(1)} %collective-permute-done.7.before_ref, f32[2,4,32,128]{3,2,1,0:T(8,128)S(1)} %get-tuple-element.10.own_ref, f32[2,4,32,128]{3,2,1,0:T(8,128)S(1)} %collective-permute-done.8.after_ref, ...), custom_call_target="tpu_custom_call" | custom-call | flops 4194304 | bytes 4194304 | tf_op jit(solution)/shard_map/pallas_call | solution.py:320
  87.7 0.0 collective-permute-start.10
  87.7 2.0 %collective-permute-start.9 = (f32[2,4,32,128]{3,2,1,0:T(8,128)S(1)}, f32[2,4,32,128]{3,2,1,0:T(8,128)S(1)}, u32[]{:S(2)}, u32[]{:S(2)}) collective-permute-start(f32[2,4,32,128]{3,2,1,0:T(8,128)S(1)} %get-tuple-element.12.own_ref), channel_id=1, source_target_pairs={{0,1},{1,2},{2,3},{3,4},{4,5},{5,6},{6,7},{7,8},{8,9},{9,10},{10,1... | collective-permute-start | bytes 393224 | tf_op jit(solution)/shard_map/ppermute | solution.py:352
  89.7 2.9 %collective-permute-done.10.after_ref = f32[2,4,32,128]{3,2,1,0:T(8,128)S(1)} collective-permute-done((f32[2,4,32,128]{3,2,1,0:T(8,128)S(1)}, f32[2,4,32,128]{3,2,1,0:T(8,128)S(1)}, u32[]{:S(2)}, u32[]{:S(2)}) %collective-permute-start.10) | collective-permute-done | bytes 131104 | tf_op jit(solution)/shard_map/ppermute | solution.py:352
  92.7 4.9 %collective-permute-done.9.before_ref = f32[2,4,32,128]{3,2,1,0:T(8,128)S(1)} collective-permute-done((f32[2,4,32,128]{3,2,1,0:T(8,128)S(1)}, f32[2,4,32,128]{3,2,1,0:T(8,128)S(1)}, u32[]{:S(2)}, u32[]{:S(2)}) %collective-permute-start.9) | collective-permute-done | bytes 131104 | tf_op jit(solution)/shard_map/ppermute | solution.py:352
  97.5 1.4 %copy-done.3 = f32[3,30,30,128]{3,2,1,0:T(8,128)S(1)} copy-done((f32[3,30,30,128]{3,2,1,0:T(8,128)S(1)}, f32[3,30,30,128]{3,2,1,0:T(8,128)}, u32[]{:S(2)}) %copy-start.3) | copy-done | bytes 1382424
  98.9 1.0 shard_map.137
  99.9 1.6 %copy.35 = f32[2,30,30,128]{3,0,2,1:T(2,128)} copy(f32[2,30,30,128]{3,2,1,0:T(8,128)S(1)} %shard_map.137) | data formatting | bytes 1843200
  (18 shorter events, 0.1 us)
Async XLA Ops:
  0.6 5.9 %copy-start.13 = (f32[2,1,256,256]{3,2,1,0:T(8,128)S(1)}, f32[2,1,256,256]{3,2,1,0:T(8,128)}, u32[]{:S(2)}) copy-start(f32[2,1,256,256]{3,2,1,0:T(8,128)} %param.19) | copy-start | bytes 1572868
  2.5 4.2 %copy-start.14 = (f32[2,1,256,256]{3,2,1,0:T(8,128)S(1)}, f32[2,1,256,256]{3,2,1,0:T(8,128)}, u32[]{:S(2)}) copy-start(f32[2,1,256,256]{3,2,1,0:T(8,128)} %param.20) | copy-start | bytes 1572868
  3.0 4.4 %collective-permute-start.6 = (f32[72,256]{1,0:T(8,128)S(1)}, f32[72,256]{1,0:T(8,128)S(1)}, u32[]{:S(2)}, u32[]{:S(2)}) collective-permute-start(f32[72,256]{1,0:T(8,128)S(1)} %get-tuple-element.22), channel_id=1, source_target_pairs={{0,3},{1,0},{2,1},{3,2},{4,7},{5,4},{6,5},{7,6},{8,11},{9,8},{10,9... | collective-permute-start | bytes 221192 | tf_op jit(solution)/shard_map/ppermute | solution.py:368
  4.3 5.8 %collective-permute-start.4 = (f32[72,256]{1,0:T(8,128)S(1)}, f32[72,256]{1,0:T(8,128)S(1)}, u32[]{:S(2)}, u32[]{:S(2)}) collective-permute-start(f32[72,256]{1,0:T(8,128)S(1)} %get-tuple-element.23), channel_id=1, source_target_pairs={{0,1},{1,2},{2,3},{3,0},{4,5},{5,6},{6,7},{7,4},{8,9},{9,10},{10,1... | collective-permute-start | bytes 221192 | tf_op jit(solution)/shard_map/ppermute | solution.py:368
  5.1 5.9 %collective-permute-start.5 = (f32[72,256]{1,0:T(8,128)S(1)}, f32[72,256]{1,0:T(8,128)S(1)}, u32[]{:S(2)}, u32[]{:S(2)}) collective-permute-start(f32[72,256]{1,0:T(8,128)S(1)} %get-tuple-element.24), channel_id=1, source_target_pairs={{0,2},{1,3},{2,0},{3,1},{4,6},{5,7},{6,4},{7,5},{8,10},{9,11},{10,... | collective-permute-start | bytes 221192 | tf_op jit(solution)/shard_map/ppermute | solution.py:368
  6.7 17.2 %copy-start.12 = (f32[2,30,30,128]{3,0,2,1:T(2,128)S(1)}, f32[2,30,30,128]{3,0,2,1:T(2,128)}, u32[]{:S(2)}) copy-start(f32[2,30,30,128]{3,0,2,1:T(2,128)} %param.12) | copy-start | bytes 2764804
  7.2 16.9 %copy-start = (s32[30,30,128]{2,1,0:T(8,128)S(1)}, s32[30,30,128]{2,1,0:T(8,128)}, u32[]{:S(2)}) copy-start(s32[30,30,128]{2,1,0:T(8,128)} %cover_ref.9) | copy-start | bytes 1382404
  11.7 36.3 %all-to-all-start = ((f32[64,2,256]{2,1,0:T(2,128)}), f32[64,2,256]{2,1,0:T(2,128)}, u32[]{:S(2)}, u32[]{:S(2)}) async-start(f32[64,2,256]{2,1,0:T(2,128)} %shard_map.133), calls=%async_computation | async-start | bytes 262144 | tf_op jit(solution)/shard_map/all_to_all | solution.py:377
  23.8 7.9 %copy-start.16 = (s32[64,1]{0,1:T(1,128)S(1)}, s32[64,1]{0,1:T(1,128)}, u32[]{:S(2)}) copy-start(s32[64,1]{0,1:T(1,128)} %param.23) | copy-start | bytes 772
  23.9 8.0 %copy-start.15 = (s32[4,128]{1,0:T(4,128)S(1)}, s32[4,128]{1,0:T(4,128)}, u32[]{:S(2)}) copy-start(s32[4,128]{1,0:T(4,128)} %param.16) | copy-start | bytes 6148
  23.9 17.7 %copy-start.1 = (f32[30,30,128]{2,1,0:T(8,128)S(1)}, f32[30,30,128]{2,1,0:T(8,128)}, u32[]{:S(2)}) copy-start(f32[30,30,128]{2,1,0:T(8,128)} %strength_ref.3) | copy-start | bytes 1382404
  23.9 17.7 %copy-start.10 = (s32[4,128]{1,0:T(4,128)S(1)}, s32[4,128]{1,0:T(4,128)}, u32[]{:S(2)}) copy-start(s32[4,128]{1,0:T(4,128)} %turn_ref.7) | copy-start | bytes 6148
  24.0 23.9 %copy-start.11 = (s32[64,1,256]{2,1,0:T(1,128)S(1)}, s32[64,1,256]{2,1,0:T(1,128)}, u32[]{:S(2)}) copy-start(s32[64,1,256]{2,1,0:T(1,128)} %cell_ref.1) | copy-start | bytes 196612
  24.1 9.5 %collective-permute-start.1 = (f32[2,4,32,128]{3,2,1,0:T(8,128)S(1)}, f32[2,4,32,128]{3,2,1,0:T(8,128)S(1)}, u32[]{:S(2)}, u32[]{:S(2)}) collective-permute-start(f32[2,4,32,128]{3,2,1,0:T(8,128)S(1)} %shard_map.131.own_ref), channel_id=1, source_target_pairs={{1,0},{2,1},{3,2},{4,3},{5,4},{6,5},{7,6},{8,7},{9,8},{10,9},{11,1... | collective-permute-start | bytes 393224 | tf_op jit(solution)/shard_map/ppermute | solution.py:352
  31.1 9.8 %collective-permute-start = (f32[2,4,32,128]{3,2,1,0:T(8,128)S(1)}, f32[2,4,32,128]{3,2,1,0:T(8,128)S(1)}, u32[]{:S(2)}, u32[]{:S(2)}) collective-permute-start(f32[2,4,32,128]{3,2,1,0:T(8,128)S(1)} %shard_map.131.own_ref), channel_id=1, source_target_pairs={{0,1},{1,2},{2,3},{3,4},{4,5},{5,6},{6,7},{7,8},{8,9},{9,10},{10,1... | collective-permute-start | bytes 393224 | tf_op jit(solution)/shard_map/ppermute | solution.py:352
  31.1 0.7 copy-start.4
  33.6 0.7 copy-start.6
  40.9 0.7 copy-start.8
  41.6 0.9 copy-start.5
  42.5 0.9 copy-start.7
  43.4 0.9 copy-start.9
  46.0 21.6 %collective-permute-start.3 = (f32[2,4,32,128]{3,2,1,0:T(8,128)}, f32[2,4,32,128]{3,2,1,0:T(8,128)}, u32[]{:S(2)}, u32[]{:S(2)}) collective-permute-start(f32[2,4,32,128]{3,2,1,0:T(8,128)} %get-tuple-element.8.own_ref), channel_id=1, source_target_pairs={{1,0},{2,1},{3,2},{4,3},{5,4},{6,5},{7,6},{8,7},{9,8},{10,9},{11,1... | collective-permute-start | bytes 393224 | tf_op jit(solution)/shard_map/ppermute | solution.py:352
  46.6 21.0 %collective-permute-start.2 = (f32[2,4,32,128]{3,2,1,0:T(8,128)}, f32[2,4,32,128]{3,2,1,0:T(8,128)}, u32[]{:S(2)}, u32[]{:S(2)}) collective-permute-start(f32[2,4,32,128]{3,2,1,0:T(8,128)} %get-tuple-element.8.own_ref), channel_id=1, source_target_pairs={{0,1},{1,2},{2,3},{3,4},{4,5},{5,6},{6,7},{7,8},{8,9},{9,10},{10,1... | collective-permute-start | bytes 393224 | tf_op jit(solution)/shard_map/ppermute | solution.py:352
  48.0 19.6 %copy-start.2 = (f32[30,30,128]{2,1,0:T(8,128)S(1)}, f32[30,30,128]{2,1,0:T(8,128)}, u32[]{:S(2)}) copy-start(f32[30,30,128]{2,1,0:T(8,128)} %mass_ref.3) | copy-start | bytes 1382404
  69.7 8.4 %collective-permute-start.8 = (f32[2,4,32,128]{3,2,1,0:T(8,128)S(1)}, f32[2,4,32,128]{3,2,1,0:T(8,128)S(1)}, u32[]{:S(2)}, u32[]{:S(2)}) collective-permute-start(f32[2,4,32,128]{3,2,1,0:T(8,128)S(1)} %get-tuple-element.10.own_ref), channel_id=1, source_target_pairs={{1,0},{2,1},{3,2},{4,3},{5,4},{6,5},{7,6},{8,7},{9,8},{10,9},{11,1... | collective-permute-start | bytes 393224 | tf_op jit(solution)/shard_map/ppermute | solution.py:352
  75.6 9.8 %collective-permute-start.7 = (f32[2,4,32,128]{3,2,1,0:T(8,128)S(1)}, f32[2,4,32,128]{3,2,1,0:T(8,128)S(1)}, u32[]{:S(2)}, u32[]{:S(2)}) collective-permute-start(f32[2,4,32,128]{3,2,1,0:T(8,128)S(1)} %get-tuple-element.10.own_ref), channel_id=1, source_target_pairs={{0,1},{1,2},{2,3},{3,4},{4,5},{5,6},{6,7},{7,8},{8,9},{9,10},{10,1... | collective-permute-start | bytes 393224 | tf_op jit(solution)/shard_map/ppermute | solution.py:352
  87.7 5.0 %collective-permute-start.10 = (f32[2,4,32,128]{3,2,1,0:T(8,128)S(1)}, f32[2,4,32,128]{3,2,1,0:T(8,128)S(1)}, u32[]{:S(2)}, u32[]{:S(2)}) collective-permute-start(f32[2,4,32,128]{3,2,1,0:T(8,128)S(1)} %get-tuple-element.12.own_ref), channel_id=1, source_target_pairs={{1,0},{2,1},{3,2},{4,3},{5,4},{6,5},{7,6},{8,7},{9,8},{10,9},{11,1... | collective-permute-start | bytes 393224 | tf_op jit(solution)/shard_map/ppermute | solution.py:352
  87.7 9.8 %collective-permute-start.9 = (f32[2,4,32,128]{3,2,1,0:T(8,128)S(1)}, f32[2,4,32,128]{3,2,1,0:T(8,128)S(1)}, u32[]{:S(2)}, u32[]{:S(2)}) collective-permute-start(f32[2,4,32,128]{3,2,1,0:T(8,128)S(1)} %get-tuple-element.12.own_ref), channel_id=1, source_target_pairs={{0,1},{1,2},{2,3},{3,4},{4,5},{5,6},{6,7},{7,8},{8,9},{9,10},{10,1... | collective-permute-start | bytes 393224 | tf_op jit(solution)/shard_map/ppermute | solution.py:352
  97.5 1.4 %copy-start.3 = (f32[3,30,30,128]{3,2,1,0:T(8,128)S(1)}, f32[3,30,30,128]{3,2,1,0:T(8,128)}, u32[]{:S(2)}) copy-start(f32[3,30,30,128]{3,2,1,0:T(8,128)} %get-tuple-element.17.stress_ref) | copy-start | bytes 4147204
where the time goes:
time: 102 us
  starting transfers between devices  32.6 us (32%)
  waiting for transfers between devices  29.8 us (29%)
  Pallas kernels  27.5 us (27%)
  local copies, waits for them, and re-layouts  10.7 us (10%)
    ppermute x8, waiting for transfers between devices, both_ways(): return (lax.ppermute(strips, BOTH, ring), lax.ppermute(strips, BOTH, back))  26 us
    pallas_call x1, Pallas kernels, scatter_rows(): pl.pallas_call(functools.partial(row_kernel, first, last), out_shape=shap...  19.6 us
    ppermute x8, starting transfers between devices, both_ways(): return (lax.ppermute(strips, BOTH, ring), lax.ppermute(strips, BOTH, back))  16.9 us
    all_to_all x1, starting transfers between devices, shards(): lax.all_to_all(summed, 'blocks', split_axis=0, concat_axis=0, tiled=True)  12.1 us
    pallas_call x6, Pallas kernels, call(): pl.pallas_call(kernel, out_shape=outs, in_specs=specs or [VMEM] * len(arg...  7.91 us
    unnamed x38, local copies, waits for them, and re-layouts  7.9 us
    ppermute x3, waiting for transfers between devices, shards(): lax.ppermute(share_of(lax.rem(cat + step, 4)), 'cat', [(i, (i + step) % 4...  3.73 us
    ppermute x3, starting transfers between devices, shards(): lax.ppermute(share_of(lax.rem(cat + step, 4)), 'cat', [(i, (i + step) % 4...  3.56 us
  transfers between devices with their start and end apart: 12, of which 9 were waited for; matrix products, arithmetic and copies ran while one was open for 1% of the time, Pallas kernels for 21%

commit v1 on v0

v1 whole, which is shorter than its diff:
```python
import functools

import jax
import jax.numpy as jnp
from jax import lax
from jax.experimental import pallas as pl
from jax.experimental.pallas import tpu as pltpu
from jax.sharding import PartitionSpec as P

F32 = jnp.float32
BF16 = jnp.bfloat16
I32 = jnp.int32

SIDE = 30
ROWS = 32
LANES = 128
OWNERS = 64
SLOTS = 256
EXTRA = 8
CHUNK = 8
INSIDE = SIDE - 4
HALF = INSIDE // 2
HALF_ROWS = 352
BOTH = ("blocks", "cat")

PARAMS = pltpu.CompilerParams(vmem_limit_bytes=6 * 1024 * 1024)
SCATTER_PARAMS = pltpu.CompilerParams(vmem_limit_bytes=8 * 1024 * 1024)
ALONE_PARAMS = pltpu.CompilerParams(vmem_limit_bytes=60 * 1024 * 1024)
ANY = pl.BlockSpec(memory_space=pl.ANY)
VMEM = pl.BlockSpec(memory_space=pltpu.VMEM)
SMEM = pl.BlockSpec(memory_space=pltpu.SMEM)


def shape(*dims, dtype=F32):
    return jax.ShapeDtypeStruct(dims, dtype)


def fill_halves(halves, value_of):
    for half in range(2):
        halves[half] = value_of(slice(half * LANES, half * LANES + LANES))


def quarter(halves, half, receiver):
    return halves[half, pl.ds(receiver, OWNERS, stride=4), :]


def pack_kernel(conc_ref, drag_ref, *rest):
    outs, halves = rest[:4], rest[4]
    cat = lax.axis_index("cat")
    row = lax.broadcasted_iota(I32, (EXTRA, SLOTS), 0)
    coefficients = jnp.where(row == 0, drag_ref[0, 0], drag_ref[0, 1])
    fill_halves(halves, lambda lanes: conc_ref[0, 0, :, lanes])
    for step, out_ref in enumerate(outs):
        receiver = lax.bitwise_and(cat + step, 3)
        for half in range(2):
            lanes = slice(half * LANES, half * LANES + LANES)
            out_ref[0:OWNERS, lanes] = quarter(halves, half, receiver)
        out_ref[OWNERS : OWNERS + EXTRA, :] = coefficients


def partial_kernel(mine_ref, first_ref, second_ref, third_ref, air_ref, ocean_ref, after_ref, *rest):
    out_ref, wind = rest
    cat = lax.axis_index("cat")
    parts = (mine_ref, first_ref, second_ref, third_ref)
    for which, ref in enumerate((air_ref, ocean_ref)):
        for member in range(2):
            fill_halves(wind.at[which, member], lambda lanes: ref[member, 0, :, lanes])
    for half in range(2):
        lanes = slice(half * LANES, half * LANES + LANES)
        totals = [0.0, 0.0]
        for which in range(2):
            weight = jnp.zeros((OWNERS, LANES), F32)
            at = OWNERS + which
            for part in parts:
                weight += part[0:OWNERS, lanes] * part[at : at + 1, lanes]
            east = quarter(wind.at[which, 0], half, cat)
            north = quarter(wind.at[which, 1], half, cat)
            weight *= jnp.sqrt(east * east + north * north)
            totals[0] += weight * east
            totals[1] += weight * north
        out_ref[:, 0, lanes] = totals[0]
        out_ref[:, 1, lanes] = totals[1]


def split_lanes(lane_hits, value):
    high = value.astype(BF16).astype(F32)
    return (
        jnp.where(lane_hits, high, 0.0).astype(BF16),
        jnp.where(lane_hits, value - high, 0.0).astype(BF16),
    )


def spread_values(cell_ref, value_ref, count_ref, spread, index):
    block = lax.broadcasted_iota(I32, (LANES, SLOTS), 0)
    slot = lax.broadcasted_iota(I32, (1, SLOTS), 1)
    columns = pl.ds(index * SLOTS, SLOTS)
    lane_hits = block == lax.bitwise_and(cell_ref[index], LANES - 1)
    live = slot < count_ref[0, pl.program_id(0) * CHUNK + index]
    for member in range(2):
        value = jnp.where(live, value_ref[index, member : member + 1, :], 0.0)
        high, low = split_lanes(lane_hits, value)
        spread[pl.ds(member * 2 * LANES, LANES), columns] = high
        spread[pl.ds(member * 2 * LANES + LANES, LANES), columns] = low


def cell_number(cell):
    return lax.shift_right_logical(cell, 7)


def accumulate(total, hot, spread):
    total[...] += lax.dot_general(
        hot[...], spread[...], (((1,), (1,)), ((), ())), preferred_element_type=F32
    )


def summed_terms(total, member):
    at = member * 2 * LANES
    return total[:, at : at + LANES] + total[:, at + LANES : at + 2 * LANES]


def edge_kernel(cell_ref, value_ref, count_ref, after_ref, out_ref, hot, spread, total):
    step = pl.program_id(0)

    @pl.when(step == 0)
    def _():
        total[...] = jnp.zeros_like(total)

    along = lax.broadcasted_iota(I32, (ROWS, SLOTS), 0)
    for index in range(CHUNK):
        number = cell_number(cell_ref[index])
        east = lax.shift_right_logical(number * 2185, 16)
        north = number - east * SIDE
        columns = pl.ds(index * SLOTS, SLOTS)
        east_hot = (along == east).astype(F32).astype(BF16)
        north_hot = (along == north).astype(F32).astype(BF16)
        empty = jnp.zeros_like(east_hot)
        for layer in range(2):
            for side, here in enumerate(
                (east == layer, north == layer, east == SIDE - 1 - layer, north == SIDE - 1 - layer)
            ):
                hot[pl.ds((layer * 4 + side) * ROWS, ROWS), columns] = jnp.where(
                    here, east_hot if side % 2 else north_hot, empty
                )
        spread_values(cell_ref, value_ref, count_ref, spread, index)
    accumulate(total, hot, spread)

    @pl.when(step == pl.num_programs(0) - 1)
    def _():
        for member in range(2):
            out_ref[member] = summed_terms(total, member).reshape(8, ROWS, LANES)


def inside_kernel(first, cell_ref, value_ref, count_ref, out_ref, hot, spread, total):
    step = pl.program_id(0)

    @pl.when(step == 0)
    def _():
        total[...] = jnp.zeros_like(total)

    row = lax.broadcasted_iota(I32, (HALF_ROWS, SLOTS), 0)
    east = lax.shift_right_logical(row * 2521, 16)
    wanted = jnp.where(
        east < HALF, (east + first) * SIDE + 2 + (row - east * INSIDE), -1
    )
    for index in range(CHUNK):
        columns = pl.ds(index * SLOTS, SLOTS)
        hits = wanted == cell_number(cell_ref[index])
        hot[:, columns] = hits.astype(F32).astype(BF16)
        spread_values(cell_ref, value_ref, count_ref, spread, index)
    accumulate(total, hot, spread)

    @pl.when(step == pl.num_programs(0) - 1)
    def _():
        for member in range(2):
            out_ref[member] = summed_terms(total, member)


def scatter_call(kernel, rows, outs, cell, value, count, *more):
    width = CHUNK * SLOTS

    def whole(ref):
        return pl.BlockSpec(ref.shape, lambda k, rank=len(ref.shape): (0,) * rank)

    return pl.pallas_call(
        kernel,
        out_shape=outs,
        grid=(OWNERS // CHUNK,),
        in_specs=[
            pl.BlockSpec((CHUNK, 1, SLOTS), lambda k: (k, 0, 0)),
            pl.BlockSpec((CHUNK, 2, SLOTS), lambda k: (k, 0, 0)),
            SMEM,
        ]
        + [ANY] * len(more),
        out_specs=jax.tree.map(whole, outs),
        scratch_shapes=[
            pltpu.VMEM((rows, width), BF16),
            pltpu.VMEM((4 * LANES, width), BF16),
            pltpu.VMEM((rows, 4 * LANES), F32),
        ],
        compiler_params=SCATTER_PARAMS,
        cost_estimate=pl.CostEstimate(
            flops=2 * rows * 4 * LANES * OWNERS * SLOTS, bytes_accessed=1 << 20, transcendentals=0
        ),
    )(cell, value, count, *more)


def gather_rims(strips, neighbour_ref, turn_ref, store):
    devices = lax.axis_size(BOTH)
    start = (lax.axis_index(BOTH) - 1) * LANES
    for side in range(4):
        place = lax.rem(
            neighbour_ref[side : side + 1, :] - start + devices * LANES, devices * LANES
        )
        turns = turn_ref[side : side + 1, :]
        source = lax.bitwise_and(turns + (side + 2), 3)
        holder = lax.shift_right_logical(place, 7)
        lane = jnp.broadcast_to(lax.bitwise_and(place, LANES - 1), (ROWS, LANES))
        rows = [jnp.zeros((ROWS, LANES), F32) for _ in range(2)]
        for where, ref in enumerate(strips):
            for edge in range(4):
                hits = jnp.broadcast_to((holder == where) & (source == edge), (ROWS, LANES))
                for member in range(2):
                    picked = jnp.take_along_axis(
                        ref[member, edge], lane, axis=1, mode="promise_in_bounds"
                    )
                    rows[member] = jnp.where(hits, picked, rows[member])
        store(side, turns, rows)


def turned_vector(turns, rows):
    cosine = (turns == 0).astype(F32) - (turns == 2).astype(F32)
    sine = (turns == 1).astype(F32) - (turns == 3).astype(F32)
    return cosine * rows[0] - sine * rows[1], sine * rows[0] + cosine * rows[1]


def turned_stress(turns, rows):
    parity = (1 - 2 * lax.bitwise_and(turns, 1)).astype(F32)
    return rows[0], parity * rows[1]


def store_rim(pad, member, side, rim):
    if side == 0 or side == 2:
        pad[member, 0 if side == 0 else SIDE + 1, 8 : 8 + SIDE, :] = rim[0:SIDE]
    else:
        column = 7 if side == 1 else 8 + SIDE
        for i in range(SIDE):
            pad[member, i + 1, column : column + 1, :] = rim[i : i + 1]


def store_strips(out_ref, member, cell_of, layer=0):
    far = SIDE - 1 - layer
    out_ref[member, :, SIDE:ROWS, :] = jnp.zeros((4, ROWS - SIDE, LANES), F32)
    out_ref[member, 0, 0:SIDE, :] = cell_of(layer, slice(0, SIDE))
    out_ref[member, 2, 0:SIDE, :] = cell_of(far, slice(0, SIDE))
    for i in range(SIDE):
        out_ref[member, 1, i : i + 1, :] = cell_of(i, slice(layer, layer + 1))
        out_ref[member, 3, i : i + 1, :] = cell_of(i, slice(far, far + 1))


def cell_rows(i, member, cells=slice(0, SIDE)):
    start = 2 * (SIDE * i + cells.start) + member
    count = cells.stop - cells.start
    return slice(start, start + 1) if count == 1 else pl.ds(start, count, stride=2)


def run_copies(pairs, sems):
    copies = [
        pltpu.make_async_copy(source, target, sems.at[at])
        for at, (source, target) in enumerate(pairs)
    ]
    for copy in copies:
        copy.start()
    return copies


VELOCITY_CUTS = ((0, 448), (448, 448), (896, 448), (1344, 456))
COVER_CUTS = ((0, 10), (10, 10), (20, 10))


def outer_strips_kernel(velocity_hbm, cover_hbm, out_ref, velocity_ref, cover_ref, sems):
    pairs = [
        (velocity_hbm.at[pl.ds(start, size)], velocity_ref.at[pl.ds(start, size)])
        for start, size in VELOCITY_CUTS
    ] + [
        (cover_hbm.at[pl.ds(start, size)], cover_ref.at[pl.ds(start, size)])
        for start, size in COVER_CUTS
    ]
    for copy in run_copies(pairs, sems):
        copy.wait()
    for member in range(2):
        store_strips(
            out_ref,
            member,
            lambda i, j: velocity_ref[cell_rows(i, member, j), :] * cover_ref[i, j, :].astype(F32),
        )


def weight_of(cover, mass):
    return cover.astype(F32) / (4.0 * mass + 1.0)


def inner_strips_kernel(
    velocity_ref, cover_ref, strength_ref, mass_ref, inner_ref, strength_strips_ref, weight_strips_ref
):
    for member in range(2):
        store_strips(
            inner_ref,
            member,
            lambda i, j: velocity_ref[cell_rows(i, member, j), :] * cover_ref[i, j, :].astype(F32),
            1,
        )
    store_strips(strength_strips_ref, 0, lambda i, j: strength_ref[i, j, :])
    for layer in range(2):
        at = slice(4 * layer, 4 * layer + 4)
        store_strips(
            weight_strips_ref.at[:, at],
            0,
            lambda i, j: weight_of(cover_ref[i, j, :], mass_ref[i, j, :]),
            layer,
        )


def derivatives(pad, member, i):
    middle = slice(8, 8 + SIDE)
    east = 0.5 * (pad[member, i + 2, middle, :] - pad[member, i, middle, :])
    north = 0.5 * (pad[member, i + 1, 9 : 9 + SIDE, :] - pad[member, i + 1, 7 : 7 + SIDE, :])
    return east, north


def targets_of(east_e, east_n, north_e, north_n, strength):
    divergence = east_e + north_n
    tension = east_e - north_n
    shearing = east_n + north_e
    inverse = lax.rsqrt(
        divergence * divergence + (tension * tension + shearing * shearing) * 0.25 + 0.25
    )
    scaled = strength * inverse
    return (
        divergence * scaled - strength,
        0.25 * (tension * scaled),
        0.125 * (shearing * scaled),
    )


def stress_targets(pad, strength, i):
    return targets_of(*derivatives(pad, 0, i), *derivatives(pad, 1, i), strength)


def forces(pad, i):
    middle = slice(8, 8 + SIDE)
    upper, lower = slice(9, 9 + SIDE), slice(7, 7 + SIDE)
    shear_east, shear_north = derivatives(pad, 1, i)
    force_east = 0.5 * (pad[0, i + 2, middle, :] - pad[0, i, middle, :]) + shear_north
    force_north = shear_east + 0.5 * (pad[2, i + 1, upper, :] - pad[2, i + 1, lower, :])
    return force_east, force_north


def stress_rims_kernel(before_ref, own_ref, after_ref, neighbour_ref, turn_ref, out_ref):
    def store(side, turns, rows):
        for member, rim in enumerate(turned_stress(turns, rows)):
            out_ref[member, side] = rim

    gather_rims((before_ref, own_ref, after_ref), neighbour_ref, turn_ref, store)


def fill_stress(pad, stress_ref):
    for i in range(SIDE):
        first_stress, second_stress = stress_ref[0, i], stress_ref[1, i]
        pad[0, i + 1, 8 : 8 + SIDE, :] = 0.5 * (first_stress + second_stress)
        pad[1, i + 1, 8 : 8 + SIDE, :] = stress_ref[2, i]
        pad[2, i + 1, 8 : 8 + SIDE, :] = 0.5 * (first_stress - second_stress)


def store_stress_rim(pad, side, normal, shear):
    store_rim(pad, 0 if side in (0, 2) else 2, side, normal)
    store_rim(pad, 1, side, shear)


def base_kernel(
    stress_rims_ref,
    rims_ref,
    velocity_ref,
    cover_ref,
    mass_ref,
    strength_ref,
    forcing_ref,
    weight_ref,
    base_ref,
    stress_ref,
    outer_ref,
    inner_ref,
    line,
    pad,
):
    for i in range(SIDE):
        covered = cover_ref[i].astype(F32)
        for member in range(2):
            line[member, i + 1, 8 : 8 + SIDE, :] = velocity_ref[cell_rows(i, member), :] * covered
    for member in range(2):
        for side in range(4):
            store_rim(line, member, side, rims_ref[member, side])
    for i in range(SIDE):
        targets = stress_targets(line, strength_ref[i], i)
        for member in range(3):
            stress_ref[member, i] = 0.5 * targets[member]
    fill_stress(pad, stress_ref)
    for side in range(4):
        store_stress_rim(pad, side, stress_rims_ref[0, side], stress_rims_ref[1, side])
    for i in range(SIDE):
        force_east, force_north = forces(pad, i)
        eastward = line[0, i + 1, 8 : 8 + SIDE, :]
        northward = line[1, i + 1, 8 : 8 + SIDE, :]
        mass = mass_ref[i]
        weight = weight_of(cover_ref[i], mass)
        base_ref[0, i] = weight * (mass * (4.0 * eastward + 0.5 * northward) + force_east)
        base_ref[1, i] = weight * (mass * (4.0 * northward - 0.5 * eastward) + force_north)
    for layer, out_ref in enumerate((outer_ref, inner_ref)):
        at = slice(4 * layer, 4 * layer + 4)
        for member in range(2):
            store_strips(out_ref, member, lambda i, j: base_ref[member, i, j, :], layer)
            out_ref[member] += weight_ref[0, at] * forcing_ref[member, at]


def edge_stress_kernel(
    before_ref,
    outer_ref,
    after_ref,
    inner_ref,
    neighbour_ref,
    turn_ref,
    strength_ref,
    *rest,
    opening,
):
    faces_ref, rims_ref, line = rest[-3:]

    def store(side, turns, rows):
        for member, rim in enumerate(turned_vector(turns, rows)):
            rims_ref[member, side] = rim

    gather_rims((before_ref, outer_ref, after_ref), neighbour_ref, turn_ref, store)
    faces_ref[:, :, SIDE:ROWS, :] = jnp.zeros((2, 4, ROWS - SIDE, LANES), F32)
    for side in range(4):
        end = 0 if side < 2 else SIDE - 1
        across, beside = [], []
        for member in range(2):
            line[member, side, 8 : 8 + SIDE, :] = outer_ref[member, side, 0:SIDE, :]
            lower, upper = (1, 3) if side % 2 == 0 else (0, 2)
            line[member, side, 7:8, :] = rims_ref[member, lower, end : end + 1, :]
            line[member, side, 8 + SIDE : 9 + SIDE, :] = rims_ref[member, upper, end : end + 1, :]
            step = 0.5 * (inner_ref[member, side, 0:SIDE, :] - rims_ref[member, side, 0:SIDE, :])
            across.append(step if side < 2 else -step)
            beside.append(
                0.5 * (line[member, side, 9 : 9 + SIDE, :] - line[member, side, 7 : 7 + SIDE, :])
            )
        east, north = (across, beside) if side % 2 == 0 else (beside, across)
        first, second, shear = targets_of(
            east[0], north[0], east[1], north[1], strength_ref[0, side, 0:SIDE, :]
        )
        normal = 0.5 * (first + second) if side % 2 == 0 else 0.5 * (first - second)
        for member, target in enumerate((normal, shear)):
            old = 0.0 if opening else rest[0][member, side, 0:SIDE, :]
            faces_ref[member, side, 0:SIDE, :] = old + 0.5 * (target - old)


def second_stress_kernel(
    base_ref,
    cover_ref,
    mass_ref,
    low_ref,
    high_ref,
    outer_ref,
    inner_ref,
    rims_ref,
    strength_ref,
    old_ref,
    moving_ref,
    stress_ref,
    stress_hbm,
    pad,
    sems,
):
    for member in range(2):
        for side in range(4):
            store_rim(pad, member, side, rims_ref[member, side])
        for i, ref, side in (
            (0, outer_ref, 0),
            (1, inner_ref, 0),
            (SIDE - 2, inner_ref, 2),
            (SIDE - 1, outer_ref, 2),
        ):
            pad[member, i + 1, 8 : 8 + SIDE, :] = ref[member, side, 0:SIDE, :]
        for i in range(2, SIDE - 2):
            for j, ref, side in (
                (0, outer_ref, 1),
                (1, inner_ref, 1),
                (SIDE - 2, inner_ref, 3),
                (SIDE - 1, outer_ref, 3),
            ):
                pad[member, i + 1, 8 + j : 9 + j, :] = ref[member, side, i : i + 1, :]
    inside = slice(2, SIDE - 2)
    for i in range(2, SIDE - 2):
        weight = weight_of(cover_ref[i, inside, :], mass_ref[i, inside, :])
        ref, at = (low_ref, i - 2) if i < 2 + HALF else (high_ref, i - 2 - HALF)
        for member in range(2):
            pad[member, i + 1, 10 : 10 + INSIDE, :] = base_ref[member, i, inside, :] + weight * (
                ref[member, at * INSIDE : at * INSIDE + INSIDE, :]
            )
    copies = []
    for i in range(SIDE):
        targets = stress_targets(pad, strength_ref[i], i)
        for member in range(3):
            old = old_ref[member, i]
            stress_ref[member, i] = old + 0.5 * (targets[member] - old)
        for member in range(2):
            moving_ref[member, i] = pad[member, i + 1, 8 : 8 + SIDE, :]
        if i % 10 == 9:
            part = pl.ds(i - 9, 10)
            copies.append(
                pltpu.make_async_copy(
                    stress_ref.at[:, part], stress_hbm.at[:, part], sems.at[i // 10]
                )
            )
            copies[-1].start()
    for copy in copies:
        copy.wait()


def last_kernel(
    before_ref,
    own_ref,
    after_ref,
    neighbour_ref,
    turn_ref,
    moving_ref,
    base_ref,
    cover_ref,
    mass_ref,
    stress_ref,
    out_hbm,
    pad,
    out_ref,
    sems,
):
    copies = []
    fill_stress(pad, stress_ref)

    def store(side, turns, rows):
        store_stress_rim(pad, side, *turned_stress(turns, rows))

    gather_rims((before_ref, own_ref, after_ref), neighbour_ref, turn_ref, store)
    for i in range(SIDE):
        force_east, force_north = forces(pad, i)
        eastward, northward = moving_ref[0, i], moving_ref[1, i]
        mass = mass_ref[i]
        weight = weight_of(cover_ref[i], mass)
        out_ref[cell_rows(i, 0), :] = weight * (
            mass * (4.0 * eastward + 0.5 * northward) + force_east
        ) + (eastward - base_ref[0, i])
        out_ref[cell_rows(i, 1), :] = weight * (
            mass * (4.0 * northward - 0.5 * eastward) + force_north
        ) + (northward - base_ref[1, i])
        if i % 6 == 5:
            part = pl.ds(60 * (i - 5), 360)
            copies.append(
                pltpu.make_async_copy(out_ref.at[part], out_hbm.at[part], sems.at[i // 6])
            )
            copies[-1].start()
    for copy in copies:
        copy.wait()


def call(kernel, outs, *args, specs=None, out_specs=None, scratch=(), work=1 << 22, params=PARAMS):
    return pl.pallas_call(
        kernel,
        out_shape=outs,
        in_specs=specs or [VMEM] * len(args),
        out_specs=out_specs or jax.tree.map(lambda _: VMEM, outs),
        scratch_shapes=list(scratch),
        compiler_params=params,
        cost_estimate=pl.CostEstimate(flops=work, bytes_accessed=1 << 22, transcendentals=0),
    )(*args)


def shards(
    velocity,
    strength,
    mass,
    ice_cover,
    neighbour,
    rotation,
    concentration,
    air_wind,
    ocean_current,
    drag,
    slot_cell,
    slot_count,
):
    devices = lax.axis_size(BOTH)
    ring = [(i, (i + 1) % devices) for i in range(devices)]
    back = [(j, i) for i, j in ring]

    def both_ways(strips):
        return lax.ppermute(strips, BOTH, ring), lax.ppermute(strips, BOTH, back)

    strip_shape = shape(2, 4, ROWS, LANES)
    block = (SIDE, SIDE, LANES)
    pad2 = [pltpu.VMEM((2, ROWS, 48, LANES), F32)]
    pad3 = [pltpu.VMEM((3, ROWS, 48, LANES), F32)]
    count = slot_count.reshape(1, OWNERS)

    sems = pltpu.SemaphoreType.DMA
    velocity = jnp.transpose(velocity, (1, 2, 0, 3)).reshape(2 * SIDE * SIDE, LANES)
    outer = call(
        outer_strips_kernel,
        strip_shape,
        velocity,
        ice_cover,
        specs=[ANY, ANY],
        scratch=[pltpu.VMEM((2 * SIDE * SIDE, LANES), F32), pltpu.VMEM(block, I32), sems((7,))],
        params=ALONE_PARAMS,
    )
    before, after = both_ways(outer)
    inner, strength_strips, weight_strips = call(
        inner_strips_kernel,
        (strip_shape, shape(1, 4, ROWS, LANES), shape(1, 8, ROWS, LANES)),
        velocity, ice_cover, strength, mass,
    )

    packed = call(
        pack_kernel,
        [shape(OWNERS + EXTRA, SLOTS)] * 4,
        concentration,
        drag.reshape(1, 2),
        specs=[VMEM, SMEM],
        scratch=[pltpu.VMEM((2, 4 * OWNERS, LANES), F32)],
    )
    parts = [packed[0]] + [
        lax.ppermute(packed[step], "cat", [(i, (i + step) % 4) for i in range(4)])
        for step in (1, 2, 3)
    ]

    line = [pltpu.VMEM((2, 4, 48, LANES), F32)]
    faces, rims = call(
        functools.partial(edge_stress_kernel, opening=True),
        (strip_shape, strip_shape),
        before, outer, after, inner, neighbour, rotation, strength_strips, *parts[1:],
        specs=[VMEM] * 7 + [ANY] * 3,
        scratch=line,
    )
    before, after = both_ways(faces)

    summed = call(
        partial_kernel,
        shape(OWNERS, 2, SLOTS),
        *parts, air_wind, ocean_current, faces,
        specs=[VMEM] * 6 + [ANY],
        scratch=[pltpu.VMEM((2, 2, 2, 4 * OWNERS, LANES), F32)],
    )
    arrived = lax.all_to_all(summed, "blocks", split_axis=0, concat_axis=0, tiled=True)

    stress_rims = call(
        stress_rims_kernel, strip_shape, before, faces, after, neighbour, rotation, work=1 << 34
    )
    forcing = scatter_call(
        edge_kernel, 8 * ROWS, shape(2, 8, ROWS, LANES), slot_cell, arrived, count, stress_rims
    )
    base, stress, outer, inner = call(
        base_kernel,
        (shape(2, *block), shape(3, *block), strip_shape, strip_shape),
        stress_rims, rims, velocity, ice_cover, mass, strength, forcing, weight_strips,
        scratch=pad2 + pad3,
    )
    before, after = both_ways(outer)
    low = scatter_call(
        functools.partial(inside_kernel, 2), HALF_ROWS, shape(2, HALF_ROWS, LANES),
        slot_cell, arrived, count,
    )
    faces, rims = call(
        functools.partial(edge_stress_kernel, opening=False),
        (strip_shape, strip_shape),
        before, outer, after, inner, neighbour, rotation, strength_strips, faces,
        scratch=line,
    )
    before, after = both_ways(faces)
    high = scatter_call(
        functools.partial(inside_kernel, 2 + HALF), HALF_ROWS, shape(2, HALF_ROWS, LANES),
        slot_cell, arrived, count,
    )
    moving, kept, stress = call(
        second_stress_kernel,
        (shape(2, *block), shape(3, *block), shape(3, *block)),
        base, ice_cover, mass, low, high, outer, inner, rims, strength, stress,
        out_specs=(VMEM, VMEM, ANY),
        scratch=pad2 + [sems((3,))],
    )
    moving = call(
        last_kernel,
        shape(2 * SIDE * SIDE, LANES),
        before, faces, after, neighbour, rotation, moving, base, ice_cover, mass, kept,
        out_specs=ANY,
        scratch=pad3 + [pltpu.VMEM((2 * SIDE * SIDE, LANES), F32), sems((5,))],
    )
    moving = jnp.transpose(moving.reshape(SIDE, SIDE, 2, LANES), (2, 0, 1, 3))
    return (moving, stress)


def solution(mesh):
    placed = (
        P(None, None, None, BOTH),
        P(None, None, BOTH),
        P(None, None, BOTH),
        P(None, None, BOTH),
        P(None, BOTH),
        P(None, BOTH),
        P("cat", "blocks", None, None),
        P(None, "blocks", None, None),
        P(None, "blocks", None, None),
        P(None, "cat"),
        P(None, BOTH, None),
        P(None, BOTH),
    )
    return jax.shard_map(
        shards,
        mesh=mesh,
        in_specs=placed,
        out_specs=(P(None, None, None, BOTH), P(None, None, None, BOTH)),
        check_vma=False,
    )
```

time: 102 us -> 83.3 us (0.82)
  waiting for transfers between devices: 29.8 us -> 11.5 us
  local copies, waits for them, and re-layouts: 10.7 us -> 3.06 us
  Pallas kernels: 27.5 us -> 34.1 us
    ppermute x8, waiting for transfers between devices: 26 us -> 0.02 us  [both_ways(): return (lax.ppermute(strips, BOTH, ring), lax.ppermute(strips, BOTH, back))]
    all_to_all x1, waiting for transfers between devices: 0.01 us -> 9.74 us  [shards(): lax.all_to_all(summed, 'blocks', split_axis=0, concat_axis=0, tiled=True)]
    ppermute x8, starting transfers between devices: 16.9 us -> 25 us  [both_ways(): return (lax.ppermute(strips, BOTH, ring), lax.ppermute(strips, BOTH, back))]
    all_to_all x1, starting transfers between devices: 12.1 us -> 4.86 us  [shards(): lax.all_to_all(summed, 'blocks', split_axis=0, concat_axis=0, tiled=True)]
    unnamed x38 -> x30, local copies, waits for them, and re-layouts: 7.9 us -> 3.06 us
    pallas_call x1 -> x3, Pallas kernels: 19.6 us -> 23.7 us  [scatter_call(): pl.pallas_call(kernel, out_shape=outs, grid=(OWNERS // CHUNK,), in_specs=...]
    pallas_call x6 -> x10, Pallas kernels: 7.91 us -> 10.4 us  [call(): pl.pallas_call(kernel, out_shape=outs, in_specs=specs or [VMEM] * len(arg...]
    ppermute x3, waiting for transfers between devices: 3.73 us -> 1.7 us  [shards(): lax.ppermute(packed[step], 'cat', [(i, (i + step) % 4) for i in range(4)])]
  transfers between devices with their start and end apart: 12 -> 12, of which waited for: 9 -> 4; matrix products, arithmetic and copies ran while one was open for 1% -> 0% of each run, Pallas kernels for 21% -> 25%
where the time goes in v1:
time: 83.3 us; the launch traced here: 82.9 us
  Pallas kernels  34.1 us (41%)
  starting transfers between devices  33.2 us (40%)
  waiting for transfers between devices  11.5 us (14%)
  local copies, waits for them, and re-layouts  3.06 us (4%)
  between operations  1.07 us (1%)
    ppermute x8, starting transfers between devices, both_ways(): return (lax.ppermute(strips, BOTH, ring), lax.ppermute(strips, BOTH, back))  25 us
    pallas_call x3, Pallas kernels, scatter_call(): pl.pallas_call(kernel, out_shape=outs, grid=(OWNERS // CHUNK,), in_specs=...  23.7 us
    pallas_call x10, Pallas kernels, call(): pl.pallas_call(kernel, out_shape=outs, in_specs=specs or [VMEM] * len(arg...  10.4 us
    all_to_all x1, waiting for transfers between devices, shards(): lax.all_to_all(summed, 'blocks', split_axis=0, concat_axis=0, tiled=True)  9.74 us
    all_to_all x1, starting transfers between devices, shards(): lax.all_to_all(summed, 'blocks', split_axis=0, concat_axis=0, tiled=True)  4.86 us
    ppermute x3, starting transfers between devices, shards(): lax.ppermute(packed[step], 'cat', [(i, (i + step) % 4) for i in range(4)])  3.3 us
    unnamed x30, local copies, waits for them, and re-layouts  3.06 us
    ppermute x3, waiting for transfers between devices, shards(): lax.ppermute(packed[step], 'cat', [(i, (i + step) % 4) for i in range(4)])  1.7 us
  transfers between devices with their start and end apart: 12, of which 4 were waited for; matrix products, arithmetic and copies ran while one was open for 0% of the time, Pallas kernels for 25%

profile of v1, /device:TPU:0, one launch (start us, length us, event | category | flops | bytes accessed | tf_op | source)
XLA Modules:
  0.0 82.9 jit_solution(1186447680369711388)
XLA Ops:
  0.6 0.0 copy-start.1
  0.6 0.0 copy-start
  0.7 0.0 copy-start.12
  0.7 0.0 copy-start.10
  0.7 0.0 copy-start.11
  0.7 2.3 %shard_map.131.outer_ref = f32[2,4,32,128]{3,2,1,0:T(8,128)} custom-call(f32[1800,128]{1,0:T(8,128)} %bitcast.8, s32[30,30,128]{2,1,0:T(8,128)} %cover_ref.7), custom_call_target="tpu_custom_call" | custom-call | flops 4194304 | bytes 4194304 | tf_op jit(solution)/shard_map/pallas_call | solution.py:574
  3.0 0.0 copy-start.8
  3.0 0.1 collective-permute-start
  3.1 8.3 %collective-permute-start.1 = (f32[2,4,32,128]{3,2,1,0:T(8,128)}, f32[2,4,32,128]{3,2,1,0:T(8,128)S(1)}, u32[]{:S(2)}, u32[]{:S(2)}) collective-permute-start(f32[2,4,32,128]{3,2,1,0:T(8,128)} %shard_map.131.outer_ref), channel_id=1, source_target_pairs={{1,0},{2,1},{3,2},{4,3},{5,4},{6,5},{7,6},{8,7},{9,8},{10,9},{11,1... | collective-permute-start | bytes 393224 | tf_op jit(solution)/shard_map/ppermute | solution.py:604
  11.4 0.0 copy-done.12
  11.4 0.0 copy-start.9
  11.4 0.9 %copy-done.9 = f32[1,1,256,256]{3,2,1,0:T(8,128)S(1)} copy-done((f32[1,1,256,256]{3,2,1,0:T(8,128)S(1)}, f32[1,1,256,256]{3,2,1,0:T(8,128)}, u32[]{:S(2)}) %copy-start.9) | copy-done | bytes 262168
  12.3 0.6 shard_map.133
  12.9 0.1 collective-permute-start.2
  13.0 0.1 collective-permute-start.3
  13.1 3.1 %collective-permute-start.4 = (f32[72,256]{1,0:T(8,128)S(1)}, f32[72,256]{1,0:T(8,128)S(1)}, u32[]{:S(2)}, u32[]{:S(2)}) collective-permute-start(f32[72,256]{1,0:T(8,128)S(1)} %get-tuple-element.24), channel_id=1, source_target_pairs={{0,3},{1,0},{2,1},{3,2},{4,7},{5,4},{6,5},{7,6},{8,11},{9,8},{10,9... | collective-permute-start | bytes 221192 | tf_op jit(solution)/shard_map/ppermute | solution.py:639
  16.2 0.0 copy-done.1
  16.2 0.0 copy-done
  16.2 0.0 copy-start.2
  16.2 1.0 %copy-done.2 = f32[30,30,128]{2,1,0:T(8,128)S(1)} copy-done((f32[30,30,128]{2,1,0:T(8,128)S(1)}, f32[30,30,128]{2,1,0:T(8,128)}, u32[]{:S(2)}) %copy-start.2) | copy-done | bytes 460824
  17.3 0.0 copy-start.4
  17.3 1.0 %copy-done.4 = f32[30,30,128]{2,1,0:T(8,128)S(1)} copy-done((f32[30,30,128]{2,1,0:T(8,128)S(1)}, f32[30,30,128]{2,1,0:T(8,128)}, u32[]{:S(2)}) %copy-start.4) | copy-done | bytes 460824
  18.3 0.0 copy-start.7
  18.3 0.2 shard_map.132
  18.5 0.5 collective-permute-done.2.rest_0_.first_ref
  19.0 0.6 collective-permute-done.3.rest_1_.second_ref
  19.5 0.7 collective-permute-done.4.rest_2_.third_ref
  20.2 0.0 collective-permute-done.before_ref
  20.2 0.0 collective-permute-done.1.after_ref
  20.2 0.0 copy-done.10
  20.2 0.0 copy-done.11
  20.2 0.0 copy-done.8
  20.2 0.6 shard_map.134
  20.8 1.3 %collective-permute-start.5 = (f32[2,4,32,128]{3,2,1,0:T(8,128)S(1)}, f32[2,4,32,128]{3,2,1,0:T(8,128)S(1)}, u32[]{:S(2)}, u32[]{:S(2)}) collective-permute-start(f32[2,4,32,128]{3,2,1,0:T(8,128)S(1)} %get-tuple-element.25.own_ref.after_ref.rest_0_), channel_id=1, source_target_pairs={{0,1},{1,2},{2,3},{3,4},{4,5},{5,6},{6,7},{7,8},{8,9},{9,10},{10,1... | collective-permute-start | bytes 393224 | tf_op jit(solution)/shard_map/ppermute | solution.py:604
  22.1 5.9 %collective-permute-start.6 = (f32[2,4,32,128]{3,2,1,0:T(8,128)S(1)}, f32[2,4,32,128]{3,2,1,0:T(8,128)S(1)}, u32[]{:S(2)}, u32[]{:S(2)}) collective-permute-start(f32[2,4,32,128]{3,2,1,0:T(8,128)S(1)} %get-tuple-element.25.own_ref.after_ref.rest_0_), channel_id=1, source_target_pairs={{1,0},{2,1},{3,2},{4,3},{5,4},{6,5},{7,6},{8,7},{9,8},{10,9},{11,1... | collective-permute-start | bytes 393224 | tf_op jit(solution)/shard_map/ppermute | solution.py:604
  28.1 0.0 copy-done.6
  28.1 0.0 copy-done.7
  28.1 0.9 %shard_map.136 = f32[64,2,256]{2,1,0:T(2,128)} custom-call(f32[72,256]{1,0:T(8,128)S(1)} %get-tuple-element.27.mine_ref, f32[72,256]{1,0:T(8,128)S(1)} %collective-permute-done.2.rest_0_.first_ref, f32[72,256]{1,0:T(8,128)S(1)} %collective-permute-done.3.rest_1_.second_ref, f32[72,256]{1,0:T(8,128)S(1)} %collective-permute-done.4.rest_2_.third_ref, ...), custom_call_target="tpu_custom_call" | custom-call | flops 4194304 | bytes 4194304 | tf_op jit(solution)/shard_map/pallas_call | solution.py:574
  29.0 4.9 %all-to-all-start = ((f32[64,2,256]{2,1,0:T(2,128)}), f32[64,2,256]{2,1,0:T(2,128)S(1)}, u32[]{:S(2)}, u32[]{:S(2)}) async-start(f32[64,2,256]{2,1,0:T(2,128)} %shard_map.136), calls=%async_computation | async-start | bytes 262144 | tf_op jit(solution)/shard_map/all_to_all | solution.py:660
  33.8 0.0 copy-start.13
  33.9 0.0 copy-start.14
  33.9 0.0 collective-permute-done.5.before_ref
  33.9 0.0 collective-permute-done.6.after_ref
  33.9 0.5 shard_map.135.after_ref.stress_rims_ref
  34.4 9.7 %all-to-all-done.value_ref = f32[64,2,256]{2,1,0:T(2,128)S(1)} async-done(((f32[64,2,256]{2,1,0:T(2,128)}), f32[64,2,256]{2,1,0:T(2,128)S(1)}, u32[]{:S(2)}, u32[]{:S(2)}) %all-to-all-start) | async-done | bytes 131104 | tf_op jit(solution)/shard_map/all_to_all | solution.py:660
  44.1 0.0 copy-done.13
  44.1 0.0 copy-done.14
  44.2 6.8 %shard_map.137.forcing_ref = f32[2,8,32,128]{3,2,1,0:T(8,128)S(1)} custom-call(s32[64,1,256]{2,1,0:T(1,128)S(1)} %copy-done.13, f32[64,2,256]{2,1,0:T(2,128)S(1)} %all-to-all-done.value_ref, s32[1,64]{1,0:T(1,128)S(1)} %bitcast.12, f32[2,4,32,128]{3,2,1,0:T(8,128)S(1)} %shard_map.135.after_ref.stress_rims_ref), custom_call_target="tpu_custom_call" | custom-call | flops 4294967296 | bytes 1048576 | tf_op jit(solution)/shard_map/pallas_call | solution.py:184
  50.9 0.0 copy-done.3
  51.0 0.0 copy-done.5
  51.0 1.3 %shard_map.138 = (f32[2,30,30,128]{3,2,1,0:T(8,128)S(1)}, f32[3,30,30,128]{3,2,1,0:T(8,128)S(1)}, f32[2,4,32,128]{3,2,1,0:T(8,128)S(1)}, f32[2,4,32,128]{3,2,1,0:T(8,128)S(1)}) custom-call(f32[2,4,32,128]{3,2,1,0:T(8,128)S(1)} %shard_map.135.after_ref.stress_rims_ref, f32[2,4,32,128]{3,2,1,0:T(8,128)S(1)} %get-tuple-element.26.rims_ref, ...), custom_call_target="tpu_custom_call" | custom-call | flops 4194304 | bytes 4194304 | tf_op jit(solution)/shard_map/pallas_call | solution.py:574
  52.2 0.1 collective-permute-start.7
  52.3 7.2 %collective-permute-start.8 = (f32[2,4,32,128]{3,2,1,0:T(8,128)S(1)}, f32[2,4,32,128]{3,2,1,0:T(8,128)S(1)}, u32[]{:S(2)}, u32[]{:S(2)}) collective-permute-start(f32[2,4,32,128]{3,2,1,0:T(8,128)S(1)} %get-tuple-element.29.outer_ref), channel_id=1, source_target_pairs={{1,0},{2,1},{3,2},{4,3},{5,4},{6,5},{7,6},{8,7},{9,8},{10,9},{11,1... | collective-permute-start | bytes 393224 | tf_op jit(solution)/shard_map/ppermute | solution.py:604
  59.5 8.5 %shard_map.140.low_ref = f32[2,352,128]{2,1,0:T(8,128)S(1)} custom-call(s32[64,1,256]{2,1,0:T(1,128)S(1)} %copy-done.13, f32[64,2,256]{2,1,0:T(2,128)S(1)} %all-to-all-done.value_ref, s32[1,64]{1,0:T(1,128)S(1)} %bitcast.13), custom_call_target="tpu_custom_call" | custom-call | flops 5905580032 | bytes 1048576 | tf_op jit(solution)/shard_map/pallas_call | solution.py:184
  68.0 0.0 collective-permute-done.7.before_ref
  68.0 0.0 collective-permute-done.8.after_ref
  68.0 0.6 shard_map.139
  68.6 1.5 %collective-permute-start.10 = (f32[2,4,32,128]{3,2,1,0:T(8,128)S(1)}, f32[2,4,32,128]{3,2,1,0:T(8,128)S(1)}, u32[]{:S(2)}, u32[]{:S(2)}) collective-permute-start(f32[2,4,32,128]{3,2,1,0:T(8,128)S(1)} %get-tuple-element.31.own_ref), channel_id=1, source_target_pairs={{1,0},{2,1},{3,2},{4,3},{5,4},{6,5},{7,6},{8,7},{9,8},{10,9},{11,1... | collective-permute-start | bytes 393224 | tf_op jit(solution)/shard_map/ppermute | solution.py:604
  70.0 0.7 collective-permute-start.9
  70.7 8.5 %shard_map.141.high_ref = f32[2,352,128]{2,1,0:T(8,128)S(1)} custom-call(s32[64,1,256]{2,1,0:T(1,128)S(1)} %copy-done.13, f32[64,2,256]{2,1,0:T(2,128)S(1)} %all-to-all-done.value_ref, s32[1,64]{1,0:T(1,128)S(1)} %bitcast.14), custom_call_target="tpu_custom_call" | custom-call | flops 5905580032 | bytes 1048576 | tf_op jit(solution)/shard_map/pallas_call | solution.py:184
  79.2 1.7 %shard_map.142 = (f32[2,30,30,128]{3,2,1,0:T(8,128)S(1)}, f32[3,30,30,128]{3,2,1,0:T(8,128)S(1)}, f32[3,30,30,128]{3,2,1,0:T(8,128)}) custom-call(f32[2,30,30,128]{3,2,1,0:T(8,128)S(1)} %get-tuple-element.32.base_ref, s32[30,30,128]{2,1,0:T(8,128)S(1)} %copy-done, f32[30,30,128]{2,1,0:T(8,128)S(1)} %copy-done.3, f32[2,352,128]{2,1,0:T(8,128)S(1)} %shard_map.140.low_ref, ...), custom_call_target="tpu_custom_call" | custom-call | flops 4194304 | bytes 4194304 | tf_op jit(solution)/shard_map/pallas_call | solution.py:574
  80.9 0.0 collective-permute-done.10.after_ref
  80.9 0.0 collective-permute-done.9.before_ref
  80.9 1.8 %shard_map.143 = f32[1800,128]{1,0:T(8,128)} custom-call(f32[2,4,32,128]{3,2,1,0:T(8,128)S(1)} %collective-permute-done.9.before_ref, f32[2,4,32,128]{3,2,1,0:T(8,128)S(1)} %get-tuple-element.31.own_ref, f32[2,4,32,128]{3,2,1,0:T(8,128)S(1)} %collective-permute-done.10.after_ref, s32[4,128]{1,0:T(4,128)S(1)} %copy-done.10, s32[4,128]{1,0:T(4,128)S(1)} %copy-done.11, ...), custom_call_target="tpu_custom_call" | custom-call | flops 4194304 | bytes 4194304 | tf_op jit(solution)/shard_map/pallas_call | solution.py:574
  (3 shorter events, 0.0 us)
Async XLA Ops:
  0.6 15.6 %copy-start.1 = (f32[2,30,30,128]{3,0,2,1:T(2,128)S(1)}, f32[2,30,30,128]{3,0,2,1:T(2,128)}, u32[]{:S(2)}) copy-start(f32[2,30,30,128]{3,0,2,1:T(2,128)} %param.12) | copy-start | bytes 2764804
  0.6 15.6 %copy-start = (s32[30,30,128]{2,1,0:T(8,128)S(1)}, s32[30,30,128]{2,1,0:T(8,128)}, u32[]{:S(2)}) copy-start(s32[30,30,128]{2,1,0:T(8,128)} %cover_ref.7) | copy-start | bytes 1382404
  0.7 10.7 %copy-start.12 = (f32[2,1]{0,1:T(1,128)S(1)}, f32[2,1]{0,1:T(1,128)}, u32[]{:S(2)}) copy-start(f32[2,1]{0,1:T(1,128)} %param.21) | copy-start | bytes 28
  0.7 19.6 %copy-start.10 = (s32[4,128]{1,0:T(4,128)S(1)}, s32[4,128]{1,0:T(4,128)}, u32[]{:S(2)}) copy-start(s32[4,128]{1,0:T(4,128)} %neighbour_ref.7) | copy-start | bytes 6148
  0.7 19.6 %copy-start.11 = (s32[4,128]{1,0:T(4,128)S(1)}, s32[4,128]{1,0:T(4,128)}, u32[]{:S(2)}) copy-start(s32[4,128]{1,0:T(4,128)} %turn_ref.7) | copy-start | bytes 6148
  3.0 17.3 %copy-start.8 = (f32[2,4,32,128]{3,2,1,0:T(8,128)S(1)}, f32[2,4,32,128]{3,2,1,0:T(8,128)}, u32[]{:S(2)}) copy-start(f32[2,4,32,128]{3,2,1,0:T(8,128)} %shard_map.131.outer_ref) | copy-start | bytes 393220
  3.0 17.2 %collective-permute-start = (f32[2,4,32,128]{3,2,1,0:T(8,128)}, f32[2,4,32,128]{3,2,1,0:T(8,128)S(1)}, u32[]{:S(2)}, u32[]{:S(2)}) collective-permute-start(f32[2,4,32,128]{3,2,1,0:T(8,128)} %shard_map.131.outer_ref), channel_id=1, source_target_pairs={{0,1},{1,2},{2,3},{3,4},{4,5},{5,6},{6,7},{7,8},{8,9},{9,10},{10,1... | collective-permute-start | bytes 393224 | tf_op jit(solution)/shard_map/ppermute | solution.py:604
  3.1 17.1 %collective-permute-start.1 = (f32[2,4,32,128]{3,2,1,0:T(8,128)}, f32[2,4,32,128]{3,2,1,0:T(8,128)S(1)}, u32[]{:S(2)}, u32[]{:S(2)}) collective-permute-start(f32[2,4,32,128]{3,2,1,0:T(8,128)} %shard_map.131.outer_ref), channel_id=1, source_target_pairs={{1,0},{2,1},{3,2},{4,3},{5,4},{6,5},{7,6},{8,7},{9,8},{10,9},{11,1... | collective-permute-start | bytes 393224 | tf_op jit(solution)/shard_map/ppermute | solution.py:604
  11.4 1.0 %copy-start.9 = (f32[1,1,256,256]{3,2,1,0:T(8,128)S(1)}, f32[1,1,256,256]{3,2,1,0:T(8,128)}, u32[]{:S(2)}) copy-start(f32[1,1,256,256]{3,2,1,0:T(8,128)} %conc_ref.1) | copy-start | bytes 786436
  12.9 6.1 %collective-permute-start.2 = (f32[72,256]{1,0:T(8,128)S(1)}, f32[72,256]{1,0:T(8,128)S(1)}, u32[]{:S(2)}, u32[]{:S(2)}) collective-permute-start(f32[72,256]{1,0:T(8,128)S(1)} %get-tuple-element.22), channel_id=1, source_target_pairs={{0,1},{1,2},{2,3},{3,0},{4,5},{5,6},{6,7},{7,4},{8,9},{9,10},{10,1... | collective-permute-start | bytes 221192 | tf_op jit(solution)/shard_map/ppermute | solution.py:639
  13.0 6.5 %collective-permute-start.3 = (f32[72,256]{1,0:T(8,128)S(1)}, f32[72,256]{1,0:T(8,128)S(1)}, u32[]{:S(2)}, u32[]{:S(2)}) collective-permute-start(f32[72,256]{1,0:T(8,128)S(1)} %get-tuple-element.23), channel_id=1, source_target_pairs={{0,2},{1,3},{2,0},{3,1},{4,6},{5,7},{6,4},{7,5},{8,10},{9,11},{10,... | collective-permute-start | bytes 221192 | tf_op jit(solution)/shard_map/ppermute | solution.py:639
  13.1 7.1 %collective-permute-start.4 = (f32[72,256]{1,0:T(8,128)S(1)}, f32[72,256]{1,0:T(8,128)S(1)}, u32[]{:S(2)}, u32[]{:S(2)}) collective-permute-start(f32[72,256]{1,0:T(8,128)S(1)} %get-tuple-element.24), channel_id=1, source_target_pairs={{0,3},{1,0},{2,1},{3,2},{4,7},{5,4},{6,5},{7,6},{8,11},{9,8},{10,9... | collective-permute-start | bytes 221192 | tf_op jit(solution)/shard_map/ppermute | solution.py:639
  16.2 1.0 %copy-start.2 = (f32[30,30,128]{2,1,0:T(8,128)S(1)}, f32[30,30,128]{2,1,0:T(8,128)}, u32[]{:S(2)}) copy-start(f32[30,30,128]{2,1,0:T(8,128)} %mass_ref.7) | copy-start | bytes 1382404
  17.3 1.0 %copy-start.4 = (f32[30,30,128]{2,1,0:T(8,128)S(1)}, f32[30,30,128]{2,1,0:T(8,128)}, u32[]{:S(2)}) copy-start(f32[30,30,128]{2,1,0:T(8,128)} %strength_ref.5) | copy-start | bytes 1382404
  18.3 9.8 %copy-start.6 = (f32[2,1,256,256]{3,2,1,0:T(8,128)S(1)}, f32[2,1,256,256]{3,2,1,0:T(8,128)}, u32[]{:S(2)}) copy-start(f32[2,1,256,256]{3,2,1,0:T(8,128)} %air_ref.1) | copy-start | bytes 1572868
  18.3 9.8 %copy-start.7 = (f32[2,1,256,256]{3,2,1,0:T(8,128)S(1)}, f32[2,1,256,256]{3,2,1,0:T(8,128)}, u32[]{:S(2)}) copy-start(f32[2,1,256,256]{3,2,1,0:T(8,128)} %ocean_ref.1) | copy-start | bytes 1572868
  20.8 13.1 %collective-permute-start.5 = (f32[2,4,32,128]{3,2,1,0:T(8,128)S(1)}, f32[2,4,32,128]{3,2,1,0:T(8,128)S(1)}, u32[]{:S(2)}, u32[]{:S(2)}) collective-permute-start(f32[2,4,32,128]{3,2,1,0:T(8,128)S(1)} %get-tuple-element.25.own_ref.after_ref.rest_0_), channel_id=1, source_target_pairs={{0,1},{1,2},{2,3},{3,4},{4,5},{5,6},{6,7},{7,8},{8,9},{9,10},{10,1... | collective-permute-start | bytes 393224 | tf_op jit(solution)/shard_map/ppermute | solution.py:604
  22.1 11.8 %collective-permute-start.6 = (f32[2,4,32,128]{3,2,1,0:T(8,128)S(1)}, f32[2,4,32,128]{3,2,1,0:T(8,128)S(1)}, u32[]{:S(2)}, u32[]{:S(2)}) collective-permute-start(f32[2,4,32,128]{3,2,1,0:T(8,128)S(1)} %get-tuple-element.25.own_ref.after_ref.rest_0_), channel_id=1, source_target_pairs={{1,0},{2,1},{3,2},{4,3},{5,4},{6,5},{7,6},{8,7},{9,8},{10,9},{11,1... | collective-permute-start | bytes 393224 | tf_op jit(solution)/shard_map/ppermute | solution.py:604
  29.0 15.2 %all-to-all-start = ((f32[64,2,256]{2,1,0:T(2,128)}), f32[64,2,256]{2,1,0:T(2,128)S(1)}, u32[]{:S(2)}, u32[]{:S(2)}) async-start(f32[64,2,256]{2,1,0:T(2,128)} %shard_map.136), calls=%async_computation | async-start | bytes 262144 | tf_op jit(solution)/shard_map/all_to_all | solution.py:660
  33.8 10.3 %copy-start.13 = (s32[64,1,256]{2,1,0:T(1,128)S(1)}, s32[64,1,256]{2,1,0:T(1,128)}, u32[]{:S(2)}) copy-start(s32[64,1,256]{2,1,0:T(1,128)} %cell_ref.5) | copy-start | bytes 196612
  33.9 10.3 %copy-start.14 = (s32[64,1]{0,1:T(1,128)S(1)}, s32[64,1]{0,1:T(1,128)}, u32[]{:S(2)}) copy-start(s32[64,1]{0,1:T(1,128)} %param.23) | copy-start | bytes 772
  44.1 6.8 %copy-start.3 = (f32[30,30,128]{2,1,0:T(8,128)S(1)}, f32[30,30,128]{2,1,0:T(8,128)}, u32[]{:S(2)}) copy-start(f32[30,30,128]{2,1,0:T(8,128)} %mass_ref.7) | copy-start | bytes 1382404
  44.2 6.8 %copy-start.5 = (f32[30,30,128]{2,1,0:T(8,128)S(1)}, f32[30,30,128]{2,1,0:T(8,128)}, u32[]{:S(2)}) copy-start(f32[30,30,128]{2,1,0:T(8,128)} %strength_ref.5) | copy-start | bytes 1382404
  52.2 15.7 %collective-permute-start.7 = (f32[2,4,32,128]{3,2,1,0:T(8,128)S(1)}, f32[2,4,32,128]{3,2,1,0:T(8,128)S(1)}, u32[]{:S(2)}, u32[]{:S(2)}) collective-permute-start(f32[2,4,32,128]{3,2,1,0:T(8,128)S(1)} %get-tuple-element.29.outer_ref), channel_id=1, source_target_pairs={{0,1},{1,2},{2,3},{3,4},{4,5},{5,6},{6,7},{7,8},{8,9},{9,10},{10,1... | collective-permute-start | bytes 393224 | tf_op jit(solution)/shard_map/ppermute | solution.py:604
  52.3 15.7 %collective-permute-start.8 = (f32[2,4,32,128]{3,2,1,0:T(8,128)S(1)}, f32[2,4,32,128]{3,2,1,0:T(8,128)S(1)}, u32[]{:S(2)}, u32[]{:S(2)}) collective-permute-start(f32[2,4,32,128]{3,2,1,0:T(8,128)S(1)} %get-tuple-element.29.outer_ref), channel_id=1, source_target_pairs={{1,0},{2,1},{3,2},{4,3},{5,4},{6,5},{7,6},{8,7},{9,8},{10,9},{11,1... | collective-permute-start | bytes 393224 | tf_op jit(solution)/shard_map/ppermute | solution.py:604
  68.6 12.3 %collective-permute-start.10 = (f32[2,4,32,128]{3,2,1,0:T(8,128)S(1)}, f32[2,4,32,128]{3,2,1,0:T(8,128)S(1)}, u32[]{:S(2)}, u32[]{:S(2)}) collective-permute-start(f32[2,4,32,128]{3,2,1,0:T(8,128)S(1)} %get-tuple-element.31.own_ref), channel_id=1, source_target_pairs={{1,0},{2,1},{3,2},{4,3},{5,4},{6,5},{7,6},{8,7},{9,8},{10,9},{11,1... | collective-permute-start | bytes 393224 | tf_op jit(solution)/shard_map/ppermute | solution.py:604
  70.0 10.9 %collective-permute-start.9 = (f32[2,4,32,128]{3,2,1,0:T(8,128)S(1)}, f32[2,4,32,128]{3,2,1,0:T(8,128)S(1)}, u32[]{:S(2)}, u32[]{:S(2)}) collective-permute-start(f32[2,4,32,128]{3,2,1,0:T(8,128)S(1)} %get-tuple-element.31.own_ref), channel_id=1, source_target_pairs={{0,1},{1,2},{2,3},{3,4},{4,5},{5,6},{6,7},{7,8},{8,9},{9,10},{10,1... | collective-permute-start | bytes 393224 | tf_op jit(solution)/shard_map/ppermute | solution.py:604

commit v2 on v1

--- a/solution.py
+++ b/solution.py
@@ -17,14 +17,14 @@
 OWNERS = 64
 SLOTS = 256
 EXTRA = 8
-CHUNK = 8
+CHUNK = 16
 INSIDE = SIDE - 4
 HALF = INSIDE // 2
 HALF_ROWS = 352
 BOTH = ("blocks", "cat")
 
 PARAMS = pltpu.CompilerParams(vmem_limit_bytes=6 * 1024 * 1024)
-SCATTER_PARAMS = pltpu.CompilerParams(vmem_limit_bytes=8 * 1024 * 1024)
+SCATTER_PARAMS = pltpu.CompilerParams(vmem_limit_bytes=12 * 1024 * 1024)
 ALONE_PARAMS = pltpu.CompilerParams(vmem_limit_bytes=60 * 1024 * 1024)
 ANY = pl.BlockSpec(memory_space=pl.ANY)
 VMEM = pl.BlockSpec(memory_space=pltpu.VMEM)
@@ -58,8 +58,7 @@
         out_ref[OWNERS : OWNERS + EXTRA, :] = coefficients
 
 
-def partial_kernel(mine_ref, first_ref, second_ref, third_ref, air_ref, ocean_ref, after_ref, *rest):
-    out_ref, wind = rest
+def partial_kernel(mine_ref, first_ref, second_ref, third_ref, air_ref, ocean_ref, out_ref, wind):
     cat = lax.axis_index("cat")
     parts = (mine_ref, first_ref, second_ref, third_ref)
     for which, ref in enumerate((air_ref, ocean_ref)):
@@ -273,26 +272,33 @@
     return copies
 
 
-VELOCITY_CUTS = ((0, 448), (448, 448), (896, 448), (1344, 456))
-COVER_CUTS = ((0, 10), (10, 10), (20, 10))
-
-
-def outer_strips_kernel(velocity_hbm, cover_hbm, out_ref, velocity_ref, cover_ref, sems):
+def outer_strips_kernel(velocity_hbm, cover_hbm, *rest):
+    out_ref, lines, cover_rows, cover_low, cover_high, sems = rest
+    last = SIDE - 1
     pairs = [
-        (velocity_hbm.at[pl.ds(start, size)], velocity_ref.at[pl.ds(start, size)])
-        for start, size in VELOCITY_CUTS
-    ] + [
-        (cover_hbm.at[pl.ds(start, size)], cover_ref.at[pl.ds(start, size)])
-        for start, size in COVER_CUTS
+        (velocity_hbm.at[0], lines.at[0]),
+        (velocity_hbm.at[:, 0], lines.at[1]),
+        (velocity_hbm.at[last], lines.at[2]),
+        (velocity_hbm.at[:, last], lines.at[3]),
+        (cover_hbm.at[0], cover_rows.at[0]),
+        (cover_hbm.at[last], cover_rows.at[1]),
+        (cover_hbm.at[:, 0:8], cover_low),
+        (cover_hbm.at[:, 24:SIDE], cover_high),
     ]
     for copy in run_copies(pairs, sems):
         copy.wait()
-    for member in range(2):
-        store_strips(
-            out_ref,
-            member,
-            lambda i, j: velocity_ref[cell_rows(i, member, j), :] * cover_ref[i, j, :].astype(F32),
-        )
+    out_ref[:, :, SIDE:ROWS, :] = jnp.zeros((2, 4, ROWS - SIDE, LANES), F32)
+    for side in range(4):
+        for t in range(SIDE):
+            if side % 2 == 0:
+                covered = cover_rows[side // 2, t : t + 1, :]
+            else:
+                covered = cover_low[t, 0:1, :] if side == 1 else cover_high[t, 5:6, :]
+            covered = covered.astype(F32)
+            for member in range(2):
+                out_ref[member, side, t : t + 1, :] = (
+                    lines[side, t, member : member + 1, :] * covered
+                )
 
 
 def weight_of(cover, mass):
@@ -355,7 +361,9 @@
     return force_east, force_north
 
 
-def stress_rims_kernel(before_ref, own_ref, after_ref, neighbour_ref, turn_ref, out_ref):
+def stress_rims_kernel(
+    before_ref, own_ref, after_ref, neighbour_ref, turn_ref, forcing_ref, out_ref
+):
     def store(side, turns, rows):
         for member, rim in enumerate(turned_stress(turns, rows)):
             out_ref[member, side] = rim
@@ -610,23 +618,6 @@
     count = slot_count.reshape(1, OWNERS)
 
     sems = pltpu.SemaphoreType.DMA
-    velocity = jnp.transpose(velocity, (1, 2, 0, 3)).reshape(2 * SIDE * SIDE, LANES)
-    outer = call(
-        outer_strips_kernel,
-        strip_shape,
-        velocity,
-        ice_cover,
-        specs=[ANY, ANY],
-        scratch=[pltpu.VMEM((2 * SIDE * SIDE, LANES), F32), pltpu.VMEM(block, I32), sems((7,))],
-        params=ALONE_PARAMS,
-    )
-    before, after = both_ways(outer)
-    inner, strength_strips, weight_strips = call(
-        inner_strips_kernel,
-        (strip_shape, shape(1, 4, ROWS, LANES), shape(1, 8, ROWS, LANES)),
-        velocity, ice_cover, strength, mass,
-    )
-
     packed = call(
         pack_kernel,
         [shape(OWNERS + EXTRA, SLOTS)] * 4,
@@ -640,30 +631,57 @@
         for step in (1, 2, 3)
     ]
 
+    by_cell = jnp.transpose(velocity, (1, 2, 0, 3))
+    velocity = by_cell.reshape(2 * SIDE * SIDE, LANES)
+    outer = call(
+        outer_strips_kernel,
+        strip_shape,
+        by_cell,
+        ice_cover,
+        specs=[ANY] * 2,
+        scratch=[
+            pltpu.VMEM((4, SIDE, 2, LANES), F32),
+            pltpu.VMEM((2, SIDE, LANES), I32),
+            pltpu.VMEM((SIDE, 8, LANES), I32),
+            pltpu.VMEM((SIDE, 6, LANES), I32),
+            sems((8,)),
+        ],
+        params=ALONE_PARAMS,
+    )
+    before, after = both_ways(outer)
+    inner, strength_strips, weight_strips = call(
+        inner_strips_kernel,
+        (strip_shape, shape(1, 4, ROWS, LANES), shape(1, 8, ROWS, LANES)),
+        velocity, ice_cover, strength, mass,
+    )
+
     line = [pltpu.VMEM((2, 4, 48, LANES), F32)]
     faces, rims = call(
         functools.partial(edge_stress_kernel, opening=True),
         (strip_shape, strip_shape),
-        before, outer, after, inner, neighbour, rotation, strength_strips, *parts[1:],
-        specs=[VMEM] * 7 + [ANY] * 3,
+        before, outer, after, inner, neighbour, rotation, strength_strips,
         scratch=line,
+        work=1 << 34,
     )
     before, after = both_ways(faces)
 
     summed = call(
         partial_kernel,
         shape(OWNERS, 2, SLOTS),
-        *parts, air_wind, ocean_current, faces,
-        specs=[VMEM] * 6 + [ANY],
+        *parts, air_wind, ocean_current,
         scratch=[pltpu.VMEM((2, 2, 2, 4 * OWNERS, LANES), F32)],
+        work=1 << 31,
     )
     arrived = lax.all_to_all(summed, "blocks", split_axis=0, concat_axis=0, tiled=True)
 
+    forcing = scatter_call(
+        edge_kernel, 8 * ROWS, shape(2, 8, ROWS, LANES), slot_cell, arrived, count, faces
+    )
     stress_rims = call(
-        stress_rims_kernel, strip_shape, before, faces, after, neighbour, rotation, work=1 << 34
-    )
-    forcing = scatter_call(
-        edge_kernel, 8 * ROWS, shape(2, 8, ROWS, LANES), slot_cell, arrived, count, stress_rims
+        stress_rims_kernel,
+        strip_shape,
+        before, faces, after, neighbour, rotation, forcing,
+        specs=[VMEM] * 5 + [ANY],
     )
     base, stress, outer, inner = call(
         base_kernel,

time: 83.3 us -> 78.1 us (0.938)
  waiting for transfers between devices: 11.5 us -> 3.07 us
  starting transfers between devices: 33.2 us -> 38.2 us
  Pallas kernels: 34.1 us -> 30.7 us
  local copies, waits for them, and re-layouts: 3.06 us -> 4.78 us
    all_to_all x1, waiting for transfers between devices: 9.74 us -> 2.41 us  [shards(): lax.all_to_all(summed, 'blocks', split_axis=0, concat_axis=0, tiled=True)]
    all_to_all x1, starting transfers between devices: 4.86 us -> 9.83 us  [shards(): lax.all_to_all(summed, 'blocks', split_axis=0, concat_axis=0, tiled=True)]
    pallas_call x3, Pallas kernels: 23.7 us -> 20.9 us  [scatter_call(): pl.pallas_call(kernel, out_shape=outs, grid=(OWNERS // CHUNK,), in_specs=...]
    unnamed x30, local copies, waits for them, and re-layouts: 3.06 us -> 4.78 us
    ppermute x3, waiting for transfers between devices: 1.7 us -> 0.01 us  [shards(): lax.ppermute(packed[step], 'cat', [(i, (i + step) % 4) for i in range(4)])]
    ppermute x3, starting transfers between devices: 3.3 us -> 4.16 us  [shards(): lax.ppermute(packed[step], 'cat', [(i, (i + step) % 4) for i in range(4)])]
  transfers between devices with their start and end apart: 12 -> 12, of which waited for: 4 -> 2; matrix products, arithmetic and copies ran while one was open for 0% -> 0% of each run, Pallas kernels for 25% -> 33%
where the time goes in v2:
time: 78.1 us; the launch traced here: 77.8 us
  starting transfers between devices  38.2 us (49%)
  Pallas kernels  30.7 us (39%)
  local copies, waits for them, and re-layouts  4.78 us (6%)
  waiting for transfers between devices  3.07 us (4%)
  between operations  1.07 us (1%)
    ppermute x8, starting transfers between devices, both_ways(): return (lax.ppermute(strips, BOTH, ring), lax.ppermute(strips, BOTH, back))  24.2 us
    pallas_call x3, Pallas kernels, scatter_call(): pl.pallas_call(kernel, out_shape=outs, grid=(OWNERS // CHUNK,), in_specs=...  20.9 us
    all_to_all x1, starting transfers between devices, shards(): lax.all_to_all(summed, 'blocks', split_axis=0, concat_axis=0, tiled=True)  9.83 us
    pallas_call x10, Pallas kernels, call(): pl.pallas_call(kernel, out_shape=outs, in_specs=specs or [VMEM] * len(arg...  9.81 us
    unnamed x30, local copies, waits for them, and re-layouts  4.78 us
    ppermute x3, starting transfers between devices, shards(): lax.ppermute(packed[step], 'cat', [(i, (i + step) % 4) for i in range(4)])  4.16 us
    all_to_all x1, waiting for transfers between devices, shards(): lax.all_to_all(summed, 'blocks', split_axis=0, concat_axis=0, tiled=True)  2.41 us
  transfers between devices with their start and end apart: 12, of which 2 were waited for; matrix products, arithmetic and copies ran while one was open for 0% of the time, Pallas kernels for 33%

profile of v2, /device:TPU:0, one launch (start us, length us, event | category | flops | bytes accessed | tf_op | source)
XLA Modules:
  0.0 77.8 jit_solution(13703733506319275536)
XLA Ops:
  0.6 0.0 copy-start
  0.6 0.0 copy-start.1
  0.7 0.0 copy-start.6
  0.7 1.0 %copy-done.6 = f32[1,1,256,256]{3,2,1,0:T(8,128)S(1)} copy-done((f32[1,1,256,256]{3,2,1,0:T(8,128)S(1)}, f32[1,1,256,256]{3,2,1,0:T(8,128)}, u32[]{:S(2)}) %copy-start.6) | copy-done | bytes 262168
  1.7 0.0 copy-start.10
  1.7 0.7 copy-done.10
  2.4 0.6 shard_map.134
  3.0 0.1 collective-permute-start.4
  3.1 2.7 %collective-permute-start.5 = (f32[72,256]{1,0:T(8,128)S(1)}, f32[72,256]{1,0:T(8,128)S(1)}, u32[]{:S(2)}, u32[]{:S(2)}) collective-permute-start(f32[72,256]{1,0:T(8,128)S(1)} %get-tuple-element.25), channel_id=1, source_target_pairs={{0,2},{1,3},{2,0},{3,1},{4,6},{5,7},{6,4},{7,5},{8,10},{9,11},{10,... | collective-permute-start | bytes 221192 | tf_op jit(solution)/shard_map/ppermute | solution.py:630
  5.8 1.3 %collective-permute-start.6 = (f32[72,256]{1,0:T(8,128)S(1)}, f32[72,256]{1,0:T(8,128)S(1)}, u32[]{:S(2)}, u32[]{:S(2)}) collective-permute-start(f32[72,256]{1,0:T(8,128)S(1)} %get-tuple-element.26), channel_id=1, source_target_pairs={{0,3},{1,0},{2,1},{3,2},{4,7},{5,4},{6,5},{7,6},{8,11},{9,8},{10,9... | collective-permute-start | bytes 221192 | tf_op jit(solution)/shard_map/ppermute | solution.py:630
  7.1 1.9 %shard_map.131.outer_ref = f32[2,4,32,128]{3,2,1,0:T(8,128)} custom-call(f32[30,30,2,128]{3,2,1,0:T(2,128)} %bitcast.8, s32[30,30,128]{2,1,0:T(8,128)} %cover_ref.7), custom_call_target="tpu_custom_call" | custom-call | flops 4194304 | bytes 4194304 | tf_op jit(solution)/shard_map/pallas_call | solution.py:582
  9.0 0.8 collective-permute-start
  9.8 6.5 %collective-permute-start.1 = (f32[2,4,32,128]{3,2,1,0:T(8,128)}, f32[2,4,32,128]{3,2,1,0:T(8,128)S(1)}, u32[]{:S(2)}, u32[]{:S(2)}) collective-permute-start(f32[2,4,32,128]{3,2,1,0:T(8,128)} %shard_map.131.outer_ref), channel_id=1, source_target_pairs={{1,0},{2,1},{3,2},{4,3},{5,4},{6,5},{7,6},{8,7},{9,8},{10,9},{11,1... | collective-permute-start | bytes 393224 | tf_op jit(solution)/shard_map/ppermute | solution.py:612
  16.3 0.0 copy-done
  16.3 0.0 copy-done.1
  16.3 0.0 copy-start.2
  16.3 1.0 %copy-done.2 = f32[30,30,128]{2,1,0:T(8,128)S(1)} copy-done((f32[30,30,128]{2,1,0:T(8,128)S(1)}, f32[30,30,128]{2,1,0:T(8,128)}, u32[]{:S(2)}) %copy-start.2) | copy-done | bytes 460824
  17.3 0.0 copy-start.4
  17.3 1.0 %copy-done.4 = f32[30,30,128]{2,1,0:T(8,128)S(1)} copy-done((f32[30,30,128]{2,1,0:T(8,128)S(1)}, f32[30,30,128]{2,1,0:T(8,128)}, u32[]{:S(2)}) %copy-start.4) | copy-done | bytes 460824
  18.4 0.0 copy-start.11
  18.4 0.0 copy-start.12
  18.4 0.2 shard_map.132
  18.6 0.0 collective-permute-done.4.first_ref
  18.6 0.0 collective-permute-done.5.second_ref
  18.6 0.0 collective-permute-done.6.third_ref
  18.6 0.8 %copy-done.11 = f32[2,1,256,256]{3,2,1,0:T(8,128)S(1)} copy-done((f32[2,1,256,256]{3,2,1,0:T(8,128)S(1)}, f32[2,1,256,256]{3,2,1,0:T(8,128)}, u32[]{:S(2)}) %copy-start.11) | copy-done | bytes 524312
  19.4 0.2 copy-done.12
  19.6 0.0 copy-start.7
  19.6 0.0 copy-start.8
  19.6 0.9 %shard_map.135 = f32[64,2,256]{2,1,0:T(2,128)} custom-call(f32[72,256]{1,0:T(8,128)S(1)} %get-tuple-element.23.mine_ref, f32[72,256]{1,0:T(8,128)S(1)} %collective-permute-done.4.first_ref, f32[72,256]{1,0:T(8,128)S(1)} %collective-permute-done.5.second_ref, f32[72,256]{1,0:T(8,128)S(1)} %collective-permute-done.6.third_ref, ...), custom_call_target="tpu_custom_call" | custom-call | flops 2147483648 | bytes 4194304 | tf_op jit(solution)/shard_map/pallas_call | solution.py:582
  20.5 9.8 %all-to-all-start = ((f32[64,2,256]{2,1,0:T(2,128)}), f32[64,2,256]{2,1,0:T(2,128)S(1)}, u32[]{:S(2)}, u32[]{:S(2)}) async-start(f32[64,2,256]{2,1,0:T(2,128)} %shard_map.135), calls=%async_computation | async-start | bytes 262144 | tf_op jit(solution)/shard_map/all_to_all | solution.py:675
  30.3 0.0 collective-permute-done.before_ref
  30.3 0.0 collective-permute-done.1.after_ref
  30.3 0.0 copy-done.7
  30.3 0.0 copy-done.8
  30.3 0.0 copy-done.9
  30.4 0.0 copy-start.13
  30.4 0.0 copy-start.14
  30.4 0.6 shard_map.133
  30.9 0.1 collective-permute-start.2
  31.0 7.2 %collective-permute-start.3 = (f32[2,4,32,128]{3,2,1,0:T(8,128)S(1)}, f32[2,4,32,128]{3,2,1,0:T(8,128)S(1)}, u32[]{:S(2)}, u32[]{:S(2)}) collective-permute-start(f32[2,4,32,128]{3,2,1,0:T(8,128)S(1)} %get-tuple-element.22.after_ref.own_ref.rest_0_), channel_id=1, source_target_pairs={{1,0},{2,1},{3,2},{4,3},{5,4},{6,5},{7,6},{8,7},{9,8},{10,9},{11,1... | collective-permute-start | bytes 393224 | tf_op jit(solution)/shard_map/ppermute | solution.py:612
  38.2 2.4 %all-to-all-done.value_ref = f32[64,2,256]{2,1,0:T(2,128)S(1)} async-done(((f32[64,2,256]{2,1,0:T(2,128)}), f32[64,2,256]{2,1,0:T(2,128)S(1)}, u32[]{:S(2)}, u32[]{:S(2)}) %all-to-all-start) | async-done | bytes 131104 | tf_op jit(solution)/shard_map/all_to_all | solution.py:675
  40.6 0.0 copy-done.13
  40.6 0.0 copy-done.14
  40.6 5.8 %shard_map.136.forcing_ref = f32[2,8,32,128]{3,2,1,0:T(8,128)S(1)} custom-call(s32[64,1,256]{2,1,0:T(1,128)S(1)} %copy-done.13, f32[64,2,256]{2,1,0:T(2,128)S(1)} %all-to-all-done.value_ref, s32[1,64]{1,0:T(1,128)S(1)} %bitcast.12, f32[2,4,32,128]{3,2,1,0:T(8,128)S(1)} %get-tuple-element.22.after_ref.own_ref.rest_0_), custom_call_target="tpu_custom_call" | custom-call | flops 4294967296 | bytes 1048576 | tf_op jit(solution)/shard_map/pallas_call | solution.py:183
  46.5 0.0 collective-permute-done.2.before_ref
  46.5 0.0 collective-permute-done.3.after_ref
  46.5 0.5 shard_map.137.stress_rims_ref
  47.0 0.0 copy-done.3
  47.0 0.0 copy-done.5
  47.0 1.2 %shard_map.138 = (f32[2,30,30,128]{3,2,1,0:T(8,128)S(1)}, f32[3,30,30,128]{3,2,1,0:T(8,128)S(1)}, f32[2,4,32,128]{3,2,1,0:T(8,128)S(1)}, f32[2,4,32,128]{3,2,1,0:T(8,128)S(1)}) custom-call(f32[2,4,32,128]{3,2,1,0:T(8,128)S(1)} %shard_map.137.stress_rims_ref, f32[2,4,32,128]{3,2,1,0:T(8,128)S(1)} %get-tuple-element.27.rims_ref, f32[1800,128]{1,0:T(8,128)S(1)} %bitcast.10, ...), custom_call_target="tpu_custom_call" | custom-call | flops 4194304 | bytes 4194304 | tf_op jit(solution)/shard_map/pallas_call | solution.py:582
  48.3 0.1 collective-permute-start.7
  48.4 7.2 %collective-permute-start.8 = (f32[2,4,32,128]{3,2,1,0:T(8,128)S(1)}, f32[2,4,32,128]{3,2,1,0:T(8,128)S(1)}, u32[]{:S(2)}, u32[]{:S(2)}) collective-permute-start(f32[2,4,32,128]{3,2,1,0:T(8,128)S(1)} %get-tuple-element.29.outer_ref), channel_id=1, source_target_pairs={{1,0},{2,1},{3,2},{4,3},{5,4},{6,5},{7,6},{8,7},{9,8},{10,9},{11,1... | collective-permute-start | bytes 393224 | tf_op jit(solution)/shard_map/ppermute | solution.py:612
  55.5 7.5 %shard_map.140.low_ref = f32[2,352,128]{2,1,0:T(8,128)S(1)} custom-call(s32[64,1,256]{2,1,0:T(1,128)S(1)} %copy-done.13, f32[64,2,256]{2,1,0:T(2,128)S(1)} %all-to-all-done.value_ref, s32[1,64]{1,0:T(1,128)S(1)} %bitcast.13), custom_call_target="tpu_custom_call" | custom-call | flops 5905580032 | bytes 1048576 | tf_op jit(solution)/shard_map/pallas_call | solution.py:183
  63.1 0.0 collective-permute-done.7.before_ref
  63.1 0.0 collective-permute-done.8.after_ref
  63.1 0.6 shard_map.139
  63.6 2.5 %collective-permute-start.10 = (f32[2,4,32,128]{3,2,1,0:T(8,128)S(1)}, f32[2,4,32,128]{3,2,1,0:T(8,128)S(1)}, u32[]{:S(2)}, u32[]{:S(2)}) collective-permute-start(f32[2,4,32,128]{3,2,1,0:T(8,128)S(1)} %get-tuple-element.31.own_ref), channel_id=1, source_target_pairs={{1,0},{2,1},{3,2},{4,3},{5,4},{6,5},{7,6},{8,7},{9,8},{10,9},{11,1... | collective-permute-start | bytes 393224 | tf_op jit(solution)/shard_map/ppermute | solution.py:612
  66.1 0.0 collective-permute-start.9
  66.1 7.5 %shard_map.141.high_ref = f32[2,352,128]{2,1,0:T(8,128)S(1)} custom-call(s32[64,1,256]{2,1,0:T(1,128)S(1)} %copy-done.13, f32[64,2,256]{2,1,0:T(2,128)S(1)} %all-to-all-done.value_ref, s32[1,64]{1,0:T(1,128)S(1)} %bitcast.14), custom_call_target="tpu_custom_call" | custom-call | flops 5905580032 | bytes 1048576 | tf_op jit(solution)/shard_map/pallas_call | solution.py:183
  73.6 1.6 %shard_map.142 = (f32[2,30,30,128]{3,2,1,0:T(8,128)S(1)}, f32[3,30,30,128]{3,2,1,0:T(8,128)S(1)}, f32[3,30,30,128]{3,2,1,0:T(8,128)}) custom-call(f32[2,30,30,128]{3,2,1,0:T(8,128)S(1)} %get-tuple-element.32.base_ref, s32[30,30,128]{2,1,0:T(8,128)S(1)} %copy-done, f32[30,30,128]{2,1,0:T(8,128)S(1)} %copy-done.3, f32[2,352,128]{2,1,0:T(8,128)S(1)} %shard_map.140.low_ref, ...), custom_call_target="tpu_custom_call" | custom-call | flops 4194304 | bytes 4194304 | tf_op jit(solution)/shard_map/pallas_call | solution.py:582
  75.3 0.0 collective-permute-done.10.after_ref
  75.3 0.6 collective-permute-done.9.before_ref
  75.9 1.7 %shard_map.143 = f32[1800,128]{1,0:T(8,128)} custom-call(f32[2,4,32,128]{3,2,1,0:T(8,128)S(1)} %collective-permute-done.9.before_ref, f32[2,4,32,128]{3,2,1,0:T(8,128)S(1)} %get-tuple-element.31.own_ref, f32[2,4,32,128]{3,2,1,0:T(8,128)S(1)} %collective-permute-done.10.after_ref, s32[4,128]{1,0:T(4,128)S(1)} %copy-done.8, s32[4,128]{1,0:T(4,128)S(1)} %copy-done.9, ...), custom_call_target="tpu_custom_call" | custom-call | flops 4194304 | bytes 4194304 | tf_op jit(solution)/shard_map/pallas_call | solution.py:582
  (3 shorter events, 0.0 us)
Async XLA Ops:
  0.6 15.7 %copy-start = (s32[30,30,128]{2,1,0:T(8,128)S(1)}, s32[30,30,128]{2,1,0:T(8,128)}, u32[]{:S(2)}) copy-start(s32[30,30,128]{2,1,0:T(8,128)} %cover_ref.7) | copy-start | bytes 1382404
  0.6 15.7 %copy-start.1 = (f32[2,30,30,128]{3,0,2,1:T(2,128)S(1)}, f32[2,30,30,128]{3,0,2,1:T(2,128)}, u32[]{:S(2)}) copy-start(f32[2,30,30,128]{3,0,2,1:T(2,128)} %param.12) | copy-start | bytes 2764804
  0.7 1.1 %copy-start.6 = (f32[1,1,256,256]{3,2,1,0:T(8,128)S(1)}, f32[1,1,256,256]{3,2,1,0:T(8,128)}, u32[]{:S(2)}) copy-start(f32[1,1,256,256]{3,2,1,0:T(8,128)} %conc_ref.1) | copy-start | bytes 786436
  1.7 0.7 copy-start.10
  3.0 15.6 %collective-permute-start.4 = (f32[72,256]{1,0:T(8,128)S(1)}, f32[72,256]{1,0:T(8,128)S(1)}, u32[]{:S(2)}, u32[]{:S(2)}) collective-permute-start(f32[72,256]{1,0:T(8,128)S(1)} %get-tuple-element.24), channel_id=1, source_target_pairs={{0,1},{1,2},{2,3},{3,0},{4,5},{5,6},{6,7},{7,4},{8,9},{9,10},{10,1... | collective-permute-start | bytes 221192 | tf_op jit(solution)/shard_map/ppermute | solution.py:630
  3.1 15.5 %collective-permute-start.5 = (f32[72,256]{1,0:T(8,128)S(1)}, f32[72,256]{1,0:T(8,128)S(1)}, u32[]{:S(2)}, u32[]{:S(2)}) collective-permute-start(f32[72,256]{1,0:T(8,128)S(1)} %get-tuple-element.25), channel_id=1, source_target_pairs={{0,2},{1,3},{2,0},{3,1},{4,6},{5,7},{6,4},{7,5},{8,10},{9,11},{10,... | collective-permute-start | bytes 221192 | tf_op jit(solution)/shard_map/ppermute | solution.py:630
  5.8 12.8 %collective-permute-start.6 = (f32[72,256]{1,0:T(8,128)S(1)}, f32[72,256]{1,0:T(8,128)S(1)}, u32[]{:S(2)}, u32[]{:S(2)}) collective-permute-start(f32[72,256]{1,0:T(8,128)S(1)} %get-tuple-element.26), channel_id=1, source_target_pairs={{0,3},{1,0},{2,1},{3,2},{4,7},{5,4},{6,5},{7,6},{8,11},{9,8},{10,9... | collective-permute-start | bytes 221192 | tf_op jit(solution)/shard_map/ppermute | solution.py:630
  9.0 21.3 %collective-permute-start = (f32[2,4,32,128]{3,2,1,0:T(8,128)}, f32[2,4,32,128]{3,2,1,0:T(8,128)S(1)}, u32[]{:S(2)}, u32[]{:S(2)}) collective-permute-start(f32[2,4,32,128]{3,2,1,0:T(8,128)} %shard_map.131.outer_ref), channel_id=1, source_target_pairs={{0,1},{1,2},{2,3},{3,4},{4,5},{5,6},{6,7},{7,8},{8,9},{9,10},{10,1... | collective-permute-start | bytes 393224 | tf_op jit(solution)/shard_map/ppermute | solution.py:612
  9.8 20.5 %collective-permute-start.1 = (f32[2,4,32,128]{3,2,1,0:T(8,128)}, f32[2,4,32,128]{3,2,1,0:T(8,128)S(1)}, u32[]{:S(2)}, u32[]{:S(2)}) collective-permute-start(f32[2,4,32,128]{3,2,1,0:T(8,128)} %shard_map.131.outer_ref), channel_id=1, source_target_pairs={{1,0},{2,1},{3,2},{4,3},{5,4},{6,5},{7,6},{8,7},{9,8},{10,9},{11,1... | collective-permute-start | bytes 393224 | tf_op jit(solution)/shard_map/ppermute | solution.py:612
  16.3 1.0 %copy-start.2 = (f32[30,30,128]{2,1,0:T(8,128)S(1)}, f32[30,30,128]{2,1,0:T(8,128)}, u32[]{:S(2)}) copy-start(f32[30,30,128]{2,1,0:T(8,128)} %mass_ref.7) | copy-start | bytes 1382404
  17.3 1.0 %copy-start.4 = (f32[30,30,128]{2,1,0:T(8,128)S(1)}, f32[30,30,128]{2,1,0:T(8,128)}, u32[]{:S(2)}) copy-start(f32[30,30,128]{2,1,0:T(8,128)} %strength_ref.5) | copy-start | bytes 1382404
  18.4 1.0 %copy-start.11 = (f32[2,1,256,256]{3,2,1,0:T(8,128)S(1)}, f32[2,1,256,256]{3,2,1,0:T(8,128)}, u32[]{:S(2)}) copy-start(f32[2,1,256,256]{3,2,1,0:T(8,128)} %air_ref.1) | copy-start | bytes 1572868
  18.4 1.2 %copy-start.12 = (f32[2,1,256,256]{3,2,1,0:T(8,128)S(1)}, f32[2,1,256,256]{3,2,1,0:T(8,128)}, u32[]{:S(2)}) copy-start(f32[2,1,256,256]{3,2,1,0:T(8,128)} %ocean_ref.1) | copy-start | bytes 1572868
  19.6 10.8 %copy-start.7 = (f32[2,4,32,128]{3,2,1,0:T(8,128)S(1)}, f32[2,4,32,128]{3,2,1,0:T(8,128)}, u32[]{:S(2)}) copy-start(f32[2,4,32,128]{3,2,1,0:T(8,128)} %shard_map.131.outer_ref) | copy-start | bytes 393220
  19.6 10.8 %copy-start.8 = (s32[4,128]{1,0:T(4,128)S(1)}, s32[4,128]{1,0:T(4,128)}, u32[]{:S(2)}) copy-start(s32[4,128]{1,0:T(4,128)} %neighbour_ref.7) | copy-start | bytes 6148
  19.6 10.8 %copy-start.9 = (s32[4,128]{1,0:T(4,128)S(1)}, s32[4,128]{1,0:T(4,128)}, u32[]{:S(2)}) copy-start(s32[4,128]{1,0:T(4,128)} %turn_ref.7) | copy-start | bytes 6148
  20.5 20.1 %all-to-all-start = ((f32[64,2,256]{2,1,0:T(2,128)}), f32[64,2,256]{2,1,0:T(2,128)S(1)}, u32[]{:S(2)}, u32[]{:S(2)}) async-start(f32[64,2,256]{2,1,0:T(2,128)} %shard_map.135), calls=%async_computation | async-start | bytes 262144 | tf_op jit(solution)/shard_map/all_to_all | solution.py:675
  30.4 10.3 %copy-start.13 = (s32[64,1,256]{2,1,0:T(1,128)S(1)}, s32[64,1,256]{2,1,0:T(1,128)}, u32[]{:S(2)}) copy-start(s32[64,1,256]{2,1,0:T(1,128)} %cell_ref.5) | copy-start | bytes 196612
  30.4 10.2 %copy-start.14 = (s32[64,1]{0,1:T(1,128)S(1)}, s32[64,1]{0,1:T(1,128)}, u32[]{:S(2)}) copy-start(s32[64,1]{0,1:T(1,128)} %param.23) | copy-start | bytes 772
  30.9 15.5 %collective-permute-start.2 = (f32[2,4,32,128]{3,2,1,0:T(8,128)S(1)}, f32[2,4,32,128]{3,2,1,0:T(8,128)S(1)}, u32[]{:S(2)}, u32[]{:S(2)}) collective-permute-start(f32[2,4,32,128]{3,2,1,0:T(8,128)S(1)} %get-tuple-element.22.after_ref.own_ref.rest_0_), channel_id=1, source_target_pairs={{0,1},{1,2},{2,3},{3,4},{4,5},{5,6},{6,7},{7,8},{8,9},{9,10},{10,1... | collective-permute-start | bytes 393224 | tf_op jit(solution)/shard_map/ppermute | solution.py:612
  31.0 15.4 %collective-permute-start.3 = (f32[2,4,32,128]{3,2,1,0:T(8,128)S(1)}, f32[2,4,32,128]{3,2,1,0:T(8,128)S(1)}, u32[]{:S(2)}, u32[]{:S(2)}) collective-permute-start(f32[2,4,32,128]{3,2,1,0:T(8,128)S(1)} %get-tuple-element.22.after_ref.own_ref.rest_0_), channel_id=1, source_target_pairs={{1,0},{2,1},{3,2},{4,3},{5,4},{6,5},{7,6},{8,7},{9,8},{10,9},{11,1... | collective-permute-start | bytes 393224 | tf_op jit(solution)/shard_map/ppermute | solution.py:612
  40.6 6.4 %copy-start.3 = (f32[30,30,128]{2,1,0:T(8,128)S(1)}, f32[30,30,128]{2,1,0:T(8,128)}, u32[]{:S(2)}) copy-start(f32[30,30,128]{2,1,0:T(8,128)} %mass_ref.7) | copy-start | bytes 1382404
  40.6 6.4 %copy-start.5 = (f32[30,30,128]{2,1,0:T(8,128)S(1)}, f32[30,30,128]{2,1,0:T(8,128)}, u32[]{:S(2)}) copy-start(f32[30,30,128]{2,1,0:T(8,128)} %strength_ref.5) | copy-start | bytes 1382404
  48.3 14.8 %collective-permute-start.7 = (f32[2,4,32,128]{3,2,1,0:T(8,128)S(1)}, f32[2,4,32,128]{3,2,1,0:T(8,128)S(1)}, u32[]{:S(2)}, u32[]{:S(2)}) collective-permute-start(f32[2,4,32,128]{3,2,1,0:T(8,128)S(1)} %get-tuple-element.29.outer_ref), channel_id=1, source_target_pairs={{0,1},{1,2},{2,3},{3,4},{4,5},{5,6},{6,7},{7,8},{8,9},{9,10},{10,1... | collective-permute-start | bytes 393224 | tf_op jit(solution)/shard_map/ppermute | solution.py:612
  48.4 14.7 %collective-permute-start.8 = (f32[2,4,32,128]{3,2,1,0:T(8,128)S(1)}, f32[2,4,32,128]{3,2,1,0:T(8,128)S(1)}, u32[]{:S(2)}, u32[]{:S(2)}) collective-permute-start(f32[2,4,32,128]{3,2,1,0:T(8,128)S(1)} %get-tuple-element.29.outer_ref), channel_id=1, source_target_pairs={{1,0},{2,1},{3,2},{4,3},{5,4},{6,5},{7,6},{8,7},{9,8},{10,9},{11,1... | collective-permute-start | bytes 393224 | tf_op jit(solution)/shard_map/ppermute | solution.py:612
  63.6 11.7 %collective-permute-start.10 = (f32[2,4,32,128]{3,2,1,0:T(8,128)S(1)}, f32[2,4,32,128]{3,2,1,0:T(8,128)S(1)}, u32[]{:S(2)}, u32[]{:S(2)}) collective-permute-start(f32[2,4,32,128]{3,2,1,0:T(8,128)S(1)} %get-tuple-element.31.own_ref), channel_id=1, source_target_pairs={{1,0},{2,1},{3,2},{4,3},{5,4},{6,5},{7,6},{8,7},{9,8},{10,9},{11,1... | collective-permute-start | bytes 393224 | tf_op jit(solution)/shard_map/ppermute | solution.py:612
  66.1 9.8 %collective-permute-start.9 = (f32[2,4,32,128]{3,2,1,0:T(8,128)S(1)}, f32[2,4,32,128]{3,2,1,0:T(8,128)S(1)}, u32[]{:S(2)}, u32[]{:S(2)}) collective-permute-start(f32[2,4,32,128]{3,2,1,0:T(8,128)S(1)} %get-tuple-element.31.own_ref), channel_id=1, source_target_pairs={{0,1},{1,2},{2,3},{3,4},{4,5},{5,6},{6,7},{7,8},{8,9},{9,10},{10,1... | collective-permute-start | bytes 393224 | tf_op jit(solution)/shard_map/ppermute | solution.py:612

commit v3 on v2

--- a/solution.py
+++ b/solution.py
@@ -42,20 +42,6 @@
 
 def quarter(halves, half, receiver):
     return halves[half, pl.ds(receiver, OWNERS, stride=4), :]
-
-
-def pack_kernel(conc_ref, drag_ref, *rest):
-    outs, halves = rest[:4], rest[4]
-    cat = lax.axis_index("cat")
-    row = lax.broadcasted_iota(I32, (EXTRA, SLOTS), 0)
-    coefficients = jnp.where(row == 0, drag_ref[0, 0], drag_ref[0, 1])
-    fill_halves(halves, lambda lanes: conc_ref[0, 0, :, lanes])
-    for step, out_ref in enumerate(outs):
-        receiver = lax.bitwise_and(cat + step, 3)
-        for half in range(2):
-            lanes = slice(half * LANES, half * LANES + LANES)
-            out_ref[0:OWNERS, lanes] = quarter(halves, half, receiver)
-        out_ref[OWNERS : OWNERS + EXTRA, :] = coefficients
 
 
 def partial_kernel(mine_ref, first_ref, second_ref, third_ref, air_ref, ocean_ref, out_ref, wind):
@@ -205,7 +191,10 @@
 
 def gather_rims(strips, neighbour_ref, turn_ref, store):
     devices = lax.axis_size(BOTH)
-    start = (lax.axis_index(BOTH) - 1) * LANES
+    here = lax.axis_index(BOTH)
+    start = (here - 1) * LANES
+    odd = lax.bitwise_and(here, 1)
+    holders = (2 * odd, 1, 2 - 2 * odd)
     for side in range(4):
         place = lax.rem(
             neighbour_ref[side : side + 1, :] - start + devices * LANES, devices * LANES
@@ -215,7 +204,7 @@
         holder = lax.shift_right_logical(place, 7)
         lane = jnp.broadcast_to(lax.bitwise_and(place, LANES - 1), (ROWS, LANES))
         rows = [jnp.zeros((ROWS, LANES), F32) for _ in range(2)]
-        for where, ref in enumerate(strips):
+        for where, ref in zip(holders, strips):
             for edge in range(4):
                 hits = jnp.broadcast_to((holder == where) & (source == edge), (ROWS, LANES))
                 for member in range(2):
@@ -272,20 +261,37 @@
     return copies
 
 
-def outer_strips_kernel(velocity_hbm, cover_hbm, *rest):
-    out_ref, lines, cover_rows, cover_low, cover_high, sems = rest
+def opening_kernel(conc_hbm, drag_ref, velocity_hbm, cover_hbm, *rest):
+    outs, out_ref = rest[:4], rest[4]
+    halves, lines, cover_rows, cover_low, cover_high, sems = rest[5:]
     last = SIDE - 1
-    pairs = [
-        (velocity_hbm.at[0], lines.at[0]),
-        (velocity_hbm.at[:, 0], lines.at[1]),
-        (velocity_hbm.at[last], lines.at[2]),
-        (velocity_hbm.at[:, last], lines.at[3]),
-        (cover_hbm.at[0], cover_rows.at[0]),
-        (cover_hbm.at[last], cover_rows.at[1]),
-        (cover_hbm.at[:, 0:8], cover_low),
-        (cover_hbm.at[:, 24:SIDE], cover_high),
-    ]
-    for copy in run_copies(pairs, sems):
+    copies = run_copies(
+        [
+            (conc_hbm.at[0, 0, :, 0:LANES], halves.at[0]),
+            (conc_hbm.at[0, 0, :, LANES : 2 * LANES], halves.at[1]),
+            (velocity_hbm.at[0], lines.at[0]),
+            (velocity_hbm.at[:, 0], lines.at[1]),
+            (velocity_hbm.at[last], lines.at[2]),
+            (velocity_hbm.at[:, last], lines.at[3]),
+            (cover_hbm.at[0], cover_rows.at[0]),
+            (cover_hbm.at[last], cover_rows.at[1]),
+            (cover_hbm.at[:, 0:8], cover_low),
+            (cover_hbm.at[:, 24:SIDE], cover_high),
+        ],
+        sems,
+    )
+    cat = lax.axis_index("cat")
+    row = lax.broadcasted_iota(I32, (EXTRA, SLOTS), 0)
+    coefficients = jnp.where(row == 0, drag_ref[0, 0], drag_ref[0, 1])
+    for half in range(2):
+        copies[half].wait()
+    for step, packed_ref in enumerate(outs):
+        receiver = lax.bitwise_xor(cat, step)
+        for half in range(2):
+            lanes = slice(half * LANES, half * LANES + LANES)
+            packed_ref[0:OWNERS, lanes] = quarter(halves, half, receiver)
+        packed_ref[OWNERS : OWNERS + EXTRA, :] = coefficients
+    for copy in copies[2:]:
         copy.wait()
     out_ref[:, :, SIDE:ROWS, :] = jnp.zeros((2, 4, ROWS - SIDE, LANES), F32)
     for side in range(4):
@@ -306,7 +312,14 @@
 
 
 def inner_strips_kernel(
-    velocity_ref, cover_ref, strength_ref, mass_ref, inner_ref, strength_strips_ref, weight_strips_ref
+    velocity_ref,
+    cover_ref,
+    strength_ref,
+    mass_ref,
+    summed_ref,
+    inner_ref,
+    strength_strips_ref,
+    weight_strips_ref,
 ):
     for member in range(2):
         store_strips(
@@ -362,13 +375,13 @@
 
 
 def stress_rims_kernel(
-    before_ref, own_ref, after_ref, neighbour_ref, turn_ref, forcing_ref, out_ref
+    one_ref, own_ref, two_ref, neighbour_ref, turn_ref, forcing_ref, out_ref
 ):
     def store(side, turns, rows):
         for member, rim in enumerate(turned_stress(turns, rows)):
             out_ref[member, side] = rim
 
-    gather_rims((before_ref, own_ref, after_ref), neighbour_ref, turn_ref, store)
+    gather_rims((one_ref, own_ref, two_ref), neighbour_ref, turn_ref, store)
 
 
 def fill_stress(pad, stress_ref):
@@ -430,9 +443,9 @@
 
 
 def edge_stress_kernel(
-    before_ref,
+    one_ref,
     outer_ref,
-    after_ref,
+    two_ref,
     inner_ref,
     neighbour_ref,
     turn_ref,
@@ -446,7 +459,7 @@
         for member, rim in enumerate(turned_vector(turns, rows)):
             rims_ref[member, side] = rim
 
-    gather_rims((before_ref, outer_ref, after_ref), neighbour_ref, turn_ref, store)
+    gather_rims((one_ref, outer_ref, two_ref), neighbour_ref, turn_ref, store)
     faces_ref[:, :, SIDE:ROWS, :] = jnp.zeros((2, 4, ROWS - SIDE, LANES), F32)
     for side in range(4):
         end = 0 if side < 2 else SIDE - 1
@@ -535,9 +548,9 @@
 
 
 def last_kernel(
-    before_ref,
+    one_ref,
     own_ref,
-    after_ref,
+    two_ref,
     neighbour_ref,
     turn_ref,
     moving_ref,
@@ -556,7 +569,7 @@
     def store(side, turns, rows):
         store_stress_rim(pad, side, *turned_stress(turns, rows))
 
-    gather_rims((before_ref, own_ref, after_ref), neighbour_ref, turn_ref, store)
+    gather_rims((one_ref, own_ref, two_ref), neighbour_ref, turn_ref, store)
     for i in range(SIDE):
         force_east, force_north = forces(pad, i)
         eastward, northward = moving_ref[0, i], moving_ref[1, i]
@@ -605,11 +618,11 @@
     slot_count,
 ):
     devices = lax.axis_size(BOTH)
-    ring = [(i, (i + 1) % devices) for i in range(devices)]
-    back = [(j, i) for i, j in ring]
+    pairs = [[(i, i + 1) for i in range(start, devices, 2)] for start in (1, 0)]
+    swaps = [[(i, j % devices) for i, j in p] + [(j % devices, i) for i, j in p] for p in pairs]
 
     def both_ways(strips):
-        return lax.ppermute(strips, BOTH, ring), lax.ppermute(strips, BOTH, back)
+        return [lax.ppermute(strips, BOTH, swap) for swap in swaps]
 
     strip_shape = shape(2, 4, ROWS, LANES)
     block = (SIDE, SIDE, LANES)
@@ -618,53 +631,32 @@
     count = slot_count.reshape(1, OWNERS)
 
     sems = pltpu.SemaphoreType.DMA
-    packed = call(
-        pack_kernel,
-        [shape(OWNERS + EXTRA, SLOTS)] * 4,
+    by_cell = jnp.transpose(velocity, (1, 2, 0, 3))
+    velocity = by_cell.reshape(2 * SIDE * SIDE, LANES)
+    *packed, outer = call(
+        opening_kernel,
+        [shape(OWNERS + EXTRA, SLOTS)] * 4 + [strip_shape],
         concentration,
         drag.reshape(1, 2),
-        specs=[VMEM, SMEM],
-        scratch=[pltpu.VMEM((2, 4 * OWNERS, LANES), F32)],
-    )
-    parts = [packed[0]] + [
-        lax.ppermute(packed[step], "cat", [(i, (i + step) % 4) for i in range(4)])
-        for step in (1, 2, 3)
-    ]
-
-    by_cell = jnp.transpose(velocity, (1, 2, 0, 3))
-    velocity = by_cell.reshape(2 * SIDE * SIDE, LANES)
-    outer = call(
-        outer_strips_kernel,
-        strip_shape,
         by_cell,
         ice_cover,
-        specs=[ANY] * 2,
+        specs=[ANY, SMEM, ANY, ANY],
         scratch=[
+            pltpu.VMEM((2, 4 * OWNERS, LANES), F32),
             pltpu.VMEM((4, SIDE, 2, LANES), F32),
             pltpu.VMEM((2, SIDE, LANES), I32),
             pltpu.VMEM((SIDE, 8, LANES), I32),
             pltpu.VMEM((SIDE, 6, LANES), I32),
-            sems((8,)),
+            sems((10,)),
         ],
         params=ALONE_PARAMS,
     )
-    before, after = both_ways(outer)
-    inner, strength_strips, weight_strips = call(
-        inner_strips_kernel,
-        (strip_shape, shape(1, 4, ROWS, LANES), shape(1, 8, ROWS, LANES)),
-        velocity, ice_cover, strength, mass,
-    )
+    parts = [packed[0]] + [
+        lax.ppermute(packed[step], "cat", [(i, i ^ step) for i in range(4)])
+        for step in (1, 2, 3)
+    ]
 
     line = [pltpu.VMEM((2, 4, 48, LANES), F32)]
-    faces, rims = call(
-        functools.partial(edge_stress_kernel, opening=True),
-        (strip_shape, strip_shape),
-        before, outer, after, inner, neighbour, rotation, strength_strips,
-        scratch=line,
-        work=1 << 34,
-    )
-    before, after = both_ways(faces)
-
     summed = call(
         partial_kernel,
         shape(OWNERS, 2, SLOTS),
@@ -674,13 +666,29 @@
     )
     arrived = lax.all_to_all(summed, "blocks", split_axis=0, concat_axis=0, tiled=True)
 
+    first, second = both_ways(outer)
+    inner, strength_strips, weight_strips = call(
+        inner_strips_kernel,
+        (strip_shape, shape(1, 4, ROWS, LANES), shape(1, 8, ROWS, LANES)),
+        velocity, ice_cover, strength, mass, summed,
+        specs=[VMEM] * 4 + [ANY],
+    )
+    faces, rims = call(
+        functools.partial(edge_stress_kernel, opening=True),
+        (strip_shape, strip_shape),
+        first, outer, second, inner, neighbour, rotation, strength_strips,
+        scratch=line,
+        work=1 << 34,
+    )
+    first, second = both_ways(faces)
+
     forcing = scatter_call(
         edge_kernel, 8 * ROWS, shape(2, 8, ROWS, LANES), slot_cell, arrived, count, faces
     )
     stress_rims = call(
         stress_rims_kernel,
         strip_shape,
-        before, faces, after, neighbour, rotation, forcing,
+        first, faces, second, neighbour, rotation, forcing,
         specs=[VMEM] * 5 + [ANY],
     )
     base, stress, outer, inner = call(
@@ -689,7 +697,7 @@
         stress_rims, rims, velocity, ice_cover, mass, strength, forcing, weight_strips,
         scratch=pad2 + pad3,
     )
-    before, after = both_ways(outer)
+    first, second = both_ways(outer)
     low = scatter_call(
         functools.partial(inside_kernel, 2), HALF_ROWS, shape(2, HALF_ROWS, LANES),
         slot_cell, arrived, count,
@@ -697,10 +705,10 @@
     faces, rims = call(
         functools.partial(edge_stress_kernel, opening=False),
         (strip_shape, strip_shape),
-        before, outer, after, inner, neighbour, rotation, strength_strips, faces,
+        first, outer, second, inner, neighbour, rotation, strength_strips, faces,
         scratch=line,
     )
-    before, after = both_ways(faces)
+    first, second = both_ways(faces)
     high = scatter_call(
         functools.partial(inside_kernel, 2 + HALF), HALF_ROWS, shape(2, HALF_ROWS, LANES),
         slot_cell, arrived, count,
@@ -715,7 +723,7 @@
     moving = call(
         last_kernel,
         shape(2 * SIDE * SIDE, LANES),
-        before, faces, after, neighbour, rotation, moving, base, ice_cover, mass, kept,
+        first, faces, second, neighbour, rotation, moving, base, ice_cover, mass, kept,
         out_specs=ANY,
         scratch=pad3 + [pltpu.VMEM((2 * SIDE * SIDE, LANES), F32), sems((5,))],
     )

time: 78.1 us -> 73.4 us (0.940)
  starting transfers between devices: 38.2 us -> 32.6 us
  waiting for transfers between devices: 3.07 us -> 7.41 us
  local copies, waits for them, and re-layouts: 4.78 us -> 0.93 us
    ppermute x11, starting transfers between devices: 28.4 us -> 23.2 us  [the longest x8 18.4 us: both_ways(): return [lax.ppermute(strips, BOTH, swap) for swap in swaps]]
    unnamed x30 -> x24, local copies, waits for them, and re-layouts: 4.78 us -> 0.93 us
    all_to_all x1, waiting for transfers between devices: 2.41 us -> 5.38 us  [shards(): lax.all_to_all(summed, 'blocks', split_axis=0, concat_axis=0, tiled=True)]
    ppermute x11, waiting for transfers between devices: 0.66 us -> 2.03 us  [the longest x8 2.03 us: both_ways(): return [lax.ppermute(strips, BOTH, swap) for swap in swaps]]
    pallas_call x10 -> x9, Pallas kernels: 9.81 us -> 10.3 us  [call(): pl.pallas_call(kernel, out_shape=outs, in_specs=specs or [VMEM] * len(arg...]
where the time goes in v3:
time: 73.4 us; the launch traced here: 73.2 us
  starting transfers between devices  32.6 us (44%)
  Pallas kernels  31.2 us (43%)
  waiting for transfers between devices  7.41 us (10%)
  between operations  1.06 us (1%)
  local copies, waits for them, and re-layouts  0.93 us (1%)
    pallas_call x3, Pallas kernels, scatter_call(): pl.pallas_call(kernel, out_shape=outs, grid=(OWNERS // CHUNK,), in_specs=...  20.9 us
    ppermute x8, starting transfers between devices, both_ways(): return [lax.ppermute(strips, BOTH, swap) for swap in swaps]  18.4 us
    pallas_call x9, Pallas kernels, call(): pl.pallas_call(kernel, out_shape=outs, in_specs=specs or [VMEM] * len(arg...  10.3 us
    all_to_all x1, starting transfers between devices, shards(): lax.all_to_all(summed, 'blocks', split_axis=0, concat_axis=0, tiled=True)  9.44 us
    all_to_all x1, waiting for transfers between devices, shards(): lax.all_to_all(summed, 'blocks', split_axis=0, concat_axis=0, tiled=True)  5.38 us
    ppermute x3, starting transfers between devices, shards(): lax.ppermute(packed[step], 'cat', [(i, i ^ step) for i in range(4)])  4.78 us
    ppermute x8, waiting for transfers between devices, both_ways(): return [lax.ppermute(strips, BOTH, swap) for swap in swaps]  2.03 us
  transfers between devices with their start and end apart: 12, of which 2 were waited for; matrix products, arithmetic and copies ran while one was open for 0% of the time, Pallas kernels for 33%

profile of v3, /device:TPU:0, one launch (start us, length us, event | category | flops | bytes accessed | tf_op | source)
XLA Modules:
  0.0 73.2 jit_solution(9385226622034376736)
XLA Ops:
  0.6 0.0 copy-start.6
  0.6 0.0 copy-start.7
  0.7 2.9 %shard_map.131 = (f32[72,256]{1,0:T(8,128)}, f32[72,256]{1,0:T(8,128)}, f32[72,256]{1,0:T(8,128)}, f32[72,256]{1,0:T(8,128)}, f32[2,4,32,128]{3,2,1,0:T(8,128)}) custom-call(f32[1,1,256,256]{3,2,1,0:T(8,128)} %conc_hbm.1, f32[1,2]{1,0:T(1,128)} %bitcast.15, f32[30,30,2,128]{3,2,1,0:T(2,128)} %bitcast.8, s32[30,30,128]{2,1,0:T(8,128)} %cover_ref.7), custom_call_target="tpu_custom_call" | custom-call | flops 4194304 | bytes 4194304 | tf_op jit(solution)/shard_map/pallas_call | solution.py:595
  3.5 0.1 collective-permute-start.2
  3.6 2.7 %collective-permute-start.3 = (f32[72,256]{1,0:T(8,128)}, f32[72,256]{1,0:T(8,128)S(1)}, u32[]{:S(2)}, u32[]{:S(2)}) collective-permute-start(f32[72,256]{1,0:T(8,128)} %get-tuple-element.24), channel_id=1, source_target_pairs={{0,2},{1,3},{2,0},{3,1},{4,6},{5,7},{6,4},{7,5},{8,10},{9,11},{10,... | collective-permute-start | bytes 221192 | tf_op jit(solution)/shard_map/ppermute | solution.py:655
  6.4 2.0 %collective-permute-start.4 = (f32[72,256]{1,0:T(8,128)}, f32[72,256]{1,0:T(8,128)S(1)}, u32[]{:S(2)}, u32[]{:S(2)}) collective-permute-start(f32[72,256]{1,0:T(8,128)} %get-tuple-element.25), channel_id=1, source_target_pairs={{0,3},{1,2},{2,1},{3,0},{4,7},{5,6},{6,5},{7,4},{8,11},{9,10},{10,... | collective-permute-start | bytes 221192 | tf_op jit(solution)/shard_map/ppermute | solution.py:655
  8.3 7.4 %collective-permute-start = (f32[2,4,32,128]{3,2,1,0:T(8,128)}, f32[2,4,32,128]{3,2,1,0:T(8,128)S(1)}, u32[]{:S(2)}, u32[]{:S(2)}) collective-permute-start(f32[2,4,32,128]{3,2,1,0:T(8,128)} %get-tuple-element.21.outer_ref), channel_id=1, source_target_pairs={{1,2},{3,4},{5,6},{7,8},{9,10},{11,12},{13,14},{15,16},{17,18},{19... | collective-permute-start | bytes 393224 | tf_op jit(solution)/shard_map/ppermute | solution.py:625
  15.7 0.0 collective-permute-start.1
  15.7 0.0 collective-permute-done.2.first_ref
  15.7 0.0 collective-permute-done.3.second_ref
  15.7 0.0 collective-permute-done.4.third_ref
  15.7 0.0 copy-done.6
  15.7 0.0 copy-done.7
  15.7 0.0 copy-start.9
  15.7 0.9 %copy-done.9 = f32[72,256]{1,0:T(8,128)S(1)} copy-done((f32[72,256]{1,0:T(8,128)S(1)}, f32[72,256]{1,0:T(8,128)}, u32[]{:S(2)}) %copy-start.9) | copy-done | bytes 73752
  16.6 0.0 copy-start
  16.6 0.0 copy-start.1
  16.6 0.0 copy-start.2
  16.6 0.0 copy-start.3
  16.6 0.9 %shard_map.132.summed_ref = f32[64,2,256]{2,1,0:T(2,128)} custom-call(f32[72,256]{1,0:T(8,128)S(1)} %copy-done.9, f32[72,256]{1,0:T(8,128)S(1)} %collective-permute-done.2.first_ref, f32[72,256]{1,0:T(8,128)S(1)} %collective-permute-done.3.second_ref, f32[72,256]{1,0:T(8,128)S(1)} %collective-permute-done.4.third_ref, f32[2,1,256,256]{3,2,1,0:T(8,128)S(1)} %copy-done.6, ...), custom_call_target="tpu_custom_call" | custom-call | flops 2147483648 | bytes 4194304 | tf_op jit(solution)/shard_map/pallas_call | solution.py:595
  17.5 0.0 copy-start.4
  17.5 0.0 copy-start.5
  17.5 0.0 copy-start.8
  17.5 9.4 %all-to-all-start = ((f32[64,2,256]{2,1,0:T(2,128)}), f32[64,2,256]{2,1,0:T(2,128)S(1)}, u32[]{:S(2)}, u32[]{:S(2)}) async-start(f32[64,2,256]{2,1,0:T(2,128)} %shard_map.132.summed_ref), calls=%async_computation | async-start | bytes 262144 | tf_op jit(solution)/shard_map/all_to_all | solution.py:667
  27.0 0.0 copy-done
  27.0 0.0 copy-done.1
  27.0 0.0 copy-done.2
  27.0 0.0 copy-done.3
  27.0 0.2 shard_map.133
  27.2 0.0 collective-permute-done.one_ref
  27.2 0.0 collective-permute-done.1.two_ref
  27.3 0.0 copy-done.4
  27.3 0.0 copy-done.5
  27.3 0.0 copy-done.8
  27.3 0.0 copy-start.10
  27.3 0.0 copy-start.11
  27.3 0.6 shard_map.134
  27.9 4.0 %collective-permute-start.5 = (f32[2,4,32,128]{3,2,1,0:T(8,128)S(1)}, f32[2,4,32,128]{3,2,1,0:T(8,128)S(1)}, u32[]{:S(2)}, u32[]{:S(2)}) collective-permute-start(f32[2,4,32,128]{3,2,1,0:T(8,128)S(1)} %get-tuple-element.28.after_ref.own_ref.rest_0_), channel_id=1, source_target_pairs={{1,2},{3,4},{5,6},{7,8},{9,10},{11,12},{13,14},{15,16},{17,18},{19... | collective-permute-start | bytes 393224 | tf_op jit(solution)/shard_map/ppermute | solution.py:625
  31.9 0.0 collective-permute-start.6
  31.9 5.4 %all-to-all-done.value_ref = f32[64,2,256]{2,1,0:T(2,128)S(1)} async-done(((f32[64,2,256]{2,1,0:T(2,128)}), f32[64,2,256]{2,1,0:T(2,128)S(1)}, u32[]{:S(2)}, u32[]{:S(2)}) %all-to-all-start) | async-done | bytes 131104 | tf_op jit(solution)/shard_map/all_to_all | solution.py:667
  37.3 0.0 copy-done.10
  37.3 0.0 copy-done.11
  37.3 5.8 %shard_map.135.forcing_ref = f32[2,8,32,128]{3,2,1,0:T(8,128)S(1)} custom-call(s32[64,1,256]{2,1,0:T(1,128)S(1)} %copy-done.10, f32[64,2,256]{2,1,0:T(2,128)S(1)} %all-to-all-done.value_ref, s32[1,64]{1,0:T(1,128)S(1)} %bitcast.11, f32[2,4,32,128]{3,2,1,0:T(8,128)S(1)} %get-tuple-element.28.after_ref.own_ref.rest_0_), custom_call_target="tpu_custom_call" | custom-call | flops 4294967296 | bytes 1048576 | tf_op jit(solution)/shard_map/pallas_call | solution.py:169
  43.1 0.0 collective-permute-done.5.one_ref
  43.1 0.0 collective-permute-done.6.two_ref
  43.1 0.5 shard_map.136.stress_rims_ref
  43.7 1.3 %shard_map.137 = (f32[2,30,30,128]{3,2,1,0:T(8,128)S(1)}, f32[3,30,30,128]{3,2,1,0:T(8,128)S(1)}, f32[2,4,32,128]{3,2,1,0:T(8,128)S(1)}, f32[2,4,32,128]{3,2,1,0:T(8,128)S(1)}) custom-call(f32[2,4,32,128]{3,2,1,0:T(8,128)S(1)} %shard_map.136.stress_rims_ref, f32[2,4,32,128]{3,2,1,0:T(8,128)S(1)} %get-tuple-element.29.rims_ref, f32[1800,128]{1,0:T(8,128)S(1)} %bitcast.10, ...), custom_call_target="tpu_custom_call" | custom-call | flops 4194304 | bytes 4194304 | tf_op jit(solution)/shard_map/pallas_call | solution.py:595
  44.9 0.1 collective-permute-start.7
  45.1 0.2 collective-permute-start.8
  45.3 7.5 %shard_map.139.low_ref = f32[2,352,128]{2,1,0:T(8,128)S(1)} custom-call(s32[64,1,256]{2,1,0:T(1,128)S(1)} %copy-done.10, f32[64,2,256]{2,1,0:T(2,128)S(1)} %all-to-all-done.value_ref, s32[1,64]{1,0:T(1,128)S(1)} %bitcast.12), custom_call_target="tpu_custom_call" | custom-call | flops 5905580032 | bytes 1048576 | tf_op jit(solution)/shard_map/pallas_call | solution.py:169
  52.8 2.0 %collective-permute-done.7.one_ref = f32[2,4,32,128]{3,2,1,0:T(8,128)S(1)} collective-permute-done((f32[2,4,32,128]{3,2,1,0:T(8,128)S(1)}, f32[2,4,32,128]{3,2,1,0:T(8,128)S(1)}, u32[]{:S(2)}, u32[]{:S(2)}) %collective-permute-start.7) | collective-permute-done | bytes 131104 | tf_op jit(solution)/shard_map/ppermute | solution.py:625
  54.9 0.0 collective-permute-done.8.two_ref
  54.9 0.5 shard_map.138
  55.4 0.3 collective-permute-start.10
  55.7 6.4 %collective-permute-start.9 = (f32[2,4,32,128]{3,2,1,0:T(8,128)S(1)}, f32[2,4,32,128]{3,2,1,0:T(8,128)S(1)}, u32[]{:S(2)}, u32[]{:S(2)}) collective-permute-start(f32[2,4,32,128]{3,2,1,0:T(8,128)S(1)} %get-tuple-element.33.own_ref), channel_id=1, source_target_pairs={{1,2},{3,4},{5,6},{7,8},{9,10},{11,12},{13,14},{15,16},{17,18},{19... | collective-permute-start | bytes 393224 | tf_op jit(solution)/shard_map/ppermute | solution.py:625
  62.0 7.5 %shard_map.140.high_ref = f32[2,352,128]{2,1,0:T(8,128)S(1)} custom-call(s32[64,1,256]{2,1,0:T(1,128)S(1)} %copy-done.10, f32[64,2,256]{2,1,0:T(2,128)S(1)} %all-to-all-done.value_ref, s32[1,64]{1,0:T(1,128)S(1)} %bitcast.13), custom_call_target="tpu_custom_call" | custom-call | flops 5905580032 | bytes 1048576 | tf_op jit(solution)/shard_map/pallas_call | solution.py:169
  69.6 1.7 %shard_map.141 = (f32[2,30,30,128]{3,2,1,0:T(8,128)S(1)}, f32[3,30,30,128]{3,2,1,0:T(8,128)S(1)}, f32[3,30,30,128]{3,2,1,0:T(8,128)}) custom-call(f32[2,30,30,128]{3,2,1,0:T(8,128)S(1)} %get-tuple-element.34.base_ref, s32[30,30,128]{2,1,0:T(8,128)S(1)} %copy-done, f32[30,30,128]{2,1,0:T(8,128)S(1)} %copy-done.2, f32[2,352,128]{2,1,0:T(8,128)S(1)} %shard_map.139.low_ref, ...), custom_call_target="tpu_custom_call" | custom-call | flops 4194304 | bytes 4194304 | tf_op jit(solution)/shard_map/pallas_call | solution.py:595
  71.2 0.0 collective-permute-done.10.two_ref
  71.3 0.0 collective-permute-done.9.one_ref
  71.3 1.8 %shard_map.142 = f32[1800,128]{1,0:T(8,128)} custom-call(f32[2,4,32,128]{3,2,1,0:T(8,128)S(1)} %collective-permute-done.9.one_ref, f32[2,4,32,128]{3,2,1,0:T(8,128)S(1)} %get-tuple-element.33.own_ref, f32[2,4,32,128]{3,2,1,0:T(8,128)S(1)} %collective-permute-done.10.two_ref, s32[4,128]{1,0:T(4,128)S(1)} %copy-done.4, s32[4,128]{1,0:T(4,128)S(1)} %copy-done.5, ...), custom_call_target="tpu_custom_call" | custom-call | flops 4194304 | bytes 4194304 | tf_op jit(solution)/shard_map/pallas_call | solution.py:595
Async XLA Ops:
  0.6 15.1 %copy-start.6 = (f32[2,1,256,256]{3,2,1,0:T(8,128)S(1)}, f32[2,1,256,256]{3,2,1,0:T(8,128)}, u32[]{:S(2)}) copy-start(f32[2,1,256,256]{3,2,1,0:T(8,128)} %air_ref.1) | copy-start | bytes 1572868
  0.6 15.1 %copy-start.7 = (f32[2,1,256,256]{3,2,1,0:T(8,128)S(1)}, f32[2,1,256,256]{3,2,1,0:T(8,128)}, u32[]{:S(2)}) copy-start(f32[2,1,256,256]{3,2,1,0:T(8,128)} %ocean_ref.1) | copy-start | bytes 1572868
  3.5 12.2 %collective-permute-start.2 = (f32[72,256]{1,0:T(8,128)}, f32[72,256]{1,0:T(8,128)S(1)}, u32[]{:S(2)}, u32[]{:S(2)}) collective-permute-start(f32[72,256]{1,0:T(8,128)} %get-tuple-element.23), channel_id=1, source_target_pairs={{0,1},{1,0},{2,3},{3,2},{4,5},{5,4},{6,7},{7,6},{8,9},{9,8},{10,11... | collective-permute-start | bytes 221192 | tf_op jit(solution)/shard_map/ppermute | solution.py:655
  3.6 12.1 %collective-permute-start.3 = (f32[72,256]{1,0:T(8,128)}, f32[72,256]{1,0:T(8,128)S(1)}, u32[]{:S(2)}, u32[]{:S(2)}) collective-permute-start(f32[72,256]{1,0:T(8,128)} %get-tuple-element.24), channel_id=1, source_target_pairs={{0,2},{1,3},{2,0},{3,1},{4,6},{5,7},{6,4},{7,5},{8,10},{9,11},{10,... | collective-permute-start | bytes 221192 | tf_op jit(solution)/shard_map/ppermute | solution.py:655
  6.4 9.3 %collective-permute-start.4 = (f32[72,256]{1,0:T(8,128)}, f32[72,256]{1,0:T(8,128)S(1)}, u32[]{:S(2)}, u32[]{:S(2)}) collective-permute-start(f32[72,256]{1,0:T(8,128)} %get-tuple-element.25), channel_id=1, source_target_pairs={{0,3},{1,2},{2,1},{3,0},{4,7},{5,6},{6,5},{7,4},{8,11},{9,10},{10,... | collective-permute-start | bytes 221192 | tf_op jit(solution)/shard_map/ppermute | solution.py:655
  8.3 18.9 %collective-permute-start = (f32[2,4,32,128]{3,2,1,0:T(8,128)}, f32[2,4,32,128]{3,2,1,0:T(8,128)S(1)}, u32[]{:S(2)}, u32[]{:S(2)}) collective-permute-start(f32[2,4,32,128]{3,2,1,0:T(8,128)} %get-tuple-element.21.outer_ref), channel_id=1, source_target_pairs={{1,2},{3,4},{5,6},{7,8},{9,10},{11,12},{13,14},{15,16},{17,18},{19... | collective-permute-start | bytes 393224 | tf_op jit(solution)/shard_map/ppermute | solution.py:625
  15.7 11.6 %collective-permute-start.1 = (f32[2,4,32,128]{3,2,1,0:T(8,128)}, f32[2,4,32,128]{3,2,1,0:T(8,128)S(1)}, u32[]{:S(2)}, u32[]{:S(2)}) collective-permute-start(f32[2,4,32,128]{3,2,1,0:T(8,128)} %get-tuple-element.21.outer_ref), channel_id=1, source_target_pairs={{0,1},{2,3},{4,5},{6,7},{8,9},{10,11},{12,13},{14,15},{16,17},{18,... | collective-permute-start | bytes 393224 | tf_op jit(solution)/shard_map/ppermute | solution.py:625
  15.7 0.9 %copy-start.9 = (f32[72,256]{1,0:T(8,128)S(1)}, f32[72,256]{1,0:T(8,128)}, u32[]{:S(2)}) copy-start(f32[72,256]{1,0:T(8,128)} %get-tuple-element.22.mine_ref) | copy-start | bytes 221188
  16.6 10.4 %copy-start = (s32[30,30,128]{2,1,0:T(8,128)S(1)}, s32[30,30,128]{2,1,0:T(8,128)}, u32[]{:S(2)}) copy-start(s32[30,30,128]{2,1,0:T(8,128)} %cover_ref.7) | copy-start | bytes 1382404
  16.6 10.4 %copy-start.1 = (f32[2,30,30,128]{3,0,2,1:T(2,128)S(1)}, f32[2,30,30,128]{3,0,2,1:T(2,128)}, u32[]{:S(2)}) copy-start(f32[2,30,30,128]{3,0,2,1:T(2,128)} %param.12) | copy-start | bytes 2764804
  16.6 10.4 %copy-start.2 = (f32[30,30,128]{2,1,0:T(8,128)S(1)}, f32[30,30,128]{2,1,0:T(8,128)}, u32[]{:S(2)}) copy-start(f32[30,30,128]{2,1,0:T(8,128)} %mass_ref.7) | copy-start | bytes 1382404
  16.6 10.4 %copy-start.3 = (f32[30,30,128]{2,1,0:T(8,128)S(1)}, f32[30,30,128]{2,1,0:T(8,128)}, u32[]{:S(2)}) copy-start(f32[30,30,128]{2,1,0:T(8,128)} %strength_ref.5) | copy-start | bytes 1382404
  17.5 9.7 %copy-start.4 = (s32[4,128]{1,0:T(4,128)S(1)}, s32[4,128]{1,0:T(4,128)}, u32[]{:S(2)}) copy-start(s32[4,128]{1,0:T(4,128)} %neighbour_ref.7) | copy-start | bytes 6148
  17.5 9.7 %copy-start.5 = (s32[4,128]{1,0:T(4,128)S(1)}, s32[4,128]{1,0:T(4,128)}, u32[]{:S(2)}) copy-start(s32[4,128]{1,0:T(4,128)} %turn_ref.7) | copy-start | bytes 6148
  17.5 9.7 %copy-start.8 = (f32[2,4,32,128]{3,2,1,0:T(8,128)S(1)}, f32[2,4,32,128]{3,2,1,0:T(8,128)}, u32[]{:S(2)}) copy-start(f32[2,4,32,128]{3,2,1,0:T(8,128)} %get-tuple-element.21.outer_ref) | copy-start | bytes 393220
  17.5 19.7 %all-to-all-start = ((f32[64,2,256]{2,1,0:T(2,128)}), f32[64,2,256]{2,1,0:T(2,128)S(1)}, u32[]{:S(2)}, u32[]{:S(2)}) async-start(f32[64,2,256]{2,1,0:T(2,128)} %shard_map.132.summed_ref), calls=%async_computation | async-start | bytes 262144 | tf_op jit(solution)/shard_map/all_to_all | solution.py:667
  27.3 10.0 %copy-start.10 = (s32[64,1,256]{2,1,0:T(1,128)S(1)}, s32[64,1,256]{2,1,0:T(1,128)}, u32[]{:S(2)}) copy-start(s32[64,1,256]{2,1,0:T(1,128)} %cell_ref.5) | copy-start | bytes 196612
  27.3 10.0 %copy-start.11 = (s32[64,1]{0,1:T(1,128)S(1)}, s32[64,1]{0,1:T(1,128)}, u32[]{:S(2)}) copy-start(s32[64,1]{0,1:T(1,128)} %param.23) | copy-start | bytes 772
  27.9 15.3 %collective-permute-start.5 = (f32[2,4,32,128]{3,2,1,0:T(8,128)S(1)}, f32[2,4,32,128]{3,2,1,0:T(8,128)S(1)}, u32[]{:S(2)}, u32[]{:S(2)}) collective-permute-start(f32[2,4,32,128]{3,2,1,0:T(8,128)S(1)} %get-tuple-element.28.after_ref.own_ref.rest_0_), channel_id=1, source_target_pairs={{1,2},{3,4},{5,6},{7,8},{9,10},{11,12},{13,14},{15,16},{17,18},{19... | collective-permute-start | bytes 393224 | tf_op jit(solution)/shard_map/ppermute | solution.py:625
  31.9 11.2 %collective-permute-start.6 = (f32[2,4,32,128]{3,2,1,0:T(8,128)S(1)}, f32[2,4,32,128]{3,2,1,0:T(8,128)S(1)}, u32[]{:S(2)}, u32[]{:S(2)}) collective-permute-start(f32[2,4,32,128]{3,2,1,0:T(8,128)S(1)} %get-tuple-element.28.after_ref.own_ref.rest_0_), channel_id=1, source_target_pairs={{0,1},{2,3},{4,5},{6,7},{8,9},{10,11},{12,13},{14,15},{16,17},{18,... | collective-permute-start | bytes 393224 | tf_op jit(solution)/shard_map/ppermute | solution.py:625
  44.9 9.9 %collective-permute-start.7 = (f32[2,4,32,128]{3,2,1,0:T(8,128)S(1)}, f32[2,4,32,128]{3,2,1,0:T(8,128)S(1)}, u32[]{:S(2)}, u32[]{:S(2)}) collective-permute-start(f32[2,4,32,128]{3,2,1,0:T(8,128)S(1)} %get-tuple-element.31.outer_ref), channel_id=1, source_target_pairs={{1,2},{3,4},{5,6},{7,8},{9,10},{11,12},{13,14},{15,16},{17,18},{19... | collective-permute-start | bytes 393224 | tf_op jit(solution)/shard_map/ppermute | solution.py:625
  45.1 9.8 %collective-permute-start.8 = (f32[2,4,32,128]{3,2,1,0:T(8,128)S(1)}, f32[2,4,32,128]{3,2,1,0:T(8,128)S(1)}, u32[]{:S(2)}, u32[]{:S(2)}) collective-permute-start(f32[2,4,32,128]{3,2,1,0:T(8,128)S(1)} %get-tuple-element.31.outer_ref), channel_id=1, source_target_pairs={{0,1},{2,3},{4,5},{6,7},{8,9},{10,11},{12,13},{14,15},{16,17},{18,... | collective-permute-start | bytes 393224 | tf_op jit(solution)/shard_map/ppermute | solution.py:625
  55.4 15.8 %collective-permute-start.10 = (f32[2,4,32,128]{3,2,1,0:T(8,128)S(1)}, f32[2,4,32,128]{3,2,1,0:T(8,128)S(1)}, u32[]{:S(2)}, u32[]{:S(2)}) collective-permute-start(f32[2,4,32,128]{3,2,1,0:T(8,128)S(1)} %get-tuple-element.33.own_ref), channel_id=1, source_target_pairs={{0,1},{2,3},{4,5},{6,7},{8,9},{10,11},{12,13},{14,15},{16,17},{18,... | collective-permute-start | bytes 393224 | tf_op jit(solution)/shard_map/ppermute | solution.py:625
  55.7 15.6 %collective-permute-start.9 = (f32[2,4,32,128]{3,2,1,0:T(8,128)S(1)}, f32[2,4,32,128]{3,2,1,0:T(8,128)S(1)}, u32[]{:S(2)}, u32[]{:S(2)}) collective-permute-start(f32[2,4,32,128]{3,2,1,0:T(8,128)S(1)} %get-tuple-element.33.own_ref), channel_id=1, source_target_pairs={{1,2},{3,4},{5,6},{7,8},{9,10},{11,12},{13,14},{15,16},{17,18},{19... | collective-permute-start | bytes 393224 | tf_op jit(solution)/shard_map/ppermute | solution.py:625

commit v4 on v3

--- a/solution.py
+++ b/solution.py
@@ -44,27 +44,33 @@
     return halves[half, pl.ds(receiver, OWNERS, stride=4), :]
 
 
-def partial_kernel(mine_ref, first_ref, second_ref, third_ref, air_ref, ocean_ref, out_ref, wind):
+def wind_kernel(air_ref, ocean_ref, out_ref, wind):
     cat = lax.axis_index("cat")
-    parts = (mine_ref, first_ref, second_ref, third_ref)
     for which, ref in enumerate((air_ref, ocean_ref)):
         for member in range(2):
             fill_halves(wind.at[which, member], lambda lanes: ref[member, 0, :, lanes])
     for half in range(2):
         lanes = slice(half * LANES, half * LANES + LANES)
-        totals = [0.0, 0.0]
         for which in range(2):
-            weight = jnp.zeros((OWNERS, LANES), F32)
-            at = OWNERS + which
-            for part in parts:
-                weight += part[0:OWNERS, lanes] * part[at : at + 1, lanes]
             east = quarter(wind.at[which, 0], half, cat)
             north = quarter(wind.at[which, 1], half, cat)
-            weight *= jnp.sqrt(east * east + north * north)
-            totals[0] += weight * east
-            totals[1] += weight * north
-        out_ref[:, 0, lanes] = totals[0]
-        out_ref[:, 1, lanes] = totals[1]
+            speed = jnp.sqrt(east * east + north * north)
+            out_ref[2 * which, :, lanes] = speed * east
+            out_ref[2 * which + 1, :, lanes] = speed * north
+
+
+def partial_kernel(mine_ref, first_ref, second_ref, third_ref, wind_ref, out_ref):
+    parts = (mine_ref, first_ref, second_ref, third_ref)
+    totals = [0.0, 0.0]
+    for which in range(2):
+        at = OWNERS + which
+        weight = jnp.zeros((OWNERS, SLOTS), F32)
+        for part in parts:
+            weight += part[0:OWNERS, :] * part[at : at + 1, :]
+        for member in range(2):
+            totals[member] += weight * wind_ref[2 * which + member]
+    for member in range(2):
+        out_ref[:, member, :] = totals[member]
 
 
 def split_lanes(lane_hits, value):
@@ -261,14 +267,39 @@
     return copies
 
 
-def opening_kernel(conc_hbm, drag_ref, velocity_hbm, cover_hbm, *rest):
-    outs, out_ref = rest[:4], rest[4]
-    halves, lines, cover_rows, cover_low, cover_high, sems = rest[5:]
+def pack_kernel(conc_hbm, drag_ref, *rest):
+    outs, halves, sems = rest[:4], rest[4], rest[5]
+    cuts = [(half, start) for half in range(2) for start in (0, 2 * OWNERS)]
+    copies = run_copies(
+        [
+            (
+                conc_hbm.at[0, 0, pl.ds(start, 2 * OWNERS), half * LANES : half * LANES + LANES],
+                halves.at[half, pl.ds(start, 2 * OWNERS)],
+            )
+            for half, start in cuts
+        ],
+        sems,
+    )
+    cat = lax.axis_index("cat")
+    row = lax.broadcasted_iota(I32, (EXTRA, SLOTS), 0)
+    coefficients = jnp.where(row == 0, drag_ref[0, 0], drag_ref[0, 1])
+    for packed_ref in outs:
+        packed_ref[OWNERS : OWNERS + EXTRA, :] = coefficients
+    for copy in copies:
+        copy.wait()
+    for step, packed_ref in enumerate(outs):
+        receiver = lax.bitwise_xor(cat, step)
+        for half in range(2):
+            lanes = slice(half * LANES, half * LANES + LANES)
+            packed_ref[0:OWNERS, lanes] = quarter(halves, half, receiver)
+
+
+def outer_strips_kernel(
+    velocity_hbm, cover_hbm, out_ref, lines, cover_rows, cover_low, cover_high, sems
+):
     last = SIDE - 1
     copies = run_copies(
         [
-            (conc_hbm.at[0, 0, :, 0:LANES], halves.at[0]),
-            (conc_hbm.at[0, 0, :, LANES : 2 * LANES], halves.at[1]),
             (velocity_hbm.at[0], lines.at[0]),
             (velocity_hbm.at[:, 0], lines.at[1]),
             (velocity_hbm.at[last], lines.at[2]),
@@ -280,18 +311,7 @@
         ],
         sems,
     )
-    cat = lax.axis_index("cat")
-    row = lax.broadcasted_iota(I32, (EXTRA, SLOTS), 0)
-    coefficients = jnp.where(row == 0, drag_ref[0, 0], drag_ref[0, 1])
-    for half in range(2):
-        copies[half].wait()
-    for step, packed_ref in enumerate(outs):
-        receiver = lax.bitwise_xor(cat, step)
-        for half in range(2):
-            lanes = slice(half * LANES, half * LANES + LANES)
-            packed_ref[0:OWNERS, lanes] = quarter(halves, half, receiver)
-        packed_ref[OWNERS : OWNERS + EXTRA, :] = coefficients
-    for copy in copies[2:]:
+    for copy in copies:
         copy.wait()
     out_ref[:, :, SIDE:ROWS, :] = jnp.zeros((2, 4, ROWS - SIDE, LANES), F32)
     for side in range(4):
@@ -633,39 +653,46 @@
     sems = pltpu.SemaphoreType.DMA
     by_cell = jnp.transpose(velocity, (1, 2, 0, 3))
     velocity = by_cell.reshape(2 * SIDE * SIDE, LANES)
-    *packed, outer = call(
-        opening_kernel,
-        [shape(OWNERS + EXTRA, SLOTS)] * 4 + [strip_shape],
+    packed = call(
+        pack_kernel,
+        [shape(OWNERS + EXTRA, SLOTS)] * 4,
         concentration,
         drag.reshape(1, 2),
+        specs=[ANY, SMEM],
+        scratch=[pltpu.VMEM((2, 4 * OWNERS, LANES), F32), sems((4,))],
+        params=ALONE_PARAMS,
+    )
+    parts = [packed[0]] + [
+        lax.ppermute(packed[step], "cat", [(i, i ^ step) for i in range(4)])
+        for step in (1, 2, 3)
+    ]
+
+    line = [pltpu.VMEM((2, 4, 48, LANES), F32)]
+    winds = call(
+        wind_kernel,
+        shape(4, OWNERS, SLOTS),
+        air_wind,
+        ocean_current,
+        scratch=[pltpu.VMEM((2, 2, 2, 4 * OWNERS, LANES), F32)],
+    )
+    summed = call(partial_kernel, shape(OWNERS, 2, SLOTS), *parts, winds, work=1 << 31)
+    arrived = lax.all_to_all(summed, "blocks", split_axis=0, concat_axis=0, tiled=True)
+
+    outer = call(
+        outer_strips_kernel,
+        strip_shape,
         by_cell,
         ice_cover,
-        specs=[ANY, SMEM, ANY, ANY],
+        specs=[ANY] * 2,
         scratch=[
-            pltpu.VMEM((2, 4 * OWNERS, LANES), F32),
             pltpu.VMEM((4, SIDE, 2, LANES), F32),
             pltpu.VMEM((2, SIDE, LANES), I32),
             pltpu.VMEM((SIDE, 8, LANES), I32),
             pltpu.VMEM((SIDE, 6, LANES), I32),
-            sems((10,)),
+            sems((8,)),
         ],
         params=ALONE_PARAMS,
     )
-    parts = [packed[0]] + [
-        lax.ppermute(packed[step], "cat", [(i, i ^ step) for i in range(4)])
-        for step in (1, 2, 3)
-    ]
-
-    line = [pltpu.VMEM((2, 4, 48, LANES), F32)]
-    summed = call(
-        partial_kernel,
-        shape(OWNERS, 2, SLOTS),
-        *parts, air_wind, ocean_current,
-        scratch=[pltpu.VMEM((2, 2, 2, 4 * OWNERS, LANES), F32)],
-        work=1 << 31,
-    )
-    arrived = lax.all_to_all(summed, "blocks", split_axis=0, concat_axis=0, tiled=True)
-
     first, second = both_ways(outer)
     inner, strength_strips, weight_strips = call(
         inner_strips_kernel,

time: 73.4 us -> 71 us (0.967)
  waiting for transfers between devices: 7.41 us -> 5.51 us
  Pallas kernels: 31.2 us -> 32.6 us
  starting transfers between devices: 32.6 us -> 31.5 us
  local copies, waits for them, and re-layouts: 0.93 us -> 0.06 us
    all_to_all x1, starting transfers between devices: 9.44 us -> 6.32 us  [shards(): lax.all_to_all(summed, 'blocks', split_axis=0, concat_axis=0, tiled=True)]
    ppermute x8, starting transfers between devices: 18.4 us -> 20.4 us  [both_ways(): return [lax.ppermute(strips, BOTH, swap) for swap in swaps]]
    pallas_call x9 -> x11, Pallas kernels: 10.3 us -> 11.7 us  [call(): pl.pallas_call(kernel, out_shape=outs, in_specs=specs or [VMEM] * len(arg...]
    all_to_all x1, waiting for transfers between devices: 5.38 us -> 4.42 us  [shards(): lax.all_to_all(summed, 'blocks', split_axis=0, concat_axis=0, tiled=True)]
    ppermute x8, waiting for transfers between devices: 2.03 us -> 1.08 us  [both_ways(): return [lax.ppermute(strips, BOTH, swap) for swap in swaps]]
    unnamed x24, local copies, waits for them, and re-layouts: 0.93 us -> 0.06 us
  transfers between devices with their start and end apart: 12 -> 12, of which waited for: 2 -> 2; matrix products, arithmetic and copies ran while one was open for 0% -> 0% of each run, Pallas kernels for 33% -> 37%
where the time goes in v4:
time: 71 us; the launch traced here: 70.8 us
  Pallas kernels  32.6 us (46%)
  starting transfers between devices  31.5 us (44%)
  waiting for transfers between devices  5.51 us (8%)
  between operations  1.1 us (2%)
    pallas_call x3, Pallas kernels, scatter_call(): pl.pallas_call(kernel, out_shape=outs, grid=(OWNERS // CHUNK,), in_specs=...  20.9 us
    ppermute x8, starting transfers between devices, both_ways(): return [lax.ppermute(strips, BOTH, swap) for swap in swaps]  20.4 us
    pallas_call x11, Pallas kernels, call(): pl.pallas_call(kernel, out_shape=outs, in_specs=specs or [VMEM] * len(arg...  11.7 us
    all_to_all x1, starting transfers between devices, shards(): lax.all_to_all(summed, 'blocks', split_axis=0, concat_axis=0, tiled=True)  6.32 us
    ppermute x3, starting transfers between devices, shards(): lax.ppermute(packed[step], 'cat', [(i, i ^ step) for i in range(4)])  4.78 us
    all_to_all x1, waiting for transfers between devices, shards(): lax.all_to_all(summed, 'blocks', split_axis=0, concat_axis=0, tiled=True)  4.42 us
  transfers between devices with their start and end apart: 12, of which 2 were waited for; matrix products, arithmetic and copies ran while one was open for 0% of the time, Pallas kernels for 37%

profile of v4, /device:TPU:0, one launch (start us, length us, event | category | flops | bytes accessed | tf_op | source)
XLA Modules:
  0.0 70.8 jit_solution(761873550070036451)
XLA Ops:
  0.6 0.0 copy-start.4
  0.6 0.0 copy-start.5
  0.7 2.5 %shard_map.132 = (f32[72,256]{1,0:T(8,128)}, f32[72,256]{1,0:T(8,128)}, f32[72,256]{1,0:T(8,128)}, f32[72,256]{1,0:T(8,128)}) custom-call(f32[1,1,256,256]{3,2,1,0:T(8,128)} %conc_hbm.1, f32[1,2]{1,0:T(1,128)} %bitcast.15), custom_call_target="tpu_custom_call" | custom-call | flops 4194304 | bytes 4194304 | tf_op jit(solution)/shard_map/pallas_call | solution.py:615
  3.2 0.0 copy-start.9
  3.2 0.1 collective-permute-start.2
  3.3 2.7 %collective-permute-start.3 = (f32[72,256]{1,0:T(8,128)}, f32[72,256]{1,0:T(8,128)S(1)}, u32[]{:S(2)}, u32[]{:S(2)}) collective-permute-start(f32[72,256]{1,0:T(8,128)} %get-tuple-element.22), channel_id=1, source_target_pairs={{0,2},{1,3},{2,0},{3,1},{4,6},{5,7},{6,4},{7,5},{8,10},{9,11},{10,... | collective-permute-start | bytes 221192 | tf_op jit(solution)/shard_map/ppermute | solution.py:666
  6.0 2.0 %collective-permute-start.4 = (f32[72,256]{1,0:T(8,128)}, f32[72,256]{1,0:T(8,128)S(1)}, u32[]{:S(2)}, u32[]{:S(2)}) collective-permute-start(f32[72,256]{1,0:T(8,128)} %get-tuple-element.23), channel_id=1, source_target_pairs={{0,3},{1,2},{2,1},{3,0},{4,7},{5,6},{6,5},{7,4},{8,11},{9,10},{10,... | collective-permute-start | bytes 221192 | tf_op jit(solution)/shard_map/ppermute | solution.py:666
  8.0 1.9 %shard_map.131.outer_ref = f32[2,4,32,128]{3,2,1,0:T(8,128)} custom-call(f32[30,30,2,128]{3,2,1,0:T(2,128)} %bitcast.8, s32[30,30,128]{2,1,0:T(8,128)} %cover_ref.7), custom_call_target="tpu_custom_call" | custom-call | flops 4194304 | bytes 4194304 | tf_op jit(solution)/shard_map/pallas_call | solution.py:615
  9.9 7.5 %collective-permute-start = (f32[2,4,32,128]{3,2,1,0:T(8,128)}, f32[2,4,32,128]{3,2,1,0:T(8,128)S(1)}, u32[]{:S(2)}, u32[]{:S(2)}) collective-permute-start(f32[2,4,32,128]{3,2,1,0:T(8,128)} %shard_map.131.outer_ref), channel_id=1, source_target_pairs={{1,2},{3,4},{5,6},{7,8},{9,10},{11,12},{13,14},{15,16},{17,18},{19... | collective-permute-start | bytes 393224 | tf_op jit(solution)/shard_map/ppermute | solution.py:645
  17.3 0.0 collective-permute-start.1
  17.3 0.0 copy-done.4
  17.3 0.0 copy-done.5
  17.3 0.1 shard_map.133.wind_ref
  17.5 0.0 collective-permute-done.2.first_ref
  17.5 0.0 collective-permute-done.3.second_ref
  17.5 0.0 collective-permute-done.4.third_ref
  17.5 0.0 copy-done.9
  17.5 0.0 copy-start
  17.5 0.0 copy-start.1
  17.5 0.0 copy-start.2
  17.5 0.0 copy-start.3
  17.6 0.7 %shard_map.134.summed_ref = f32[64,2,256]{2,1,0:T(2,128)} custom-call(f32[72,256]{1,0:T(8,128)S(1)} %copy-done.9, f32[72,256]{1,0:T(8,128)S(1)} %collective-permute-done.2.first_ref, f32[72,256]{1,0:T(8,128)S(1)} %collective-permute-done.3.second_ref, f32[72,256]{1,0:T(8,128)S(1)} %collective-permute-done.4.third_ref, f32[4,64,256]{2,1,0:T(8,128)S(1)} %shard_map.133.wind_ref), custom_call_target="tpu_custom_call" | custom-call | flops 2147483648 | bytes 4194304 | tf_op jit(solution)/shard_map/pallas_call | solution.py:615
  18.3 0.0 copy-start.6
  18.3 0.0 copy-start.7
  18.3 0.0 copy-start.8
  18.3 6.3 %all-to-all-start = ((f32[64,2,256]{2,1,0:T(2,128)}), f32[64,2,256]{2,1,0:T(2,128)S(1)}, u32[]{:S(2)}, u32[]{:S(2)}) async-start(f32[64,2,256]{2,1,0:T(2,128)} %shard_map.134.summed_ref), calls=%async_computation | async-start | bytes 262144 | tf_op jit(solution)/shard_map/all_to_all | solution.py:679
  24.6 0.0 copy-done
  24.6 0.0 copy-done.1
  24.7 0.0 copy-done.2
  24.7 0.0 copy-done.3
  24.7 0.2 shard_map.135
  24.9 0.0 collective-permute-done.one_ref
  24.9 0.0 collective-permute-done.1.two_ref
  24.9 0.0 copy-done.6
  24.9 0.0 copy-done.7
  24.9 0.0 copy-done.8
  24.9 0.0 copy-start.10
  24.9 0.0 copy-start.11
  25.0 0.6 shard_map.136
  25.5 5.0 %collective-permute-start.5 = (f32[2,4,32,128]{3,2,1,0:T(8,128)S(1)}, f32[2,4,32,128]{3,2,1,0:T(8,128)S(1)}, u32[]{:S(2)}, u32[]{:S(2)}) collective-permute-start(f32[2,4,32,128]{3,2,1,0:T(8,128)S(1)} %get-tuple-element.26.after_ref.own_ref.rest_0_), channel_id=1, source_target_pairs={{1,2},{3,4},{5,6},{7,8},{9,10},{11,12},{13,14},{15,16},{17,18},{19... | collective-permute-start | bytes 393224 | tf_op jit(solution)/shard_map/ppermute | solution.py:645
  30.5 0.0 collective-permute-start.6
  30.5 4.4 %all-to-all-done.value_ref = f32[64,2,256]{2,1,0:T(2,128)S(1)} async-done(((f32[64,2,256]{2,1,0:T(2,128)}), f32[64,2,256]{2,1,0:T(2,128)S(1)}, u32[]{:S(2)}, u32[]{:S(2)}) %all-to-all-start) | async-done | bytes 131104 | tf_op jit(solution)/shard_map/all_to_all | solution.py:679
  34.9 0.0 copy-done.10
  34.9 0.0 copy-done.11
  34.9 5.8 %shard_map.137.forcing_ref = f32[2,8,32,128]{3,2,1,0:T(8,128)S(1)} custom-call(s32[64,1,256]{2,1,0:T(1,128)S(1)} %copy-done.10, f32[64,2,256]{2,1,0:T(2,128)S(1)} %all-to-all-done.value_ref, s32[1,64]{1,0:T(1,128)S(1)} %bitcast.11, f32[2,4,32,128]{3,2,1,0:T(8,128)S(1)} %get-tuple-element.26.after_ref.own_ref.rest_0_), custom_call_target="tpu_custom_call" | custom-call | flops 4294967296 | bytes 1048576 | tf_op jit(solution)/shard_map/pallas_call | solution.py:175
  40.8 0.0 collective-permute-done.5.one_ref
  40.8 0.0 collective-permute-done.6.two_ref
  40.8 0.5 shard_map.138.stress_rims_ref
  41.3 1.2 %shard_map.139 = (f32[2,30,30,128]{3,2,1,0:T(8,128)S(1)}, f32[3,30,30,128]{3,2,1,0:T(8,128)S(1)}, f32[2,4,32,128]{3,2,1,0:T(8,128)S(1)}, f32[2,4,32,128]{3,2,1,0:T(8,128)S(1)}) custom-call(f32[2,4,32,128]{3,2,1,0:T(8,128)S(1)} %shard_map.138.stress_rims_ref, f32[2,4,32,128]{3,2,1,0:T(8,128)S(1)} %get-tuple-element.27.rims_ref, f32[1800,128]{1,0:T(8,128)S(1)} %bitcast.10, ...), custom_call_target="tpu_custom_call" | custom-call | flops 4194304 | bytes 4194304 | tf_op jit(solution)/shard_map/pallas_call | solution.py:615
  42.6 1.1 %collective-permute-start.7 = (f32[2,4,32,128]{3,2,1,0:T(8,128)S(1)}, f32[2,4,32,128]{3,2,1,0:T(8,128)S(1)}, u32[]{:S(2)}, u32[]{:S(2)}) collective-permute-start(f32[2,4,32,128]{3,2,1,0:T(8,128)S(1)} %get-tuple-element.29.outer_ref), channel_id=1, source_target_pairs={{1,2},{3,4},{5,6},{7,8},{9,10},{11,12},{13,14},{15,16},{17,18},{19... | collective-permute-start | bytes 393224 | tf_op jit(solution)/shard_map/ppermute | solution.py:645
  43.7 0.2 collective-permute-start.8
  43.9 7.5 %shard_map.141.low_ref = f32[2,352,128]{2,1,0:T(8,128)S(1)} custom-call(s32[64,1,256]{2,1,0:T(1,128)S(1)} %copy-done.10, f32[64,2,256]{2,1,0:T(2,128)S(1)} %all-to-all-done.value_ref, s32[1,64]{1,0:T(1,128)S(1)} %bitcast.12), custom_call_target="tpu_custom_call" | custom-call | flops 5905580032 | bytes 1048576 | tf_op jit(solution)/shard_map/pallas_call | solution.py:175
  51.4 1.1 %collective-permute-done.7.one_ref = f32[2,4,32,128]{3,2,1,0:T(8,128)S(1)} collective-permute-done((f32[2,4,32,128]{3,2,1,0:T(8,128)S(1)}, f32[2,4,32,128]{3,2,1,0:T(8,128)S(1)}, u32[]{:S(2)}, u32[]{:S(2)}) %collective-permute-start.7) | collective-permute-done | bytes 131104 | tf_op jit(solution)/shard_map/ppermute | solution.py:645
  52.5 0.0 collective-permute-done.8.two_ref
  52.5 0.6 shard_map.140
  53.0 1.1 %collective-permute-start.10 = (f32[2,4,32,128]{3,2,1,0:T(8,128)S(1)}, f32[2,4,32,128]{3,2,1,0:T(8,128)S(1)}, u32[]{:S(2)}, u32[]{:S(2)}) collective-permute-start(f32[2,4,32,128]{3,2,1,0:T(8,128)S(1)} %get-tuple-element.31.own_ref), channel_id=1, source_target_pairs={{0,1},{2,3},{4,5},{6,7},{8,9},{10,11},{12,13},{14,15},{16,17},{18,... | collective-permute-start | bytes 393224 | tf_op jit(solution)/shard_map/ppermute | solution.py:645
  54.1 5.6 %collective-permute-start.9 = (f32[2,4,32,128]{3,2,1,0:T(8,128)S(1)}, f32[2,4,32,128]{3,2,1,0:T(8,128)S(1)}, u32[]{:S(2)}, u32[]{:S(2)}) collective-permute-start(f32[2,4,32,128]{3,2,1,0:T(8,128)S(1)} %get-tuple-element.31.own_ref), channel_id=1, source_target_pairs={{1,2},{3,4},{5,6},{7,8},{9,10},{11,12},{13,14},{15,16},{17,18},{19... | collective-permute-start | bytes 393224 | tf_op jit(solution)/shard_map/ppermute | solution.py:645
  59.7 7.5 %shard_map.142.high_ref = f32[2,352,128]{2,1,0:T(8,128)S(1)} custom-call(s32[64,1,256]{2,1,0:T(1,128)S(1)} %copy-done.10, f32[64,2,256]{2,1,0:T(2,128)S(1)} %all-to-all-done.value_ref, s32[1,64]{1,0:T(1,128)S(1)} %bitcast.13), custom_call_target="tpu_custom_call" | custom-call | flops 5905580032 | bytes 1048576 | tf_op jit(solution)/shard_map/pallas_call | solution.py:175
  67.2 1.6 %shard_map.143 = (f32[2,30,30,128]{3,2,1,0:T(8,128)S(1)}, f32[3,30,30,128]{3,2,1,0:T(8,128)S(1)}, f32[3,30,30,128]{3,2,1,0:T(8,128)}) custom-call(f32[2,30,30,128]{3,2,1,0:T(8,128)S(1)} %get-tuple-element.32.base_ref, s32[30,30,128]{2,1,0:T(8,128)S(1)} %copy-done, f32[30,30,128]{2,1,0:T(8,128)S(1)} %copy-done.2, f32[2,352,128]{2,1,0:T(8,128)S(1)} %shard_map.141.low_ref, ...), custom_call_target="tpu_custom_call" | custom-call | flops 4194304 | bytes 4194304 | tf_op jit(solution)/shard_map/pallas_call | solution.py:615
  68.8 0.0 collective-permute-done.10.two_ref
  68.8 0.0 collective-permute-done.9.one_ref
  68.9 1.7 %shard_map.144 = f32[1800,128]{1,0:T(8,128)} custom-call(f32[2,4,32,128]{3,2,1,0:T(8,128)S(1)} %collective-permute-done.9.one_ref, f32[2,4,32,128]{3,2,1,0:T(8,128)S(1)} %get-tuple-element.31.own_ref, f32[2,4,32,128]{3,2,1,0:T(8,128)S(1)} %collective-permute-done.10.two_ref, s32[4,128]{1,0:T(4,128)S(1)} %copy-done.7, s32[4,128]{1,0:T(4,128)S(1)} %copy-done.8, ...), custom_call_target="tpu_custom_call" | custom-call | flops 4194304 | bytes 4194304 | tf_op jit(solution)/shard_map/pallas_call | solution.py:615
Async XLA Ops:
  0.6 16.7 %copy-start.4 = (f32[2,1,256,256]{3,2,1,0:T(8,128)S(1)}, f32[2,1,256,256]{3,2,1,0:T(8,128)}, u32[]{:S(2)}) copy-start(f32[2,1,256,256]{3,2,1,0:T(8,128)} %air_ref.1) | copy-start | bytes 1572868
  0.6 16.7 %copy-start.5 = (f32[2,1,256,256]{3,2,1,0:T(8,128)S(1)}, f32[2,1,256,256]{3,2,1,0:T(8,128)}, u32[]{:S(2)}) copy-start(f32[2,1,256,256]{3,2,1,0:T(8,128)} %ocean_ref.1) | copy-start | bytes 1572868
  3.2 14.3 %copy-start.9 = (f32[72,256]{1,0:T(8,128)S(1)}, f32[72,256]{1,0:T(8,128)}, u32[]{:S(2)}) copy-start(f32[72,256]{1,0:T(8,128)} %get-tuple-element.20.mine_ref) | copy-start | bytes 221188
  3.2 14.3 %collective-permute-start.2 = (f32[72,256]{1,0:T(8,128)}, f32[72,256]{1,0:T(8,128)S(1)}, u32[]{:S(2)}, u32[]{:S(2)}) collective-permute-start(f32[72,256]{1,0:T(8,128)} %get-tuple-element.21), channel_id=1, source_target_pairs={{0,1},{1,0},{2,3},{3,2},{4,5},{5,4},{6,7},{7,6},{8,9},{9,8},{10,11... | collective-permute-start | bytes 221192 | tf_op jit(solution)/shard_map/ppermute | solution.py:666
  3.3 14.2 %collective-permute-start.3 = (f32[72,256]{1,0:T(8,128)}, f32[72,256]{1,0:T(8,128)S(1)}, u32[]{:S(2)}, u32[]{:S(2)}) collective-permute-start(f32[72,256]{1,0:T(8,128)} %get-tuple-element.22), channel_id=1, source_target_pairs={{0,2},{1,3},{2,0},{3,1},{4,6},{5,7},{6,4},{7,5},{8,10},{9,11},{10,... | collective-permute-start | bytes 221192 | tf_op jit(solution)/shard_map/ppermute | solution.py:666
  6.0 11.5 %collective-permute-start.4 = (f32[72,256]{1,0:T(8,128)}, f32[72,256]{1,0:T(8,128)S(1)}, u32[]{:S(2)}, u32[]{:S(2)}) collective-permute-start(f32[72,256]{1,0:T(8,128)} %get-tuple-element.23), channel_id=1, source_target_pairs={{0,3},{1,2},{2,1},{3,0},{4,7},{5,6},{6,5},{7,4},{8,11},{9,10},{10,... | collective-permute-start | bytes 221192 | tf_op jit(solution)/shard_map/ppermute | solution.py:666
  9.9 15.0 %collective-permute-start = (f32[2,4,32,128]{3,2,1,0:T(8,128)}, f32[2,4,32,128]{3,2,1,0:T(8,128)S(1)}, u32[]{:S(2)}, u32[]{:S(2)}) collective-permute-start(f32[2,4,32,128]{3,2,1,0:T(8,128)} %shard_map.131.outer_ref), channel_id=1, source_target_pairs={{1,2},{3,4},{5,6},{7,8},{9,10},{11,12},{13,14},{15,16},{17,18},{19... | collective-permute-start | bytes 393224 | tf_op jit(solution)/shard_map/ppermute | solution.py:645
  17.3 7.6 %collective-permute-start.1 = (f32[2,4,32,128]{3,2,1,0:T(8,128)}, f32[2,4,32,128]{3,2,1,0:T(8,128)S(1)}, u32[]{:S(2)}, u32[]{:S(2)}) collective-permute-start(f32[2,4,32,128]{3,2,1,0:T(8,128)} %shard_map.131.outer_ref), channel_id=1, source_target_pairs={{0,1},{2,3},{4,5},{6,7},{8,9},{10,11},{12,13},{14,15},{16,17},{18,... | collective-permute-start | bytes 393224 | tf_op jit(solution)/shard_map/ppermute | solution.py:645
  17.5 7.1 %copy-start = (s32[30,30,128]{2,1,0:T(8,128)S(1)}, s32[30,30,128]{2,1,0:T(8,128)}, u32[]{:S(2)}) copy-start(s32[30,30,128]{2,1,0:T(8,128)} %cover_ref.7) | copy-start | bytes 1382404
  17.5 7.1 %copy-start.1 = (f32[2,30,30,128]{3,0,2,1:T(2,128)S(1)}, f32[2,30,30,128]{3,0,2,1:T(2,128)}, u32[]{:S(2)}) copy-start(f32[2,30,30,128]{3,0,2,1:T(2,128)} %param.12) | copy-start | bytes 2764804
  17.5 7.1 %copy-start.2 = (f32[30,30,128]{2,1,0:T(8,128)S(1)}, f32[30,30,128]{2,1,0:T(8,128)}, u32[]{:S(2)}) copy-start(f32[30,30,128]{2,1,0:T(8,128)} %mass_ref.7) | copy-start | bytes 1382404
  17.5 7.1 %copy-start.3 = (f32[30,30,128]{2,1,0:T(8,128)S(1)}, f32[30,30,128]{2,1,0:T(8,128)}, u32[]{:S(2)}) copy-start(f32[30,30,128]{2,1,0:T(8,128)} %strength_ref.5) | copy-start | bytes 1382404
  18.3 6.6 %copy-start.6 = (f32[2,4,32,128]{3,2,1,0:T(8,128)S(1)}, f32[2,4,32,128]{3,2,1,0:T(8,128)}, u32[]{:S(2)}) copy-start(f32[2,4,32,128]{3,2,1,0:T(8,128)} %shard_map.131.outer_ref) | copy-start | bytes 393220
  18.3 6.6 %copy-start.7 = (s32[4,128]{1,0:T(4,128)S(1)}, s32[4,128]{1,0:T(4,128)}, u32[]{:S(2)}) copy-start(s32[4,128]{1,0:T(4,128)} %neighbour_ref.7) | copy-start | bytes 6148
  18.3 6.6 %copy-start.8 = (s32[4,128]{1,0:T(4,128)S(1)}, s32[4,128]{1,0:T(4,128)}, u32[]{:S(2)}) copy-start(s32[4,128]{1,0:T(4,128)} %turn_ref.7) | copy-start | bytes 6148
  18.3 16.6 %all-to-all-start = ((f32[64,2,256]{2,1,0:T(2,128)}), f32[64,2,256]{2,1,0:T(2,128)S(1)}, u32[]{:S(2)}, u32[]{:S(2)}) async-start(f32[64,2,256]{2,1,0:T(2,128)} %shard_map.134.summed_ref), calls=%async_computation | async-start | bytes 262144 | tf_op jit(solution)/shard_map/all_to_all | solution.py:679
  24.9 10.0 %copy-start.10 = (s32[64,1,256]{2,1,0:T(1,128)S(1)}, s32[64,1,256]{2,1,0:T(1,128)}, u32[]{:S(2)}) copy-start(s32[64,1,256]{2,1,0:T(1,128)} %cell_ref.5) | copy-start | bytes 196612
  24.9 10.0 %copy-start.11 = (s32[64,1]{0,1:T(1,128)S(1)}, s32[64,1]{0,1:T(1,128)}, u32[]{:S(2)}) copy-start(s32[64,1]{0,1:T(1,128)} %param.23) | copy-start | bytes 772
  25.5 15.3 %collective-permute-start.5 = (f32[2,4,32,128]{3,2,1,0:T(8,128)S(1)}, f32[2,4,32,128]{3,2,1,0:T(8,128)S(1)}, u32[]{:S(2)}, u32[]{:S(2)}) collective-permute-start(f32[2,4,32,128]{3,2,1,0:T(8,128)S(1)} %get-tuple-element.26.after_ref.own_ref.rest_0_), channel_id=1, source_target_pairs={{1,2},{3,4},{5,6},{7,8},{9,10},{11,12},{13,14},{15,16},{17,18},{19... | collective-permute-start | bytes 393224 | tf_op jit(solution)/shard_map/ppermute | solution.py:645
  30.5 10.3 %collective-permute-start.6 = (f32[2,4,32,128]{3,2,1,0:T(8,128)S(1)}, f32[2,4,32,128]{3,2,1,0:T(8,128)S(1)}, u32[]{:S(2)}, u32[]{:S(2)}) collective-permute-start(f32[2,4,32,128]{3,2,1,0:T(8,128)S(1)} %get-tuple-element.26.after_ref.own_ref.rest_0_), channel_id=1, source_target_pairs={{0,1},{2,3},{4,5},{6,7},{8,9},{10,11},{12,13},{14,15},{16,17},{18,... | collective-permute-start | bytes 393224 | tf_op jit(solution)/shard_map/ppermute | solution.py:645
  42.6 9.9 %collective-permute-start.7 = (f32[2,4,32,128]{3,2,1,0:T(8,128)S(1)}, f32[2,4,32,128]{3,2,1,0:T(8,128)S(1)}, u32[]{:S(2)}, u32[]{:S(2)}) collective-permute-start(f32[2,4,32,128]{3,2,1,0:T(8,128)S(1)} %get-tuple-element.29.outer_ref), channel_id=1, source_target_pairs={{1,2},{3,4},{5,6},{7,8},{9,10},{11,12},{13,14},{15,16},{17,18},{19... | collective-permute-start | bytes 393224 | tf_op jit(solution)/shard_map/ppermute | solution.py:645
  43.7 8.8 %collective-permute-start.8 = (f32[2,4,32,128]{3,2,1,0:T(8,128)S(1)}, f32[2,4,32,128]{3,2,1,0:T(8,128)S(1)}, u32[]{:S(2)}, u32[]{:S(2)}) collective-permute-start(f32[2,4,32,128]{3,2,1,0:T(8,128)S(1)} %get-tuple-element.29.outer_ref), channel_id=1, source_target_pairs={{0,1},{2,3},{4,5},{6,7},{8,9},{10,11},{12,13},{14,15},{16,17},{18,... | collective-permute-start | bytes 393224 | tf_op jit(solution)/shard_map/ppermute | solution.py:645
  53.0 15.8 %collective-permute-start.10 = (f32[2,4,32,128]{3,2,1,0:T(8,128)S(1)}, f32[2,4,32,128]{3,2,1,0:T(8,128)S(1)}, u32[]{:S(2)}, u32[]{:S(2)}) collective-permute-start(f32[2,4,32,128]{3,2,1,0:T(8,128)S(1)} %get-tuple-element.31.own_ref), channel_id=1, source_target_pairs={{0,1},{2,3},{4,5},{6,7},{8,9},{10,11},{12,13},{14,15},{16,17},{18,... | collective-permute-start | bytes 393224 | tf_op jit(solution)/shard_map/ppermute | solution.py:645
  54.1 14.8 %collective-permute-start.9 = (f32[2,4,32,128]{3,2,1,0:T(8,128)S(1)}, f32[2,4,32,128]{3,2,1,0:T(8,128)S(1)}, u32[]{:S(2)}, u32[]{:S(2)}) collective-permute-start(f32[2,4,32,128]{3,2,1,0:T(8,128)S(1)} %get-tuple-element.31.own_ref), channel_id=1, source_target_pairs={{1,2},{3,4},{5,6},{7,8},{9,10},{11,12},{13,14},{15,16},{17,18},{19... | collective-permute-start | bytes 393224 | tf_op jit(solution)/shard_map/ppermute | solution.py:645

commit v5 on v4

--- a/solution.py
+++ b/solution.py
@@ -26,6 +26,7 @@
 PARAMS = pltpu.CompilerParams(vmem_limit_bytes=6 * 1024 * 1024)
 SCATTER_PARAMS = pltpu.CompilerParams(vmem_limit_bytes=12 * 1024 * 1024)
 ALONE_PARAMS = pltpu.CompilerParams(vmem_limit_bytes=60 * 1024 * 1024)
+WIND_PARAMS = pltpu.CompilerParams(vmem_limit_bytes=59600 * 1024)
 ANY = pl.BlockSpec(memory_space=pl.ANY)
 VMEM = pl.BlockSpec(memory_space=pltpu.VMEM)
 SMEM = pl.BlockSpec(memory_space=pltpu.SMEM)
@@ -44,11 +45,22 @@
     return halves[half, pl.ds(receiver, OWNERS, stride=4), :]
 
 
-def wind_kernel(air_ref, ocean_ref, out_ref, wind):
+def wind_kernel(air_hbm, ocean_hbm, out_ref, wind, sems):
     cat = lax.axis_index("cat")
-    for which, ref in enumerate((air_ref, ocean_ref)):
-        for member in range(2):
-            fill_halves(wind.at[which, member], lambda lanes: ref[member, 0, :, lanes])
+    copies = run_copies(
+        [
+            (
+                hbm.at[member, 0, :, half * LANES : half * LANES + LANES],
+                wind.at[which, member, half],
+            )
+            for which, hbm in enumerate((air_hbm, ocean_hbm))
+            for member in range(2)
+            for half in range(2)
+        ],
+        sems,
+    )
+    for copy in copies:
+        copy.wait()
     for half in range(2):
         lanes = slice(half * LANES, half * LANES + LANES)
         for which in range(2):
@@ -200,7 +212,7 @@
     here = lax.axis_index(BOTH)
     start = (here - 1) * LANES
     odd = lax.bitwise_and(here, 1)
-    holders = (2 * odd, 1, 2 - 2 * odd)
+    holders = (2 - 2 * odd, 1, 2 * odd)
     for side in range(4):
         place = lax.rem(
             neighbour_ref[side : side + 1, :] - start + devices * LANES, devices * LANES
@@ -267,31 +279,18 @@
     return copies
 
 
-def pack_kernel(conc_hbm, drag_ref, *rest):
-    outs, halves, sems = rest[:4], rest[4], rest[5]
-    cuts = [(half, start) for half in range(2) for start in (0, 2 * OWNERS)]
-    copies = run_copies(
-        [
-            (
-                conc_hbm.at[0, 0, pl.ds(start, 2 * OWNERS), half * LANES : half * LANES + LANES],
-                halves.at[half, pl.ds(start, 2 * OWNERS)],
-            )
-            for half, start in cuts
-        ],
-        sems,
-    )
+def pack_kernel(conc_ref, drag_ref, *rest):
+    outs, halves = rest[:4], rest[4]
     cat = lax.axis_index("cat")
     row = lax.broadcasted_iota(I32, (EXTRA, SLOTS), 0)
     coefficients = jnp.where(row == 0, drag_ref[0, 0], drag_ref[0, 1])
-    for packed_ref in outs:
-        packed_ref[OWNERS : OWNERS + EXTRA, :] = coefficients
-    for copy in copies:
-        copy.wait()
+    fill_halves(halves, lambda lanes: conc_ref[0, 0, :, lanes])
     for step, packed_ref in enumerate(outs):
         receiver = lax.bitwise_xor(cat, step)
         for half in range(2):
             lanes = slice(half * LANES, half * LANES + LANES)
             packed_ref[0:OWNERS, lanes] = quarter(halves, half, receiver)
+        packed_ref[OWNERS : OWNERS + EXTRA, :] = coefficients
 
 
 def outer_strips_kernel(
@@ -504,7 +503,12 @@
             faces_ref[member, side, 0:SIDE, :] = old + 0.5 * (target - old)
 
 
-def second_stress_kernel(
+def last_kernel(
+    one_ref,
+    own_ref,
+    two_ref,
+    neighbour_ref,
+    turn_ref,
     base_ref,
     cover_ref,
     mass_ref,
@@ -515,22 +519,24 @@
     rims_ref,
     strength_ref,
     old_ref,
-    moving_ref,
+    out_hbm,
+    stress_hbm,
+    line,
+    pad,
     stress_ref,
-    stress_hbm,
-    pad,
+    out_ref,
     sems,
 ):
     for member in range(2):
         for side in range(4):
-            store_rim(pad, member, side, rims_ref[member, side])
+            store_rim(line, member, side, rims_ref[member, side])
         for i, ref, side in (
             (0, outer_ref, 0),
             (1, inner_ref, 0),
             (SIDE - 2, inner_ref, 2),
             (SIDE - 1, outer_ref, 2),
         ):
-            pad[member, i + 1, 8 : 8 + SIDE, :] = ref[member, side, 0:SIDE, :]
+            line[member, i + 1, 8 : 8 + SIDE, :] = ref[member, side, 0:SIDE, :]
         for i in range(2, SIDE - 2):
             for j, ref, side in (
                 (0, outer_ref, 1),
@@ -538,23 +544,26 @@
                 (SIDE - 2, inner_ref, 3),
                 (SIDE - 1, outer_ref, 3),
             ):
-                pad[member, i + 1, 8 + j : 9 + j, :] = ref[member, side, i : i + 1, :]
+                line[member, i + 1, 8 + j : 9 + j, :] = ref[member, side, i : i + 1, :]
     inside = slice(2, SIDE - 2)
     for i in range(2, SIDE - 2):
         weight = weight_of(cover_ref[i, inside, :], mass_ref[i, inside, :])
         ref, at = (low_ref, i - 2) if i < 2 + HALF else (high_ref, i - 2 - HALF)
         for member in range(2):
-            pad[member, i + 1, 10 : 10 + INSIDE, :] = base_ref[member, i, inside, :] + weight * (
+            line[member, i + 1, 10 : 10 + INSIDE, :] = base_ref[member, i, inside, :] + weight * (
                 ref[member, at * INSIDE : at * INSIDE + INSIDE, :]
             )
     copies = []
     for i in range(SIDE):
-        targets = stress_targets(pad, strength_ref[i], i)
+        targets = stress_targets(line, strength_ref[i], i)
+        now = []
         for member in range(3):
             old = old_ref[member, i]
-            stress_ref[member, i] = old + 0.5 * (targets[member] - old)
-        for member in range(2):
-            moving_ref[member, i] = pad[member, i + 1, 8 : 8 + SIDE, :]
+            now.append(old + 0.5 * (targets[member] - old))
+            stress_ref[member, i] = now[member]
+        pad[0, i + 1, 8 : 8 + SIDE, :] = 0.5 * (now[0] + now[1])
+        pad[1, i + 1, 8 : 8 + SIDE, :] = now[2]
+        pad[2, i + 1, 8 : 8 + SIDE, :] = 0.5 * (now[0] - now[1])
         if i % 10 == 9:
             part = pl.ds(i - 9, 10)
             copies.append(
@@ -563,28 +572,6 @@
                 )
             )
             copies[-1].start()
-    for copy in copies:
-        copy.wait()
-
-
-def last_kernel(
-    one_ref,
-    own_ref,
-    two_ref,
-    neighbour_ref,
-    turn_ref,
-    moving_ref,
-    base_ref,
-    cover_ref,
-    mass_ref,
-    stress_ref,
-    out_hbm,
-    pad,
-    out_ref,
-    sems,
-):
-    copies = []
-    fill_stress(pad, stress_ref)
 
     def store(side, turns, rows):
         store_stress_rim(pad, side, *turned_stress(turns, rows))
@@ -592,7 +579,8 @@
     gather_rims((one_ref, own_ref, two_ref), neighbour_ref, turn_ref, store)
     for i in range(SIDE):
         force_east, force_north = forces(pad, i)
-        eastward, northward = moving_ref[0, i], moving_ref[1, i]
+        eastward = line[0, i + 1, 8 : 8 + SIDE, :]
+        northward = line[1, i + 1, 8 : 8 + SIDE, :]
         mass = mass_ref[i]
         weight = weight_of(cover_ref[i], mass)
         out_ref[cell_rows(i, 0), :] = weight * (
@@ -604,7 +592,7 @@
         if i % 6 == 5:
             part = pl.ds(60 * (i - 5), 360)
             copies.append(
-                pltpu.make_async_copy(out_ref.at[part], out_hbm.at[part], sems.at[i // 6])
+                pltpu.make_async_copy(out_ref.at[part], out_hbm.at[part], sems.at[3 + i // 6])
             )
             copies[-1].start()
     for copy in copies:
@@ -638,7 +626,7 @@
     slot_count,
 ):
     devices = lax.axis_size(BOTH)
-    pairs = [[(i, i + 1) for i in range(start, devices, 2)] for start in (1, 0)]
+    pairs = [[(i, i + 1) for i in range(start, devices, 2)] for start in (0, 1)]
     swaps = [[(i, j % devices) for i, j in p] + [(j % devices, i) for i, j in p] for p in pairs]
 
     def both_ways(strips):
@@ -658,9 +646,8 @@
         [shape(OWNERS + EXTRA, SLOTS)] * 4,
         concentration,
         drag.reshape(1, 2),
-        specs=[ANY, SMEM],
-        scratch=[pltpu.VMEM((2, 4 * OWNERS, LANES), F32), sems((4,))],
-        params=ALONE_PARAMS,
+        specs=[VMEM, SMEM],
+        scratch=[pltpu.VMEM((2, 4 * OWNERS, LANES), F32)],
     )
     parts = [packed[0]] + [
         lax.ppermute(packed[step], "cat", [(i, i ^ step) for i in range(4)])
@@ -673,7 +660,9 @@
         shape(4, OWNERS, SLOTS),
         air_wind,
         ocean_current,
-        scratch=[pltpu.VMEM((2, 2, 2, 4 * OWNERS, LANES), F32)],
+        specs=[ANY] * 2,
+        scratch=[pltpu.VMEM((2, 2, 2, 4 * OWNERS, LANES), F32), sems((8,))],
+        params=WIND_PARAMS,
     )
     summed = call(partial_kernel, shape(OWNERS, 2, SLOTS), *parts, winds, work=1 << 31)
     arrived = lax.all_to_all(summed, "blocks", split_axis=0, concat_axis=0, tiled=True)
@@ -740,19 +729,15 @@
         functools.partial(inside_kernel, 2 + HALF), HALF_ROWS, shape(2, HALF_ROWS, LANES),
         slot_cell, arrived, count,
     )
-    moving, kept, stress = call(
-        second_stress_kernel,
-        (shape(2, *block), shape(3, *block), shape(3, *block)),
-        base, ice_cover, mass, low, high, outer, inner, rims, strength, stress,
-        out_specs=(VMEM, VMEM, ANY),
-        scratch=pad2 + [sems((3,))],
-    )
-    moving = call(
+    moving, stress = call(
         last_kernel,
-        shape(2 * SIDE * SIDE, LANES),
-        first, faces, second, neighbour, rotation, moving, base, ice_cover, mass, kept,
-        out_specs=ANY,
-        scratch=pad3 + [pltpu.VMEM((2 * SIDE * SIDE, LANES), F32), sems((5,))],
+        (shape(2 * SIDE * SIDE, LANES), shape(3, *block)),
+        first, faces, second, neighbour, rotation, base, ice_cover, mass, low, high,
+        outer, inner, rims, strength, stress,
+        out_specs=(ANY, ANY),
+        scratch=pad2 + pad3
+        + [pltpu.VMEM((3, *block), F32), pltpu.VMEM((2 * SIDE * SIDE, LANES), F32), sems((8,))],
+        params=SCATTER_PARAMS,
     )
     moving = jnp.transpose(moving.reshape(SIDE, SIDE, 2, LANES), (2, 0, 1, 3))
     return (moving, stress)

time: 71 us -> 73.1 us (1.030)
  the two profiles are of different devices: /device:TPU:0 before, /device:TPU:8 now
where the time goes in v5:
time: 73.1 us; the launch traced here: 72.8 us
  starting transfers between devices  33.1 us (45%)
  Pallas kernels  32.1 us (44%)
  waiting for transfers between devices  4.02 us (5%)
  local copies, waits for them, and re-layouts  2.58 us (4%)
  between operations  1.06 us (1%)
    ppermute x8, starting transfers between devices, both_ways(): return [lax.ppermute(strips, BOTH, swap) for swap in swaps]  23.8 us
    pallas_call x3, Pallas kernels, scatter_call(): pl.pallas_call(kernel, out_shape=outs, grid=(OWNERS // CHUNK,), in_specs=...  20.9 us
    pallas_call x10, Pallas kernels, call(): pl.pallas_call(kernel, out_shape=outs, in_specs=specs or [VMEM] * len(arg...  11.2 us
    all_to_all x1, starting transfers between devices, shards(): lax.all_to_all(summed, 'blocks', split_axis=0, concat_axis=0, tiled=True)  5.42 us
    all_to_all x1, waiting for transfers between devices, shards(): lax.all_to_all(summed, 'blocks', split_axis=0, concat_axis=0, tiled=True)  4 us
    ppermute x3, starting transfers between devices, shards(): lax.ppermute(packed[step], 'cat', [(i, i ^ step) for i in range(4)])  3.83 us
    unnamed x24, local copies, waits for them, and re-layouts  2.58 us
  transfers between devices with their start and end apart: 12, of which 1 were waited for; matrix products, arithmetic and copies ran while one was open for 0% of the time, Pallas kernels for 36%

profile of v5, /device:TPU:8, one launch (start us, length us, event | category | flops | bytes accessed | tf_op | source)
XLA Modules:
  0.0 72.8 jit_solution(6382546870483335995)
XLA Ops:
  0.6 0.0 copy-start.5
  0.6 0.9 %copy-done.5 = f32[1,1,256,256]{3,2,1,0:T(8,128)S(1)} copy-done((f32[1,1,256,256]{3,2,1,0:T(8,128)S(1)}, f32[1,1,256,256]{3,2,1,0:T(8,128)}, u32[]{:S(2)}) %copy-start.5) | copy-done | bytes 262168
  1.6 0.0 copy-start.9
  1.6 0.7 copy-done.9
  2.2 0.6 shard_map.132
  2.8 2.3 %collective-permute-start.2 = (f32[72,256]{1,0:T(8,128)S(1)}, f32[72,256]{1,0:T(8,128)S(1)}, u32[]{:S(2)}, u32[]{:S(2)}) collective-permute-start(f32[72,256]{1,0:T(8,128)S(1)} %get-tuple-element.20), channel_id=1, source_target_pairs={{0,1},{1,0},{2,3},{3,2},{4,5},{5,4},{6,7},{7,6},{8,9},{9,8},{10,11... | collective-permute-start | bytes 221192 | tf_op jit(solution)/shard_map/ppermute | solution.py:653
  5.1 0.9 %collective-permute-start.3 = (f32[72,256]{1,0:T(8,128)S(1)}, f32[72,256]{1,0:T(8,128)S(1)}, u32[]{:S(2)}, u32[]{:S(2)}) collective-permute-start(f32[72,256]{1,0:T(8,128)S(1)} %get-tuple-element.21), channel_id=1, source_target_pairs={{0,2},{1,3},{2,0},{3,1},{4,6},{5,7},{6,4},{7,5},{8,10},{9,11},{10,... | collective-permute-start | bytes 221192 | tf_op jit(solution)/shard_map/ppermute | solution.py:653
  6.0 0.7 collective-permute-start.4
  6.7 1.9 %shard_map.131.outer_ref = f32[2,4,32,128]{3,2,1,0:T(8,128)} custom-call(f32[30,30,2,128]{3,2,1,0:T(2,128)} %bitcast.8, s32[30,30,128]{2,1,0:T(8,128)} %cover_ref.5), custom_call_target="tpu_custom_call" | custom-call | flops 4194304 | bytes 4194304 | tf_op jit(solution)/shard_map/pallas_call | solution.py:603
  8.6 1.4 %collective-permute-start.1 = (f32[2,4,32,128]{3,2,1,0:T(8,128)}, f32[2,4,32,128]{3,2,1,0:T(8,128)S(1)}, u32[]{:S(2)}, u32[]{:S(2)}) collective-permute-start(f32[2,4,32,128]{3,2,1,0:T(8,128)} %shard_map.131.outer_ref), channel_id=1, source_target_pairs={{1,2},{3,4},{5,6},{7,8},{9,10},{11,12},{13,14},{15,16},{17,18},{19... | collective-permute-start | bytes 393224 | tf_op jit(solution)/shard_map/ppermute | solution.py:633
  10.0 9.2 %collective-permute-start = (f32[2,4,32,128]{3,2,1,0:T(8,128)}, f32[2,4,32,128]{3,2,1,0:T(8,128)S(1)}, u32[]{:S(2)}, u32[]{:S(2)}) collective-permute-start(f32[2,4,32,128]{3,2,1,0:T(8,128)} %shard_map.131.outer_ref), channel_id=1, source_target_pairs={{0,1},{2,3},{4,5},{6,7},{8,9},{10,11},{12,13},{14,15},{16,17},{18,... | collective-permute-start | bytes 393224 | tf_op jit(solution)/shard_map/ppermute | solution.py:633
  19.2 2.1 %shard_map.133.wind_ref = f32[4,64,256]{2,1,0:T(8,128)} custom-call(f32[2,1,256,256]{3,2,1,0:T(8,128)} %air_hbm.1, f32[2,1,256,256]{3,2,1,0:T(8,128)} %ocean_hbm.1), custom_call_target="tpu_custom_call" | custom-call | flops 4194304 | bytes 4194304 | tf_op jit(solution)/shard_map/pallas_call | solution.py:603
  21.3 0.0 collective-permute-done.2.first_ref
  21.3 0.0 collective-permute-done.3.second_ref
  21.3 0.0 collective-permute-done.4.third_ref
  21.3 0.0 copy-start.4
  21.3 0.9 %copy-done.4 = f32[4,64,256]{2,1,0:T(8,128)S(1)} copy-done((f32[4,64,256]{2,1,0:T(8,128)S(1)}, f32[4,64,256]{2,1,0:T(8,128)}, u32[]{:S(2)}) %copy-start.4) | copy-done | bytes 262168
  22.3 0.0 copy-start
  22.3 0.0 copy-start.1
  22.3 0.0 copy-start.2
  22.3 0.0 copy-start.3
  22.3 0.7 %shard_map.134.summed_ref = f32[64,2,256]{2,1,0:T(2,128)} custom-call(f32[72,256]{1,0:T(8,128)S(1)} %get-tuple-element.19.mine_ref, f32[72,256]{1,0:T(8,128)S(1)} %collective-permute-done.2.first_ref, f32[72,256]{1,0:T(8,128)S(1)} %collective-permute-done.3.second_ref, f32[72,256]{1,0:T(8,128)S(1)} %collective-permute-done.4.third_ref, ...), custom_call_target="tpu_custom_call" | custom-call | flops 2147483648 | bytes 4194304 | tf_op jit(solution)/shard_map/pallas_call | solution.py:603
  23.0 0.0 copy-start.6
  23.0 0.0 copy-start.7
  23.0 0.0 copy-start.8
  23.0 5.4 %all-to-all-start = ((f32[64,2,256]{2,1,0:T(2,128)}), f32[64,2,256]{2,1,0:T(2,128)S(1)}, u32[]{:S(2)}, u32[]{:S(2)}) async-start(f32[64,2,256]{2,1,0:T(2,128)} %shard_map.134.summed_ref), calls=%async_computation | async-start | bytes 262144 | tf_op jit(solution)/shard_map/all_to_all | solution.py:668
  28.5 0.0 copy-done
  28.5 0.0 copy-done.1
  28.5 0.0 copy-done.2
  28.5 0.0 copy-done.3
  28.5 0.2 shard_map.135
  28.7 0.0 collective-permute-done.1.two_ref
  28.7 0.0 collective-permute-done.one_ref
  28.7 0.0 copy-done.6
  28.7 0.0 copy-done.7
  28.7 0.0 copy-done.8
  28.8 0.0 copy-start.10
  28.8 0.0 copy-start.11
  28.8 0.6 shard_map.136
  29.3 0.2 collective-permute-start.6
  29.5 5.3 %collective-permute-start.5 = (f32[2,4,32,128]{3,2,1,0:T(8,128)S(1)}, f32[2,4,32,128]{3,2,1,0:T(8,128)S(1)}, u32[]{:S(2)}, u32[]{:S(2)}) collective-permute-start(f32[2,4,32,128]{3,2,1,0:T(8,128)S(1)} %get-tuple-element.25.after_ref.own_ref.rest_0_), channel_id=1, source_target_pairs={{0,1},{2,3},{4,5},{6,7},{8,9},{10,11},{12,13},{14,15},{16,17},{18,... | collective-permute-start | bytes 393224 | tf_op jit(solution)/shard_map/ppermute | solution.py:633
  34.8 4.0 %all-to-all-done.value_ref = f32[64,2,256]{2,1,0:T(2,128)S(1)} async-done(((f32[64,2,256]{2,1,0:T(2,128)}), f32[64,2,256]{2,1,0:T(2,128)S(1)}, u32[]{:S(2)}, u32[]{:S(2)}) %all-to-all-start) | async-done | bytes 131104 | tf_op jit(solution)/shard_map/all_to_all | solution.py:668
  38.8 0.0 copy-done.10
  38.8 0.0 copy-done.11
  38.8 5.8 %shard_map.137.forcing_ref = f32[2,8,32,128]{3,2,1,0:T(8,128)S(1)} custom-call(s32[64,1,256]{2,1,0:T(1,128)S(1)} %copy-done.10, f32[64,2,256]{2,1,0:T(2,128)S(1)} %all-to-all-done.value_ref, s32[1,64]{1,0:T(1,128)S(1)} %bitcast.12, f32[2,4,32,128]{3,2,1,0:T(8,128)S(1)} %get-tuple-element.25.after_ref.own_ref.rest_0_), custom_call_target="tpu_custom_call" | custom-call | flops 4294967296 | bytes 1048576 | tf_op jit(solution)/shard_map/pallas_call | solution.py:187
  44.6 0.0 collective-permute-done.6.two_ref
  44.6 0.0 collective-permute-done.5.one_ref
  44.6 0.5 shard_map.138.stress_rims_ref
  45.1 1.3 %shard_map.139 = (f32[2,30,30,128]{3,2,1,0:T(8,128)S(1)}, f32[3,30,30,128]{3,2,1,0:T(8,128)S(1)}, f32[2,4,32,128]{3,2,1,0:T(8,128)S(1)}, f32[2,4,32,128]{3,2,1,0:T(8,128)S(1)}) custom-call(f32[2,4,32,128]{3,2,1,0:T(8,128)S(1)} %shard_map.138.stress_rims_ref, f32[2,4,32,128]{3,2,1,0:T(8,128)S(1)} %get-tuple-element.26.rims_ref, f32[1800,128]{1,0:T(8,128)S(1)} %bitcast.10, ...), custom_call_target="tpu_custom_call" | custom-call | flops 4194304 | bytes 4194304 | tf_op jit(solution)/shard_map/pallas_call | solution.py:603
  46.5 0.2 collective-permute-start.8
  46.6 1.4 %collective-permute-start.7 = (f32[2,4,32,128]{3,2,1,0:T(8,128)S(1)}, f32[2,4,32,128]{3,2,1,0:T(8,128)S(1)}, u32[]{:S(2)}, u32[]{:S(2)}) collective-permute-start(f32[2,4,32,128]{3,2,1,0:T(8,128)S(1)} %get-tuple-element.28.outer_ref), channel_id=1, source_target_pairs={{0,1},{2,3},{4,5},{6,7},{8,9},{10,11},{12,13},{14,15},{16,17},{18,... | collective-permute-start | bytes 393224 | tf_op jit(solution)/shard_map/ppermute | solution.py:633
  48.0 7.5 %shard_map.142.high_ref = f32[2,352,128]{2,1,0:T(8,128)S(1)} custom-call(s32[64,1,256]{2,1,0:T(1,128)S(1)} %copy-done.10, f32[64,2,256]{2,1,0:T(2,128)S(1)} %all-to-all-done.value_ref, s32[1,64]{1,0:T(1,128)S(1)} %bitcast.13), custom_call_target="tpu_custom_call" | custom-call | flops 5905580032 | bytes 1048576 | tf_op jit(solution)/shard_map/pallas_call | solution.py:187
  55.5 0.0 collective-permute-done.8.two_ref
  55.6 0.0 collective-permute-done.7.one_ref
  55.6 0.6 shard_map.140
  56.1 1.4 %collective-permute-start.10 = (f32[2,4,32,128]{3,2,1,0:T(8,128)S(1)}, f32[2,4,32,128]{3,2,1,0:T(8,128)S(1)}, u32[]{:S(2)}, u32[]{:S(2)}) collective-permute-start(f32[2,4,32,128]{3,2,1,0:T(8,128)S(1)} %get-tuple-element.30.own_ref), channel_id=1, source_target_pairs={{1,2},{3,4},{5,6},{7,8},{9,10},{11,12},{13,14},{15,16},{17,18},{19... | collective-permute-start | bytes 393224 | tf_op jit(solution)/shard_map/ppermute | solution.py:633
  57.6 4.8 %collective-permute-start.9 = (f32[2,4,32,128]{3,2,1,0:T(8,128)S(1)}, f32[2,4,32,128]{3,2,1,0:T(8,128)S(1)}, u32[]{:S(2)}, u32[]{:S(2)}) collective-permute-start(f32[2,4,32,128]{3,2,1,0:T(8,128)S(1)} %get-tuple-element.30.own_ref), channel_id=1, source_target_pairs={{0,1},{2,3},{4,5},{6,7},{8,9},{10,11},{12,13},{14,15},{16,17},{18,... | collective-permute-start | bytes 393224 | tf_op jit(solution)/shard_map/ppermute | solution.py:633
  62.4 7.5 %shard_map.141.low_ref = f32[2,352,128]{2,1,0:T(8,128)S(1)} custom-call(s32[64,1,256]{2,1,0:T(1,128)S(1)} %copy-done.10, f32[64,2,256]{2,1,0:T(2,128)S(1)} %all-to-all-done.value_ref, s32[1,64]{1,0:T(1,128)S(1)} %bitcast.14), custom_call_target="tpu_custom_call" | custom-call | flops 5905580032 | bytes 1048576 | tf_op jit(solution)/shard_map/pallas_call | solution.py:187
  69.9 0.0 collective-permute-done.10.two_ref
  69.9 0.0 collective-permute-done.9.one_ref
  69.9 2.7 %shard_map.143 = (f32[1800,128]{1,0:T(8,128)}, f32[3,30,30,128]{3,2,1,0:T(8,128)}) custom-call(f32[2,4,32,128]{3,2,1,0:T(8,128)S(1)} %collective-permute-done.9.one_ref, f32[2,4,32,128]{3,2,1,0:T(8,128)S(1)} %get-tuple-element.30.own_ref, f32[2,4,32,128]{3,2,1,0:T(8,128)S(1)} %collective-permute-done.10.two_ref, s32[4,128]{1,0:T(4,128)S(1)} %copy-done.7, ...), custom_call_target="tpu_custom_call" | custom-call | flops 4194304 | bytes 4194304 | tf_op jit(solution)/shard_map/pallas_call | solution.py:603
Async XLA Ops:
  0.6 1.0 %copy-start.5 = (f32[1,1,256,256]{3,2,1,0:T(8,128)S(1)}, f32[1,1,256,256]{3,2,1,0:T(8,128)}, u32[]{:S(2)}) copy-start(f32[1,1,256,256]{3,2,1,0:T(8,128)} %conc_ref.1) | copy-start | bytes 786436
  1.6 0.7 copy-start.9
  2.8 18.4 %collective-permute-start.2 = (f32[72,256]{1,0:T(8,128)S(1)}, f32[72,256]{1,0:T(8,128)S(1)}, u32[]{:S(2)}, u32[]{:S(2)}) collective-permute-start(f32[72,256]{1,0:T(8,128)S(1)} %get-tuple-element.20), channel_id=1, source_target_pairs={{0,1},{1,0},{2,3},{3,2},{4,5},{5,4},{6,7},{7,6},{8,9},{9,8},{10,11... | collective-permute-start | bytes 221192 | tf_op jit(solution)/shard_map/ppermute | solution.py:653
  5.1 16.2 %collective-permute-start.3 = (f32[72,256]{1,0:T(8,128)S(1)}, f32[72,256]{1,0:T(8,128)S(1)}, u32[]{:S(2)}, u32[]{:S(2)}) collective-permute-start(f32[72,256]{1,0:T(8,128)S(1)} %get-tuple-element.21), channel_id=1, source_target_pairs={{0,2},{1,3},{2,0},{3,1},{4,6},{5,7},{6,4},{7,5},{8,10},{9,11},{10,... | collective-permute-start | bytes 221192 | tf_op jit(solution)/shard_map/ppermute | solution.py:653
  6.0 15.3 %collective-permute-start.4 = (f32[72,256]{1,0:T(8,128)S(1)}, f32[72,256]{1,0:T(8,128)S(1)}, u32[]{:S(2)}, u32[]{:S(2)}) collective-permute-start(f32[72,256]{1,0:T(8,128)S(1)} %get-tuple-element.22), channel_id=1, source_target_pairs={{0,3},{1,2},{2,1},{3,0},{4,7},{5,6},{6,5},{7,4},{8,11},{9,10},{10,... | collective-permute-start | bytes 221192 | tf_op jit(solution)/shard_map/ppermute | solution.py:653
  8.6 20.1 %collective-permute-start.1 = (f32[2,4,32,128]{3,2,1,0:T(8,128)}, f32[2,4,32,128]{3,2,1,0:T(8,128)S(1)}, u32[]{:S(2)}, u32[]{:S(2)}) collective-permute-start(f32[2,4,32,128]{3,2,1,0:T(8,128)} %shard_map.131.outer_ref), channel_id=1, source_target_pairs={{1,2},{3,4},{5,6},{7,8},{9,10},{11,12},{13,14},{15,16},{17,18},{19... | collective-permute-start | bytes 393224 | tf_op jit(solution)/shard_map/ppermute | solution.py:633
  10.0 18.7 %collective-permute-start = (f32[2,4,32,128]{3,2,1,0:T(8,128)}, f32[2,4,32,128]{3,2,1,0:T(8,128)S(1)}, u32[]{:S(2)}, u32[]{:S(2)}) collective-permute-start(f32[2,4,32,128]{3,2,1,0:T(8,128)} %shard_map.131.outer_ref), channel_id=1, source_target_pairs={{0,1},{2,3},{4,5},{6,7},{8,9},{10,11},{12,13},{14,15},{16,17},{18,... | collective-permute-start | bytes 393224 | tf_op jit(solution)/shard_map/ppermute | solution.py:633
  21.3 1.0 %copy-start.4 = (f32[4,64,256]{2,1,0:T(8,128)S(1)}, f32[4,64,256]{2,1,0:T(8,128)}, u32[]{:S(2)}) copy-start(f32[4,64,256]{2,1,0:T(8,128)} %shard_map.133.wind_ref) | copy-start | bytes 786436
  22.3 6.2 %copy-start = (f32[2,30,30,128]{3,0,2,1:T(2,128)S(1)}, f32[2,30,30,128]{3,0,2,1:T(2,128)}, u32[]{:S(2)}) copy-start(f32[2,30,30,128]{3,0,2,1:T(2,128)} %param.12) | copy-start | bytes 2764804
  22.3 6.2 %copy-start.1 = (s32[30,30,128]{2,1,0:T(8,128)S(1)}, s32[30,30,128]{2,1,0:T(8,128)}, u32[]{:S(2)}) copy-start(s32[30,30,128]{2,1,0:T(8,128)} %cover_ref.5) | copy-start | bytes 1382404
  22.3 6.2 %copy-start.2 = (f32[30,30,128]{2,1,0:T(8,128)S(1)}, f32[30,30,128]{2,1,0:T(8,128)}, u32[]{:S(2)}) copy-start(f32[30,30,128]{2,1,0:T(8,128)} %strength_ref.5) | copy-start | bytes 1382404
  22.3 6.2 %copy-start.3 = (f32[30,30,128]{2,1,0:T(8,128)S(1)}, f32[30,30,128]{2,1,0:T(8,128)}, u32[]{:S(2)}) copy-start(f32[30,30,128]{2,1,0:T(8,128)} %mass_ref.5) | copy-start | bytes 1382404
  23.0 5.7 %copy-start.6 = (f32[2,4,32,128]{3,2,1,0:T(8,128)S(1)}, f32[2,4,32,128]{3,2,1,0:T(8,128)}, u32[]{:S(2)}) copy-start(f32[2,4,32,128]{3,2,1,0:T(8,128)} %shard_map.131.outer_ref) | copy-start | bytes 393220
  23.0 5.7 %copy-start.7 = (s32[4,128]{1,0:T(4,128)S(1)}, s32[4,128]{1,0:T(4,128)}, u32[]{:S(2)}) copy-start(s32[4,128]{1,0:T(4,128)} %neighbour_ref.7) | copy-start | bytes 6148
  23.0 5.7 %copy-start.8 = (s32[4,128]{1,0:T(4,128)S(1)}, s32[4,128]{1,0:T(4,128)}, u32[]{:S(2)}) copy-start(s32[4,128]{1,0:T(4,128)} %turn_ref.7) | copy-start | bytes 6148
  23.0 15.7 %all-to-all-start = ((f32[64,2,256]{2,1,0:T(2,128)}), f32[64,2,256]{2,1,0:T(2,128)S(1)}, u32[]{:S(2)}, u32[]{:S(2)}) async-start(f32[64,2,256]{2,1,0:T(2,128)} %shard_map.134.summed_ref), calls=%async_computation | async-start | bytes 262144 | tf_op jit(solution)/shard_map/all_to_all | solution.py:668
  28.8 10.0 %copy-start.10 = (s32[64,1,256]{2,1,0:T(1,128)S(1)}, s32[64,1,256]{2,1,0:T(1,128)}, u32[]{:S(2)}) copy-start(s32[64,1,256]{2,1,0:T(1,128)} %cell_ref.5) | copy-start | bytes 196612
  28.8 10.0 %copy-start.11 = (s32[64,1]{0,1:T(1,128)S(1)}, s32[64,1]{0,1:T(1,128)}, u32[]{:S(2)}) copy-start(s32[64,1]{0,1:T(1,128)} %param.23) | copy-start | bytes 772
  29.3 15.3 %collective-permute-start.6 = (f32[2,4,32,128]{3,2,1,0:T(8,128)S(1)}, f32[2,4,32,128]{3,2,1,0:T(8,128)S(1)}, u32[]{:S(2)}, u32[]{:S(2)}) collective-permute-start(f32[2,4,32,128]{3,2,1,0:T(8,128)S(1)} %get-tuple-element.25.after_ref.own_ref.rest_0_), channel_id=1, source_target_pairs={{1,2},{3,4},{5,6},{7,8},{9,10},{11,12},{13,14},{15,16},{17,18},{19... | collective-permute-start | bytes 393224 | tf_op jit(solution)/shard_map/ppermute | solution.py:633
  29.5 15.1 %collective-permute-start.5 = (f32[2,4,32,128]{3,2,1,0:T(8,128)S(1)}, f32[2,4,32,128]{3,2,1,0:T(8,128)S(1)}, u32[]{:S(2)}, u32[]{:S(2)}) collective-permute-start(f32[2,4,32,128]{3,2,1,0:T(8,128)S(1)} %get-tuple-element.25.after_ref.own_ref.rest_0_), channel_id=1, source_target_pairs={{0,1},{2,3},{4,5},{6,7},{8,9},{10,11},{12,13},{14,15},{16,17},{18,... | collective-permute-start | bytes 393224 | tf_op jit(solution)/shard_map/ppermute | solution.py:633
  46.5 9.1 %collective-permute-start.8 = (f32[2,4,32,128]{3,2,1,0:T(8,128)S(1)}, f32[2,4,32,128]{3,2,1,0:T(8,128)S(1)}, u32[]{:S(2)}, u32[]{:S(2)}) collective-permute-start(f32[2,4,32,128]{3,2,1,0:T(8,128)S(1)} %get-tuple-element.28.outer_ref), channel_id=1, source_target_pairs={{1,2},{3,4},{5,6},{7,8},{9,10},{11,12},{13,14},{15,16},{17,18},{19... | collective-permute-start | bytes 393224 | tf_op jit(solution)/shard_map/ppermute | solution.py:633
  46.6 8.9 %collective-permute-start.7 = (f32[2,4,32,128]{3,2,1,0:T(8,128)S(1)}, f32[2,4,32,128]{3,2,1,0:T(8,128)S(1)}, u32[]{:S(2)}, u32[]{:S(2)}) collective-permute-start(f32[2,4,32,128]{3,2,1,0:T(8,128)S(1)} %get-tuple-element.28.outer_ref), channel_id=1, source_target_pairs={{0,1},{2,3},{4,5},{6,7},{8,9},{10,11},{12,13},{14,15},{16,17},{18,... | collective-permute-start | bytes 393224 | tf_op jit(solution)/shard_map/ppermute | solution.py:633
  56.1 13.8 %collective-permute-start.10 = (f32[2,4,32,128]{3,2,1,0:T(8,128)S(1)}, f32[2,4,32,128]{3,2,1,0:T(8,128)S(1)}, u32[]{:S(2)}, u32[]{:S(2)}) collective-permute-start(f32[2,4,32,128]{3,2,1,0:T(8,128)S(1)} %get-tuple-element.30.own_ref), channel_id=1, source_target_pairs={{1,2},{3,4},{5,6},{7,8},{9,10},{11,12},{13,14},{15,16},{17,18},{19... | collective-permute-start | bytes 393224 | tf_op jit(solution)/shard_map/ppermute | solution.py:633
  57.6 12.4 %collective-permute-start.9 = (f32[2,4,32,128]{3,2,1,0:T(8,128)S(1)}, f32[2,4,32,128]{3,2,1,0:T(8,128)S(1)}, u32[]{:S(2)}, u32[]{:S(2)}) collective-permute-start(f32[2,4,32,128]{3,2,1,0:T(8,128)S(1)} %get-tuple-element.30.own_ref), channel_id=1, source_target_pairs={{0,1},{2,3},{4,5},{6,7},{8,9},{10,11},{12,13},{14,15},{16,17},{18,... | collective-permute-start | bytes 393224 | tf_op jit(solution)/shard_map/ppermute | solution.py:633

commit v6 on v5

--- a/solution.py
+++ b/solution.py
@@ -26,7 +26,7 @@
 PARAMS = pltpu.CompilerParams(vmem_limit_bytes=6 * 1024 * 1024)
 SCATTER_PARAMS = pltpu.CompilerParams(vmem_limit_bytes=12 * 1024 * 1024)
 ALONE_PARAMS = pltpu.CompilerParams(vmem_limit_bytes=60 * 1024 * 1024)
-WIND_PARAMS = pltpu.CompilerParams(vmem_limit_bytes=59600 * 1024)
+PACK_PARAMS = pltpu.CompilerParams(vmem_limit_bytes=65000 * 1024)
 ANY = pl.BlockSpec(memory_space=pl.ANY)
 VMEM = pl.BlockSpec(memory_space=pltpu.VMEM)
 SMEM = pl.BlockSpec(memory_space=pltpu.SMEM)
@@ -45,22 +45,11 @@
     return halves[half, pl.ds(receiver, OWNERS, stride=4), :]
 
 
-def wind_kernel(air_hbm, ocean_hbm, out_ref, wind, sems):
+def wind_kernel(air_ref, ocean_ref, out_ref, wind):
     cat = lax.axis_index("cat")
-    copies = run_copies(
-        [
-            (
-                hbm.at[member, 0, :, half * LANES : half * LANES + LANES],
-                wind.at[which, member, half],
-            )
-            for which, hbm in enumerate((air_hbm, ocean_hbm))
-            for member in range(2)
-            for half in range(2)
-        ],
-        sems,
-    )
-    for copy in copies:
-        copy.wait()
+    for which, ref in enumerate((air_ref, ocean_ref)):
+        for member in range(2):
+            fill_halves(wind.at[which, member], lambda lanes: ref[member, 0, :, lanes])
     for half in range(2):
         lanes = slice(half * LANES, half * LANES + LANES)
         for which in range(2):
@@ -279,18 +268,31 @@
     return copies
 
 
-def pack_kernel(conc_ref, drag_ref, *rest):
-    outs, halves = rest[:4], rest[4]
+def pack_kernel(conc_hbm, drag_ref, *rest):
+    outs, halves, sems = rest[:4], rest[4], rest[5]
+    cuts = [(half, start) for half in range(2) for start in (0, 2 * OWNERS)]
+    copies = run_copies(
+        [
+            (
+                conc_hbm.at[0, 0, pl.ds(start, 2 * OWNERS), half * LANES : half * LANES + LANES],
+                halves.at[half, pl.ds(start, 2 * OWNERS)],
+            )
+            for half, start in cuts
+        ],
+        sems,
+    )
     cat = lax.axis_index("cat")
     row = lax.broadcasted_iota(I32, (EXTRA, SLOTS), 0)
     coefficients = jnp.where(row == 0, drag_ref[0, 0], drag_ref[0, 1])
-    fill_halves(halves, lambda lanes: conc_ref[0, 0, :, lanes])
+    for packed_ref in outs:
+        packed_ref[OWNERS : OWNERS + EXTRA, :] = coefficients
+    for copy in copies:
+        copy.wait()
     for step, packed_ref in enumerate(outs):
         receiver = lax.bitwise_xor(cat, step)
         for half in range(2):
             lanes = slice(half * LANES, half * LANES + LANES)
             packed_ref[0:OWNERS, lanes] = quarter(halves, half, receiver)
-        packed_ref[OWNERS : OWNERS + EXTRA, :] = coefficients
 
 
 def outer_strips_kernel(
@@ -646,8 +648,9 @@
         [shape(OWNERS + EXTRA, SLOTS)] * 4,
         concentration,
         drag.reshape(1, 2),
-        specs=[VMEM, SMEM],
-        scratch=[pltpu.VMEM((2, 4 * OWNERS, LANES), F32)],
+        specs=[ANY, SMEM],
+        scratch=[pltpu.VMEM((2, 4 * OWNERS, LANES), F32), sems((4,))],
+        params=PACK_PARAMS,
     )
     parts = [packed[0]] + [
         lax.ppermute(packed[step], "cat", [(i, i ^ step) for i in range(4)])
@@ -660,9 +663,7 @@
         shape(4, OWNERS, SLOTS),
         air_wind,
         ocean_current,
-        specs=[ANY] * 2,
-        scratch=[pltpu.VMEM((2, 2, 2, 4 * OWNERS, LANES), F32), sems((8,))],
-        params=WIND_PARAMS,
+        scratch=[pltpu.VMEM((2, 2, 2, 4 * OWNERS, LANES), F32)],
     )
     summed = call(partial_kernel, shape(OWNERS, 2, SLOTS), *parts, winds, work=1 << 31)
     arrived = lax.all_to_all(summed, "blocks", split_axis=0, concat_axis=0, tiled=True)

time: 73.1 us -> 71 us (0.971)
  local copies, waits for them, and re-layouts: 2.58 us -> 0.07 us
  starting transfers between devices: 33.1 us -> 34.2 us
    unnamed x24, local copies, waits for them, and re-layouts: 2.58 us -> 0.07 us
    ppermute x8, starting transfers between devices: 23.8 us -> 24.9 us  [both_ways(): return [lax.ppermute(strips, BOTH, swap) for swap in swaps]]
  transfers between devices with their start and end apart: 12 -> 12, of which waited for: 1 -> 1; matrix products, arithmetic and copies ran while one was open for 0% -> 0% of each run, Pallas kernels for 36% -> 34%
where the time goes in v6:
time: 71 us; the launch traced here: 70.8 us
  starting transfers between devices  34.2 us (48%)
  Pallas kernels  31.9 us (45%)
  waiting for transfers between devices  3.55 us (5%)
  between operations  1.09 us (2%)
    ppermute x8, starting transfers between devices, both_ways(): return [lax.ppermute(strips, BOTH, swap) for swap in swaps]  24.9 us
    pallas_call x3, Pallas kernels, scatter_call(): pl.pallas_call(kernel, out_shape=outs, grid=(OWNERS // CHUNK,), in_specs=...  20.9 us
    pallas_call x10, Pallas kernels, call(): pl.pallas_call(kernel, out_shape=outs, in_specs=specs or [VMEM] * len(arg...  11 us
    all_to_all x1, starting transfers between devices, shards(): lax.all_to_all(summed, 'blocks', split_axis=0, concat_axis=0, tiled=True)  5.42 us
    ppermute x3, starting transfers between devices, shards(): lax.ppermute(packed[step], 'cat', [(i, i ^ step) for i in range(4)])  3.83 us
    all_to_all x1, waiting for transfers between devices, shards(): lax.all_to_all(summed, 'blocks', split_axis=0, concat_axis=0, tiled=True)  3.52 us
  transfers between devices with their start and end apart: 12, of which 1 were waited for; matrix products, arithmetic and copies ran while one was open for 0% of the time, Pallas kernels for 34%

profile of v6, /device:TPU:8, one launch (start us, length us, event | category | flops | bytes accessed | tf_op | source)
XLA Modules:
  0.0 70.8 jit_solution(1873512686303059606)
XLA Ops:
  0.6 2.4 %shard_map.132 = (f32[72,256]{1,0:T(8,128)}, f32[72,256]{1,0:T(8,128)}, f32[72,256]{1,0:T(8,128)}, f32[72,256]{1,0:T(8,128)}) custom-call(f32[1,1,256,256]{3,2,1,0:T(8,128)} %conc_hbm.1, f32[1,2]{1,0:T(1,128)} %bitcast.14), custom_call_target="tpu_custom_call" | custom-call | flops 4194304 | bytes 4194304 | tf_op jit(solution)/shard_map/pallas_call | solution.py:605
  3.0 0.0 copy-start.4
  3.0 0.0 copy-start.5
  3.0 0.0 copy-start.9
  3.0 2.3 %collective-permute-start.2 = (f32[72,256]{1,0:T(8,128)}, f32[72,256]{1,0:T(8,128)S(1)}, u32[]{:S(2)}, u32[]{:S(2)}) collective-permute-start(f32[72,256]{1,0:T(8,128)} %get-tuple-element.20), channel_id=1, source_target_pairs={{0,1},{1,0},{2,3},{3,2},{4,5},{5,4},{6,7},{7,6},{8,9},{9,8},{10,11... | collective-permute-start | bytes 221192 | tf_op jit(solution)/shard_map/ppermute | solution.py:656
  5.3 0.9 %collective-permute-start.3 = (f32[72,256]{1,0:T(8,128)}, f32[72,256]{1,0:T(8,128)S(1)}, u32[]{:S(2)}, u32[]{:S(2)}) collective-permute-start(f32[72,256]{1,0:T(8,128)} %get-tuple-element.21), channel_id=1, source_target_pairs={{0,2},{1,3},{2,0},{3,1},{4,6},{5,7},{6,4},{7,5},{8,10},{9,11},{10,... | collective-permute-start | bytes 221192 | tf_op jit(solution)/shard_map/ppermute | solution.py:656
  6.2 0.7 %collective-permute-start.4 = (f32[72,256]{1,0:T(8,128)}, f32[72,256]{1,0:T(8,128)S(1)}, u32[]{:S(2)}, u32[]{:S(2)}) collective-permute-start(f32[72,256]{1,0:T(8,128)} %get-tuple-element.22), channel_id=1, source_target_pairs={{0,3},{1,2},{2,1},{3,0},{4,7},{5,6},{6,5},{7,4},{8,11},{9,10},{10,... | collective-permute-start | bytes 221192 | tf_op jit(solution)/shard_map/ppermute | solution.py:656
  6.9 1.9 %shard_map.131.outer_ref = f32[2,4,32,128]{3,2,1,0:T(8,128)} custom-call(f32[30,30,2,128]{3,2,1,0:T(2,128)} %bitcast.8, s32[30,30,128]{2,1,0:T(8,128)} %cover_ref.5), custom_call_target="tpu_custom_call" | custom-call | flops 4194304 | bytes 4194304 | tf_op jit(solution)/shard_map/pallas_call | solution.py:605
  8.8 1.4 %collective-permute-start.1 = (f32[2,4,32,128]{3,2,1,0:T(8,128)}, f32[2,4,32,128]{3,2,1,0:T(8,128)S(1)}, u32[]{:S(2)}, u32[]{:S(2)}) collective-permute-start(f32[2,4,32,128]{3,2,1,0:T(8,128)} %shard_map.131.outer_ref), channel_id=1, source_target_pairs={{1,2},{3,4},{5,6},{7,8},{9,10},{11,12},{13,14},{15,16},{17,18},{19... | collective-permute-start | bytes 393224 | tf_op jit(solution)/shard_map/ppermute | solution.py:635
  10.2 9.2 %collective-permute-start = (f32[2,4,32,128]{3,2,1,0:T(8,128)}, f32[2,4,32,128]{3,2,1,0:T(8,128)S(1)}, u32[]{:S(2)}, u32[]{:S(2)}) collective-permute-start(f32[2,4,32,128]{3,2,1,0:T(8,128)} %shard_map.131.outer_ref), channel_id=1, source_target_pairs={{0,1},{2,3},{4,5},{6,7},{8,9},{10,11},{12,13},{14,15},{16,17},{18,... | collective-permute-start | bytes 393224 | tf_op jit(solution)/shard_map/ppermute | solution.py:635
  19.4 0.0 copy-done.4
  19.4 0.0 copy-done.5
  19.4 0.1 shard_map.133.wind_ref
  19.5 0.0 collective-permute-done.2.first_ref
  19.5 0.0 collective-permute-done.3.second_ref
  19.5 0.0 collective-permute-done.4.third_ref
  19.5 0.0 copy-done.9
  19.6 0.0 copy-start
  19.6 0.0 copy-start.1
  19.6 0.0 copy-start.2
  19.6 0.0 copy-start.3
  19.6 0.7 %shard_map.134.summed_ref = f32[64,2,256]{2,1,0:T(2,128)} custom-call(f32[72,256]{1,0:T(8,128)S(1)} %copy-done.9, f32[72,256]{1,0:T(8,128)S(1)} %collective-permute-done.2.first_ref, f32[72,256]{1,0:T(8,128)S(1)} %collective-permute-done.3.second_ref, f32[72,256]{1,0:T(8,128)S(1)} %collective-permute-done.4.third_ref, f32[4,64,256]{2,1,0:T(8,128)S(1)} %shard_map.133.wind_ref), custom_call_target="tpu_custom_call" | custom-call | flops 2147483648 | bytes 4194304 | tf_op jit(solution)/shard_map/pallas_call | solution.py:605
  20.3 0.0 copy-start.6
  20.4 0.0 copy-start.7
  20.4 0.0 copy-start.8
  20.4 5.4 %all-to-all-start = ((f32[64,2,256]{2,1,0:T(2,128)}), f32[64,2,256]{2,1,0:T(2,128)S(1)}, u32[]{:S(2)}, u32[]{:S(2)}) async-start(f32[64,2,256]{2,1,0:T(2,128)} %shard_map.134.summed_ref), calls=%async_computation | async-start | bytes 262144 | tf_op jit(solution)/shard_map/all_to_all | solution.py:669
  25.8 0.0 copy-done
  25.8 0.0 copy-done.1
  25.8 0.0 copy-done.2
  25.8 0.0 copy-done.3
  25.8 0.2 shard_map.135
  26.0 0.0 collective-permute-done.1.two_ref
  26.0 0.0 collective-permute-done.one_ref
  26.0 0.0 copy-done.6
  26.1 0.0 copy-done.7
  26.1 0.0 copy-done.8
  26.1 0.0 copy-start.10
  26.1 0.0 copy-start.11
  26.1 0.6 shard_map.136
  26.7 0.2 collective-permute-start.6
  26.8 5.7 %collective-permute-start.5 = (f32[2,4,32,128]{3,2,1,0:T(8,128)S(1)}, f32[2,4,32,128]{3,2,1,0:T(8,128)S(1)}, u32[]{:S(2)}, u32[]{:S(2)}) collective-permute-start(f32[2,4,32,128]{3,2,1,0:T(8,128)S(1)} %get-tuple-element.25.after_ref.own_ref.rest_0_), channel_id=1, source_target_pairs={{0,1},{2,3},{4,5},{6,7},{8,9},{10,11},{12,13},{14,15},{16,17},{18,... | collective-permute-start | bytes 393224 | tf_op jit(solution)/shard_map/ppermute | solution.py:635
  32.6 3.5 %all-to-all-done.value_ref = f32[64,2,256]{2,1,0:T(2,128)S(1)} async-done(((f32[64,2,256]{2,1,0:T(2,128)}), f32[64,2,256]{2,1,0:T(2,128)S(1)}, u32[]{:S(2)}, u32[]{:S(2)}) %all-to-all-start) | async-done | bytes 131104 | tf_op jit(solution)/shard_map/all_to_all | solution.py:669
  36.1 0.0 copy-done.10
  36.1 0.0 copy-done.11
  36.1 5.8 %shard_map.137.forcing_ref = f32[2,8,32,128]{3,2,1,0:T(8,128)S(1)} custom-call(s32[64,1,256]{2,1,0:T(1,128)S(1)} %copy-done.10, f32[64,2,256]{2,1,0:T(2,128)S(1)} %all-to-all-done.value_ref, s32[1,64]{1,0:T(1,128)S(1)} %bitcast.11, f32[2,4,32,128]{3,2,1,0:T(8,128)S(1)} %get-tuple-element.25.after_ref.own_ref.rest_0_), custom_call_target="tpu_custom_call" | custom-call | flops 4294967296 | bytes 1048576 | tf_op jit(solution)/shard_map/pallas_call | solution.py:176
  41.9 0.0 collective-permute-done.6.two_ref
  41.9 0.0 collective-permute-done.5.one_ref
  41.9 0.5 shard_map.138.stress_rims_ref
  42.5 1.3 %shard_map.139 = (f32[2,30,30,128]{3,2,1,0:T(8,128)S(1)}, f32[3,30,30,128]{3,2,1,0:T(8,128)S(1)}, f32[2,4,32,128]{3,2,1,0:T(8,128)S(1)}, f32[2,4,32,128]{3,2,1,0:T(8,128)S(1)}) custom-call(f32[2,4,32,128]{3,2,1,0:T(8,128)S(1)} %shard_map.138.stress_rims_ref, f32[2,4,32,128]{3,2,1,0:T(8,128)S(1)} %get-tuple-element.26.rims_ref, f32[1800,128]{1,0:T(8,128)S(1)} %bitcast.10, ...), custom_call_target="tpu_custom_call" | custom-call | flops 4194304 | bytes 4194304 | tf_op jit(solution)/shard_map/pallas_call | solution.py:605
  43.8 0.2 collective-permute-start.8
  44.0 1.8 %collective-permute-start.7 = (f32[2,4,32,128]{3,2,1,0:T(8,128)S(1)}, f32[2,4,32,128]{3,2,1,0:T(8,128)S(1)}, u32[]{:S(2)}, u32[]{:S(2)}) collective-permute-start(f32[2,4,32,128]{3,2,1,0:T(8,128)S(1)} %get-tuple-element.28.outer_ref), channel_id=1, source_target_pairs={{0,1},{2,3},{4,5},{6,7},{8,9},{10,11},{12,13},{14,15},{16,17},{18,... | collective-permute-start | bytes 393224 | tf_op jit(solution)/shard_map/ppermute | solution.py:635
  45.8 7.5 %shard_map.142.high_ref = f32[2,352,128]{2,1,0:T(8,128)S(1)} custom-call(s32[64,1,256]{2,1,0:T(1,128)S(1)} %copy-done.10, f32[64,2,256]{2,1,0:T(2,128)S(1)} %all-to-all-done.value_ref, s32[1,64]{1,0:T(1,128)S(1)} %bitcast.12), custom_call_target="tpu_custom_call" | custom-call | flops 5905580032 | bytes 1048576 | tf_op jit(solution)/shard_map/pallas_call | solution.py:176
  53.3 0.0 collective-permute-done.8.two_ref
  53.3 0.0 collective-permute-done.7.one_ref
  53.3 0.6 shard_map.140
  53.9 1.6 %collective-permute-start.10 = (f32[2,4,32,128]{3,2,1,0:T(8,128)S(1)}, f32[2,4,32,128]{3,2,1,0:T(8,128)S(1)}, u32[]{:S(2)}, u32[]{:S(2)}) collective-permute-start(f32[2,4,32,128]{3,2,1,0:T(8,128)S(1)} %get-tuple-element.30.own_ref), channel_id=1, source_target_pairs={{1,2},{3,4},{5,6},{7,8},{9,10},{11,12},{13,14},{15,16},{17,18},{19... | collective-permute-start | bytes 393224 | tf_op jit(solution)/shard_map/ppermute | solution.py:635
  55.5 4.8 %collective-permute-start.9 = (f32[2,4,32,128]{3,2,1,0:T(8,128)S(1)}, f32[2,4,32,128]{3,2,1,0:T(8,128)S(1)}, u32[]{:S(2)}, u32[]{:S(2)}) collective-permute-start(f32[2,4,32,128]{3,2,1,0:T(8,128)S(1)} %get-tuple-element.30.own_ref), channel_id=1, source_target_pairs={{0,1},{2,3},{4,5},{6,7},{8,9},{10,11},{12,13},{14,15},{16,17},{18,... | collective-permute-start | bytes 393224 | tf_op jit(solution)/shard_map/ppermute | solution.py:635
  60.3 7.5 %shard_map.141.low_ref = f32[2,352,128]{2,1,0:T(8,128)S(1)} custom-call(s32[64,1,256]{2,1,0:T(1,128)S(1)} %copy-done.10, f32[64,2,256]{2,1,0:T(2,128)S(1)} %all-to-all-done.value_ref, s32[1,64]{1,0:T(1,128)S(1)} %bitcast.13), custom_call_target="tpu_custom_call" | custom-call | flops 5905580032 | bytes 1048576 | tf_op jit(solution)/shard_map/pallas_call | solution.py:176
  67.9 0.0 collective-permute-done.10.two_ref
  67.9 0.0 collective-permute-done.9.one_ref
  67.9 2.7 %shard_map.143 = (f32[1800,128]{1,0:T(8,128)}, f32[3,30,30,128]{3,2,1,0:T(8,128)}) custom-call(f32[2,4,32,128]{3,2,1,0:T(8,128)S(1)} %collective-permute-done.9.one_ref, f32[2,4,32,128]{3,2,1,0:T(8,128)S(1)} %get-tuple-element.30.own_ref, f32[2,4,32,128]{3,2,1,0:T(8,128)S(1)} %collective-permute-done.10.two_ref, s32[4,128]{1,0:T(4,128)S(1)} %copy-done.7, ...), custom_call_target="tpu_custom_call" | custom-call | flops 4194304 | bytes 4194304 | tf_op jit(solution)/shard_map/pallas_call | solution.py:605
Async XLA Ops:
  3.0 16.4 %copy-start.4 = (f32[2,1,256,256]{3,2,1,0:T(8,128)S(1)}, f32[2,1,256,256]{3,2,1,0:T(8,128)}, u32[]{:S(2)}) copy-start(f32[2,1,256,256]{3,2,1,0:T(8,128)} %air_ref.1) | copy-start | bytes 1572868
  3.0 16.4 %copy-start.5 = (f32[2,1,256,256]{3,2,1,0:T(8,128)S(1)}, f32[2,1,256,256]{3,2,1,0:T(8,128)}, u32[]{:S(2)}) copy-start(f32[2,1,256,256]{3,2,1,0:T(8,128)} %ocean_ref.1) | copy-start | bytes 1572868
  3.0 16.5 %copy-start.9 = (f32[72,256]{1,0:T(8,128)S(1)}, f32[72,256]{1,0:T(8,128)}, u32[]{:S(2)}) copy-start(f32[72,256]{1,0:T(8,128)} %get-tuple-element.19.mine_ref) | copy-start | bytes 221188
  3.0 16.5 %collective-permute-start.2 = (f32[72,256]{1,0:T(8,128)}, f32[72,256]{1,0:T(8,128)S(1)}, u32[]{:S(2)}, u32[]{:S(2)}) collective-permute-start(f32[72,256]{1,0:T(8,128)} %get-tuple-element.20), channel_id=1, source_target_pairs={{0,1},{1,0},{2,3},{3,2},{4,5},{5,4},{6,7},{7,6},{8,9},{9,8},{10,11... | collective-permute-start | bytes 221192 | tf_op jit(solution)/shard_map/ppermute | solution.py:656
  5.3 14.2 %collective-permute-start.3 = (f32[72,256]{1,0:T(8,128)}, f32[72,256]{1,0:T(8,128)S(1)}, u32[]{:S(2)}, u32[]{:S(2)}) collective-permute-start(f32[72,256]{1,0:T(8,128)} %get-tuple-element.21), channel_id=1, source_target_pairs={{0,2},{1,3},{2,0},{3,1},{4,6},{5,7},{6,4},{7,5},{8,10},{9,11},{10,... | collective-permute-start | bytes 221192 | tf_op jit(solution)/shard_map/ppermute | solution.py:656
  6.2 13.4 %collective-permute-start.4 = (f32[72,256]{1,0:T(8,128)}, f32[72,256]{1,0:T(8,128)S(1)}, u32[]{:S(2)}, u32[]{:S(2)}) collective-permute-start(f32[72,256]{1,0:T(8,128)} %get-tuple-element.22), channel_id=1, source_target_pairs={{0,3},{1,2},{2,1},{3,0},{4,7},{5,6},{6,5},{7,4},{8,11},{9,10},{10,... | collective-permute-start | bytes 221192 | tf_op jit(solution)/shard_map/ppermute | solution.py:656
  8.8 17.2 %collective-permute-start.1 = (f32[2,4,32,128]{3,2,1,0:T(8,128)}, f32[2,4,32,128]{3,2,1,0:T(8,128)S(1)}, u32[]{:S(2)}, u32[]{:S(2)}) collective-permute-start(f32[2,4,32,128]{3,2,1,0:T(8,128)} %shard_map.131.outer_ref), channel_id=1, source_target_pairs={{1,2},{3,4},{5,6},{7,8},{9,10},{11,12},{13,14},{15,16},{17,18},{19... | collective-permute-start | bytes 393224 | tf_op jit(solution)/shard_map/ppermute | solution.py:635
  10.2 15.8 %collective-permute-start = (f32[2,4,32,128]{3,2,1,0:T(8,128)}, f32[2,4,32,128]{3,2,1,0:T(8,128)S(1)}, u32[]{:S(2)}, u32[]{:S(2)}) collective-permute-start(f32[2,4,32,128]{3,2,1,0:T(8,128)} %shard_map.131.outer_ref), channel_id=1, source_target_pairs={{0,1},{2,3},{4,5},{6,7},{8,9},{10,11},{12,13},{14,15},{16,17},{18,... | collective-permute-start | bytes 393224 | tf_op jit(solution)/shard_map/ppermute | solution.py:635
  19.6 6.2 %copy-start = (f32[2,30,30,128]{3,0,2,1:T(2,128)S(1)}, f32[2,30,30,128]{3,0,2,1:T(2,128)}, u32[]{:S(2)}) copy-start(f32[2,30,30,128]{3,0,2,1:T(2,128)} %param.12) | copy-start | bytes 2764804
  19.6 6.2 %copy-start.1 = (s32[30,30,128]{2,1,0:T(8,128)S(1)}, s32[30,30,128]{2,1,0:T(8,128)}, u32[]{:S(2)}) copy-start(s32[30,30,128]{2,1,0:T(8,128)} %cover_ref.5) | copy-start | bytes 1382404
  19.6 6.2 %copy-start.2 = (f32[30,30,128]{2,1,0:T(8,128)S(1)}, f32[30,30,128]{2,1,0:T(8,128)}, u32[]{:S(2)}) copy-start(f32[30,30,128]{2,1,0:T(8,128)} %strength_ref.5) | copy-start | bytes 1382404
  19.6 6.2 %copy-start.3 = (f32[30,30,128]{2,1,0:T(8,128)S(1)}, f32[30,30,128]{2,1,0:T(8,128)}, u32[]{:S(2)}) copy-start(f32[30,30,128]{2,1,0:T(8,128)} %mass_ref.5) | copy-start | bytes 1382404
  20.3 5.7 %copy-start.6 = (f32[2,4,32,128]{3,2,1,0:T(8,128)S(1)}, f32[2,4,32,128]{3,2,1,0:T(8,128)}, u32[]{:S(2)}) copy-start(f32[2,4,32,128]{3,2,1,0:T(8,128)} %shard_map.131.outer_ref) | copy-start | bytes 393220
  20.4 5.7 %copy-start.7 = (s32[4,128]{1,0:T(4,128)S(1)}, s32[4,128]{1,0:T(4,128)}, u32[]{:S(2)}) copy-start(s32[4,128]{1,0:T(4,128)} %neighbour_ref.7) | copy-start | bytes 6148
  20.4 5.7 %copy-start.8 = (s32[4,128]{1,0:T(4,128)S(1)}, s32[4,128]{1,0:T(4,128)}, u32[]{:S(2)}) copy-start(s32[4,128]{1,0:T(4,128)} %turn_ref.7) | copy-start | bytes 6148
  20.4 15.7 %all-to-all-start = ((f32[64,2,256]{2,1,0:T(2,128)}), f32[64,2,256]{2,1,0:T(2,128)S(1)}, u32[]{:S(2)}, u32[]{:S(2)}) async-start(f32[64,2,256]{2,1,0:T(2,128)} %shard_map.134.summed_ref), calls=%async_computation | async-start | bytes 262144 | tf_op jit(solution)/shard_map/all_to_all | solution.py:669
  26.1 10.0 %copy-start.10 = (s32[64,1,256]{2,1,0:T(1,128)S(1)}, s32[64,1,256]{2,1,0:T(1,128)}, u32[]{:S(2)}) copy-start(s32[64,1,256]{2,1,0:T(1,128)} %cell_ref.5) | copy-start | bytes 196612
  26.1 10.0 %copy-start.11 = (s32[64,1]{0,1:T(1,128)S(1)}, s32[64,1]{0,1:T(1,128)}, u32[]{:S(2)}) copy-start(s32[64,1]{0,1:T(1,128)} %param.23) | copy-start | bytes 772
  26.7 15.3 %collective-permute-start.6 = (f32[2,4,32,128]{3,2,1,0:T(8,128)S(1)}, f32[2,4,32,128]{3,2,1,0:T(8,128)S(1)}, u32[]{:S(2)}, u32[]{:S(2)}) collective-permute-start(f32[2,4,32,128]{3,2,1,0:T(8,128)S(1)} %get-tuple-element.25.after_ref.own_ref.rest_0_), channel_id=1, source_target_pairs={{1,2},{3,4},{5,6},{7,8},{9,10},{11,12},{13,14},{15,16},{17,18},{19... | collective-permute-start | bytes 393224 | tf_op jit(solution)/shard_map/ppermute | solution.py:635
  26.8 15.1 %collective-permute-start.5 = (f32[2,4,32,128]{3,2,1,0:T(8,128)S(1)}, f32[2,4,32,128]{3,2,1,0:T(8,128)S(1)}, u32[]{:S(2)}, u32[]{:S(2)}) collective-permute-start(f32[2,4,32,128]{3,2,1,0:T(8,128)S(1)} %get-tuple-element.25.after_ref.own_ref.rest_0_), channel_id=1, source_target_pairs={{0,1},{2,3},{4,5},{6,7},{8,9},{10,11},{12,13},{14,15},{16,17},{18,... | collective-permute-start | bytes 393224 | tf_op jit(solution)/shard_map/ppermute | solution.py:635
  43.8 9.5 %collective-permute-start.8 = (f32[2,4,32,128]{3,2,1,0:T(8,128)S(1)}, f32[2,4,32,128]{3,2,1,0:T(8,128)S(1)}, u32[]{:S(2)}, u32[]{:S(2)}) collective-permute-start(f32[2,4,32,128]{3,2,1,0:T(8,128)S(1)} %get-tuple-element.28.outer_ref), channel_id=1, source_target_pairs={{1,2},{3,4},{5,6},{7,8},{9,10},{11,12},{13,14},{15,16},{17,18},{19... | collective-permute-start | bytes 393224 | tf_op jit(solution)/shard_map/ppermute | solution.py:635
  44.0 9.4 %collective-permute-start.7 = (f32[2,4,32,128]{3,2,1,0:T(8,128)S(1)}, f32[2,4,32,128]{3,2,1,0:T(8,128)S(1)}, u32[]{:S(2)}, u32[]{:S(2)}) collective-permute-start(f32[2,4,32,128]{3,2,1,0:T(8,128)S(1)} %get-tuple-element.28.outer_ref), channel_id=1, source_target_pairs={{0,1},{2,3},{4,5},{6,7},{8,9},{10,11},{12,13},{14,15},{16,17},{18,... | collective-permute-start | bytes 393224 | tf_op jit(solution)/shard_map/ppermute | solution.py:635
  53.9 14.0 %collective-permute-start.10 = (f32[2,4,32,128]{3,2,1,0:T(8,128)S(1)}, f32[2,4,32,128]{3,2,1,0:T(8,128)S(1)}, u32[]{:S(2)}, u32[]{:S(2)}) collective-permute-start(f32[2,4,32,128]{3,2,1,0:T(8,128)S(1)} %get-tuple-element.30.own_ref), channel_id=1, source_target_pairs={{1,2},{3,4},{5,6},{7,8},{9,10},{11,12},{13,14},{15,16},{17,18},{19... | collective-permute-start | bytes 393224 | tf_op jit(solution)/shard_map/ppermute | solution.py:635
  55.5 12.4 %collective-permute-start.9 = (f32[2,4,32,128]{3,2,1,0:T(8,128)S(1)}, f32[2,4,32,128]{3,2,1,0:T(8,128)S(1)}, u32[]{:S(2)}, u32[]{:S(2)}) collective-permute-start(f32[2,4,32,128]{3,2,1,0:T(8,128)S(1)} %get-tuple-element.30.own_ref), channel_id=1, source_target_pairs={{0,1},{2,3},{4,5},{6,7},{8,9},{10,11},{12,13},{14,15},{16,17},{18,... | collective-permute-start | bytes 393224 | tf_op jit(solution)/shard_map/ppermute | solution.py:635

commit v7 on v6

--- a/solution.py
+++ b/solution.py
@@ -268,31 +268,25 @@
     return copies
 
 
-def pack_kernel(conc_hbm, drag_ref, *rest):
-    outs, halves, sems = rest[:4], rest[4], rest[5]
-    cuts = [(half, start) for half in range(2) for start in (0, 2 * OWNERS)]
+def pack_kernel(conc_hbm, drag_hbm, *rest):
+    outs = rest[:4]
+    whole, halves, drag, sems = rest[4:]
+    parts = [pl.ds(start, 2 * OWNERS) for start in (0, 2 * OWNERS)]
     copies = run_copies(
-        [
-            (
-                conc_hbm.at[0, 0, pl.ds(start, 2 * OWNERS), half * LANES : half * LANES + LANES],
-                halves.at[half, pl.ds(start, 2 * OWNERS)],
-            )
-            for half, start in cuts
-        ],
-        sems,
-    )
+        [(conc_hbm.at[0, 0, part], whole.at[part]) for part in parts] + [(drag_hbm, drag)], sems
+    )
+    for copy in copies:
+        copy.wait()
     cat = lax.axis_index("cat")
     row = lax.broadcasted_iota(I32, (EXTRA, SLOTS), 0)
-    coefficients = jnp.where(row == 0, drag_ref[0, 0], drag_ref[0, 1])
-    for packed_ref in outs:
-        packed_ref[OWNERS : OWNERS + EXTRA, :] = coefficients
-    for copy in copies:
-        copy.wait()
+    coefficients = jnp.where(row == 0, drag[0:1, 0:1], drag[0:1, 1:2])
+    fill_halves(halves, lambda lanes: whole[:, lanes])
     for step, packed_ref in enumerate(outs):
         receiver = lax.bitwise_xor(cat, step)
         for half in range(2):
             lanes = slice(half * LANES, half * LANES + LANES)
             packed_ref[0:OWNERS, lanes] = quarter(halves, half, receiver)
+        packed_ref[OWNERS : OWNERS + EXTRA, :] = coefficients
 
 
 def outer_strips_kernel(
@@ -648,8 +642,13 @@
         [shape(OWNERS + EXTRA, SLOTS)] * 4,
         concentration,
         drag.reshape(1, 2),
-        specs=[ANY, SMEM],
-        scratch=[pltpu.VMEM((2, 4 * OWNERS, LANES), F32), sems((4,))],
+        specs=[ANY, ANY],
+        scratch=[
+            pltpu.VMEM((4 * OWNERS, SLOTS), F32),
+            pltpu.VMEM((2, 4 * OWNERS, LANES), F32),
+            pltpu.VMEM((1, 2), F32),
+            sems((3,)),
+        ],
         params=PACK_PARAMS,
     )
     parts = [packed[0]] + [

time: 71 us -> 70.3 us (level)
  transfers between devices with their start and end apart: 12 -> 12, of which waited for: 1 -> 1; matrix products, arithmetic and copies ran while one was open for 0% -> 0% of each run, Pallas kernels for 34% -> 35%
where the time goes in v7:
time: 70.3 us; the launch traced here: 70.2 us
  starting transfers between devices  34.2 us (49%)
  Pallas kernels  31.3 us (45%)
  waiting for transfers between devices  3.55 us (5%)
  between operations  1.09 us (2%)
    ppermute x8, starting transfers between devices, both_ways(): return [lax.ppermute(strips, BOTH, swap) for swap in swaps]  24.9 us
    pallas_call x3, Pallas kernels, scatter_call(): pl.pallas_call(kernel, out_shape=outs, grid=(OWNERS // CHUNK,), in_specs=...  20.9 us
    pallas_call x10, Pallas kernels, call(): pl.pallas_call(kernel, out_shape=outs, in_specs=specs or [VMEM] * len(arg...  10.4 us
    all_to_all x1, starting transfers between devices, shards(): lax.all_to_all(summed, 'blocks', split_axis=0, concat_axis=0, tiled=True)  5.42 us
    ppermute x3, starting transfers between devices, shards(): lax.ppermute(packed[step], 'cat', [(i, i ^ step) for i in range(4)])  3.83 us
    all_to_all x1, waiting for transfers between devices, shards(): lax.all_to_all(summed, 'blocks', split_axis=0, concat_axis=0, tiled=True)  3.52 us
  transfers between devices with their start and end apart: 12, of which 1 were waited for; matrix products, arithmetic and copies ran while one was open for 0% of the time, Pallas kernels for 35%

profile of v7, /device:TPU:8, one launch (start us, length us, event | category | flops | bytes accessed | tf_op | source)
XLA Modules:
  0.0 70.2 jit_solution(11749381572504532273)
XLA Ops:
  0.6 1.8 %shard_map.132 = (f32[72,256]{1,0:T(8,128)}, f32[72,256]{1,0:T(8,128)}, f32[72,256]{1,0:T(8,128)}, f32[72,256]{1,0:T(8,128)}) custom-call(f32[1,1,256,256]{3,2,1,0:T(8,128)} %conc_hbm.1, f32[1,2]{1,0:T(1,128)} %bitcast.14), custom_call_target="tpu_custom_call" | custom-call | flops 4194304 | bytes 4194304 | tf_op jit(solution)/shard_map/pallas_call | solution.py:599
  2.4 0.0 copy-start.4
  2.4 0.0 copy-start.5
  2.4 0.0 copy-start.9
  2.5 2.3 %collective-permute-start.2 = (f32[72,256]{1,0:T(8,128)}, f32[72,256]{1,0:T(8,128)S(1)}, u32[]{:S(2)}, u32[]{:S(2)}) collective-permute-start(f32[72,256]{1,0:T(8,128)} %get-tuple-element.20), channel_id=1, source_target_pairs={{0,1},{1,0},{2,3},{3,2},{4,5},{5,4},{6,7},{7,6},{8,9},{9,8},{10,11... | collective-permute-start | bytes 221192 | tf_op jit(solution)/shard_map/ppermute | solution.py:655
  4.7 0.9 %collective-permute-start.3 = (f32[72,256]{1,0:T(8,128)}, f32[72,256]{1,0:T(8,128)S(1)}, u32[]{:S(2)}, u32[]{:S(2)}) collective-permute-start(f32[72,256]{1,0:T(8,128)} %get-tuple-element.21), channel_id=1, source_target_pairs={{0,2},{1,3},{2,0},{3,1},{4,6},{5,7},{6,4},{7,5},{8,10},{9,11},{10,... | collective-permute-start | bytes 221192 | tf_op jit(solution)/shard_map/ppermute | solution.py:655
  5.6 0.7 %collective-permute-start.4 = (f32[72,256]{1,0:T(8,128)}, f32[72,256]{1,0:T(8,128)S(1)}, u32[]{:S(2)}, u32[]{:S(2)}) collective-permute-start(f32[72,256]{1,0:T(8,128)} %get-tuple-element.22), channel_id=1, source_target_pairs={{0,3},{1,2},{2,1},{3,0},{4,7},{5,6},{6,5},{7,4},{8,11},{9,10},{10,... | collective-permute-start | bytes 221192 | tf_op jit(solution)/shard_map/ppermute | solution.py:655
  6.3 1.9 %shard_map.131.outer_ref = f32[2,4,32,128]{3,2,1,0:T(8,128)} custom-call(f32[30,30,2,128]{3,2,1,0:T(2,128)} %bitcast.8, s32[30,30,128]{2,1,0:T(8,128)} %cover_ref.5), custom_call_target="tpu_custom_call" | custom-call | flops 4194304 | bytes 4194304 | tf_op jit(solution)/shard_map/pallas_call | solution.py:599
  8.2 1.4 %collective-permute-start.1 = (f32[2,4,32,128]{3,2,1,0:T(8,128)}, f32[2,4,32,128]{3,2,1,0:T(8,128)S(1)}, u32[]{:S(2)}, u32[]{:S(2)}) collective-permute-start(f32[2,4,32,128]{3,2,1,0:T(8,128)} %shard_map.131.outer_ref), channel_id=1, source_target_pairs={{1,2},{3,4},{5,6},{7,8},{9,10},{11,12},{13,14},{15,16},{17,18},{19... | collective-permute-start | bytes 393224 | tf_op jit(solution)/shard_map/ppermute | solution.py:629
  9.6 9.2 %collective-permute-start = (f32[2,4,32,128]{3,2,1,0:T(8,128)}, f32[2,4,32,128]{3,2,1,0:T(8,128)S(1)}, u32[]{:S(2)}, u32[]{:S(2)}) collective-permute-start(f32[2,4,32,128]{3,2,1,0:T(8,128)} %shard_map.131.outer_ref), channel_id=1, source_target_pairs={{0,1},{2,3},{4,5},{6,7},{8,9},{10,11},{12,13},{14,15},{16,17},{18,... | collective-permute-start | bytes 393224 | tf_op jit(solution)/shard_map/ppermute | solution.py:629
  18.8 0.0 copy-done.4
  18.8 0.0 copy-done.5
  18.8 0.1 shard_map.133.wind_ref
  18.9 0.0 collective-permute-done.2.first_ref
  18.9 0.0 collective-permute-done.3.second_ref
  18.9 0.0 collective-permute-done.4.third_ref
  18.9 0.0 copy-done.9
  19.0 0.0 copy-start
  19.0 0.0 copy-start.1
  19.0 0.0 copy-start.2
  19.0 0.0 copy-start.3
  19.0 0.7 %shard_map.134.summed_ref = f32[64,2,256]{2,1,0:T(2,128)} custom-call(f32[72,256]{1,0:T(8,128)S(1)} %copy-done.9, f32[72,256]{1,0:T(8,128)S(1)} %collective-permute-done.2.first_ref, f32[72,256]{1,0:T(8,128)S(1)} %collective-permute-done.3.second_ref, f32[72,256]{1,0:T(8,128)S(1)} %collective-permute-done.4.third_ref, f32[4,64,256]{2,1,0:T(8,128)S(1)} %shard_map.133.wind_ref), custom_call_target="tpu_custom_call" | custom-call | flops 2147483648 | bytes 4194304 | tf_op jit(solution)/shard_map/pallas_call | solution.py:599
  19.7 0.0 copy-start.6
  19.8 0.0 copy-start.7
  19.8 0.0 copy-start.8
  19.8 5.4 %all-to-all-start = ((f32[64,2,256]{2,1,0:T(2,128)}), f32[64,2,256]{2,1,0:T(2,128)S(1)}, u32[]{:S(2)}, u32[]{:S(2)}) async-start(f32[64,2,256]{2,1,0:T(2,128)} %shard_map.134.summed_ref), calls=%async_computation | async-start | bytes 262144 | tf_op jit(solution)/shard_map/all_to_all | solution.py:668
  25.2 0.0 copy-done
  25.2 0.0 copy-done.1
  25.2 0.0 copy-done.2
  25.2 0.0 copy-done.3
  25.2 0.2 shard_map.135
  25.4 0.0 collective-permute-done.1.two_ref
  25.4 0.0 collective-permute-done.one_ref
  25.5 0.0 copy-done.6
  25.5 0.0 copy-done.7
  25.5 0.0 copy-done.8
  25.5 0.0 copy-start.10
  25.5 0.0 copy-start.11
  25.5 0.6 shard_map.136
  26.1 0.2 collective-permute-start.6
  26.2 5.7 %collective-permute-start.5 = (f32[2,4,32,128]{3,2,1,0:T(8,128)S(1)}, f32[2,4,32,128]{3,2,1,0:T(8,128)S(1)}, u32[]{:S(2)}, u32[]{:S(2)}) collective-permute-start(f32[2,4,32,128]{3,2,1,0:T(8,128)S(1)} %get-tuple-element.25.after_ref.own_ref.rest_0_), channel_id=1, source_target_pairs={{0,1},{2,3},{4,5},{6,7},{8,9},{10,11},{12,13},{14,15},{16,17},{18,... | collective-permute-start | bytes 393224 | tf_op jit(solution)/shard_map/ppermute | solution.py:629
  32.0 3.5 %all-to-all-done.value_ref = f32[64,2,256]{2,1,0:T(2,128)S(1)} async-done(((f32[64,2,256]{2,1,0:T(2,128)}), f32[64,2,256]{2,1,0:T(2,128)S(1)}, u32[]{:S(2)}, u32[]{:S(2)}) %all-to-all-start) | async-done | bytes 131104 | tf_op jit(solution)/shard_map/all_to_all | solution.py:668
  35.5 0.0 copy-done.10
  35.5 0.0 copy-done.11
  35.5 5.8 %shard_map.137.forcing_ref = f32[2,8,32,128]{3,2,1,0:T(8,128)S(1)} custom-call(s32[64,1,256]{2,1,0:T(1,128)S(1)} %copy-done.10, f32[64,2,256]{2,1,0:T(2,128)S(1)} %all-to-all-done.value_ref, s32[1,64]{1,0:T(1,128)S(1)} %bitcast.11, f32[2,4,32,128]{3,2,1,0:T(8,128)S(1)} %get-tuple-element.25.after_ref.own_ref.rest_0_), custom_call_target="tpu_custom_call" | custom-call | flops 4294967296 | bytes 1048576 | tf_op jit(solution)/shard_map/pallas_call | solution.py:176
  41.3 0.0 collective-permute-done.6.two_ref
  41.3 0.0 collective-permute-done.5.one_ref
  41.4 0.5 shard_map.138.stress_rims_ref
  41.9 1.3 %shard_map.139 = (f32[2,30,30,128]{3,2,1,0:T(8,128)S(1)}, f32[3,30,30,128]{3,2,1,0:T(8,128)S(1)}, f32[2,4,32,128]{3,2,1,0:T(8,128)S(1)}, f32[2,4,32,128]{3,2,1,0:T(8,128)S(1)}) custom-call(f32[2,4,32,128]{3,2,1,0:T(8,128)S(1)} %shard_map.138.stress_rims_ref, f32[2,4,32,128]{3,2,1,0:T(8,128)S(1)} %get-tuple-element.26.rims_ref, f32[1800,128]{1,0:T(8,128)S(1)} %bitcast.10, ...), custom_call_target="tpu_custom_call" | custom-call | flops 4194304 | bytes 4194304 | tf_op jit(solution)/shard_map/pallas_call | solution.py:599
  43.2 0.2 collective-permute-start.8
  43.4 1.8 %collective-permute-start.7 = (f32[2,4,32,128]{3,2,1,0:T(8,128)S(1)}, f32[2,4,32,128]{3,2,1,0:T(8,128)S(1)}, u32[]{:S(2)}, u32[]{:S(2)}) collective-permute-start(f32[2,4,32,128]{3,2,1,0:T(8,128)S(1)} %get-tuple-element.28.outer_ref), channel_id=1, source_target_pairs={{0,1},{2,3},{4,5},{6,7},{8,9},{10,11},{12,13},{14,15},{16,17},{18,... | collective-permute-start | bytes 393224 | tf_op jit(solution)/shard_map/ppermute | solution.py:629
  45.2 7.5 %shard_map.142.high_ref = f32[2,352,128]{2,1,0:T(8,128)S(1)} custom-call(s32[64,1,256]{2,1,0:T(1,128)S(1)} %copy-done.10, f32[64,2,256]{2,1,0:T(2,128)S(1)} %all-to-all-done.value_ref, s32[1,64]{1,0:T(1,128)S(1)} %bitcast.12), custom_call_target="tpu_custom_call" | custom-call | flops 5905580032 | bytes 1048576 | tf_op jit(solution)/shard_map/pallas_call | solution.py:176
  52.7 0.0 collective-permute-done.8.two_ref
  52.7 0.0 collective-permute-done.7.one_ref
  52.7 0.6 shard_map.140
  53.3 1.6 %collective-permute-start.10 = (f32[2,4,32,128]{3,2,1,0:T(8,128)S(1)}, f32[2,4,32,128]{3,2,1,0:T(8,128)S(1)}, u32[]{:S(2)}, u32[]{:S(2)}) collective-permute-start(f32[2,4,32,128]{3,2,1,0:T(8,128)S(1)} %get-tuple-element.30.own_ref), channel_id=1, source_target_pairs={{1,2},{3,4},{5,6},{7,8},{9,10},{11,12},{13,14},{15,16},{17,18},{19... | collective-permute-start | bytes 393224 | tf_op jit(solution)/shard_map/ppermute | solution.py:629
  54.9 4.8 %collective-permute-start.9 = (f32[2,4,32,128]{3,2,1,0:T(8,128)S(1)}, f32[2,4,32,128]{3,2,1,0:T(8,128)S(1)}, u32[]{:S(2)}, u32[]{:S(2)}) collective-permute-start(f32[2,4,32,128]{3,2,1,0:T(8,128)S(1)} %get-tuple-element.30.own_ref), channel_id=1, source_target_pairs={{0,1},{2,3},{4,5},{6,7},{8,9},{10,11},{12,13},{14,15},{16,17},{18,... | collective-permute-start | bytes 393224 | tf_op jit(solution)/shard_map/ppermute | solution.py:629
  59.7 7.5 %shard_map.141.low_ref = f32[2,352,128]{2,1,0:T(8,128)S(1)} custom-call(s32[64,1,256]{2,1,0:T(1,128)S(1)} %copy-done.10, f32[64,2,256]{2,1,0:T(2,128)S(1)} %all-to-all-done.value_ref, s32[1,64]{1,0:T(1,128)S(1)} %bitcast.13), custom_call_target="tpu_custom_call" | custom-call | flops 5905580032 | bytes 1048576 | tf_op jit(solution)/shard_map/pallas_call | solution.py:176
  67.3 0.0 collective-permute-done.10.two_ref
  67.3 0.0 collective-permute-done.9.one_ref
  67.3 2.7 %shard_map.143 = (f32[1800,128]{1,0:T(8,128)}, f32[3,30,30,128]{3,2,1,0:T(8,128)}) custom-call(f32[2,4,32,128]{3,2,1,0:T(8,128)S(1)} %collective-permute-done.9.one_ref, f32[2,4,32,128]{3,2,1,0:T(8,128)S(1)} %get-tuple-element.30.own_ref, f32[2,4,32,128]{3,2,1,0:T(8,128)S(1)} %collective-permute-done.10.two_ref, s32[4,128]{1,0:T(4,128)S(1)} %copy-done.7, ...), custom_call_target="tpu_custom_call" | custom-call | flops 4194304 | bytes 4194304 | tf_op jit(solution)/shard_map/pallas_call | solution.py:599
Async XLA Ops:
  2.4 16.4 %copy-start.4 = (f32[2,1,256,256]{3,2,1,0:T(8,128)S(1)}, f32[2,1,256,256]{3,2,1,0:T(8,128)}, u32[]{:S(2)}) copy-start(f32[2,1,256,256]{3,2,1,0:T(8,128)} %air_ref.1) | copy-start | bytes 1572868
  2.4 16.4 %copy-start.5 = (f32[2,1,256,256]{3,2,1,0:T(8,128)S(1)}, f32[2,1,256,256]{3,2,1,0:T(8,128)}, u32[]{:S(2)}) copy-start(f32[2,1,256,256]{3,2,1,0:T(8,128)} %ocean_ref.1) | copy-start | bytes 1572868
  2.4 16.5 %copy-start.9 = (f32[72,256]{1,0:T(8,128)S(1)}, f32[72,256]{1,0:T(8,128)}, u32[]{:S(2)}) copy-start(f32[72,256]{1,0:T(8,128)} %get-tuple-element.19.mine_ref) | copy-start | bytes 221188
  2.5 16.5 %collective-permute-start.2 = (f32[72,256]{1,0:T(8,128)}, f32[72,256]{1,0:T(8,128)S(1)}, u32[]{:S(2)}, u32[]{:S(2)}) collective-permute-start(f32[72,256]{1,0:T(8,128)} %get-tuple-element.20), channel_id=1, source_target_pairs={{0,1},{1,0},{2,3},{3,2},{4,5},{5,4},{6,7},{7,6},{8,9},{9,8},{10,11... | collective-permute-start | bytes 221192 | tf_op jit(solution)/shard_map/ppermute | solution.py:655
  4.7 14.2 %collective-permute-start.3 = (f32[72,256]{1,0:T(8,128)}, f32[72,256]{1,0:T(8,128)S(1)}, u32[]{:S(2)}, u32[]{:S(2)}) collective-permute-start(f32[72,256]{1,0:T(8,128)} %get-tuple-element.21), channel_id=1, source_target_pairs={{0,2},{1,3},{2,0},{3,1},{4,6},{5,7},{6,4},{7,5},{8,10},{9,11},{10,... | collective-permute-start | bytes 221192 | tf_op jit(solution)/shard_map/ppermute | solution.py:655
  5.6 13.4 %collective-permute-start.4 = (f32[72,256]{1,0:T(8,128)}, f32[72,256]{1,0:T(8,128)S(1)}, u32[]{:S(2)}, u32[]{:S(2)}) collective-permute-start(f32[72,256]{1,0:T(8,128)} %get-tuple-element.22), channel_id=1, source_target_pairs={{0,3},{1,2},{2,1},{3,0},{4,7},{5,6},{6,5},{7,4},{8,11},{9,10},{10,... | collective-permute-start | bytes 221192 | tf_op jit(solution)/shard_map/ppermute | solution.py:655
  8.2 17.2 %collective-permute-start.1 = (f32[2,4,32,128]{3,2,1,0:T(8,128)}, f32[2,4,32,128]{3,2,1,0:T(8,128)S(1)}, u32[]{:S(2)}, u32[]{:S(2)}) collective-permute-start(f32[2,4,32,128]{3,2,1,0:T(8,128)} %shard_map.131.outer_ref), channel_id=1, source_target_pairs={{1,2},{3,4},{5,6},{7,8},{9,10},{11,12},{13,14},{15,16},{17,18},{19... | collective-permute-start | bytes 393224 | tf_op jit(solution)/shard_map/ppermute | solution.py:629
  9.6 15.8 %collective-permute-start = (f32[2,4,32,128]{3,2,1,0:T(8,128)}, f32[2,4,32,128]{3,2,1,0:T(8,128)S(1)}, u32[]{:S(2)}, u32[]{:S(2)}) collective-permute-start(f32[2,4,32,128]{3,2,1,0:T(8,128)} %shard_map.131.outer_ref), channel_id=1, source_target_pairs={{0,1},{2,3},{4,5},{6,7},{8,9},{10,11},{12,13},{14,15},{16,17},{18,... | collective-permute-start | bytes 393224 | tf_op jit(solution)/shard_map/ppermute | solution.py:629
  19.0 6.2 %copy-start = (f32[2,30,30,128]{3,0,2,1:T(2,128)S(1)}, f32[2,30,30,128]{3,0,2,1:T(2,128)}, u32[]{:S(2)}) copy-start(f32[2,30,30,128]{3,0,2,1:T(2,128)} %param.12) | copy-start | bytes 2764804
  19.0 6.2 %copy-start.1 = (s32[30,30,128]{2,1,0:T(8,128)S(1)}, s32[30,30,128]{2,1,0:T(8,128)}, u32[]{:S(2)}) copy-start(s32[30,30,128]{2,1,0:T(8,128)} %cover_ref.5) | copy-start | bytes 1382404
  19.0 6.2 %copy-start.2 = (f32[30,30,128]{2,1,0:T(8,128)S(1)}, f32[30,30,128]{2,1,0:T(8,128)}, u32[]{:S(2)}) copy-start(f32[30,30,128]{2,1,0:T(8,128)} %strength_ref.5) | copy-start | bytes 1382404
  19.0 6.2 %copy-start.3 = (f32[30,30,128]{2,1,0:T(8,128)S(1)}, f32[30,30,128]{2,1,0:T(8,128)}, u32[]{:S(2)}) copy-start(f32[30,30,128]{2,1,0:T(8,128)} %mass_ref.5) | copy-start | bytes 1382404
  19.7 5.7 %copy-start.6 = (f32[2,4,32,128]{3,2,1,0:T(8,128)S(1)}, f32[2,4,32,128]{3,2,1,0:T(8,128)}, u32[]{:S(2)}) copy-start(f32[2,4,32,128]{3,2,1,0:T(8,128)} %shard_map.131.outer_ref) | copy-start | bytes 393220
  19.8 5.7 %copy-start.7 = (s32[4,128]{1,0:T(4,128)S(1)}, s32[4,128]{1,0:T(4,128)}, u32[]{:S(2)}) copy-start(s32[4,128]{1,0:T(4,128)} %neighbour_ref.7) | copy-start | bytes 6148
  19.8 5.7 %copy-start.8 = (s32[4,128]{1,0:T(4,128)S(1)}, s32[4,128]{1,0:T(4,128)}, u32[]{:S(2)}) copy-start(s32[4,128]{1,0:T(4,128)} %turn_ref.7) | copy-start | bytes 6148
  19.8 15.7 %all-to-all-start = ((f32[64,2,256]{2,1,0:T(2,128)}), f32[64,2,256]{2,1,0:T(2,128)S(1)}, u32[]{:S(2)}, u32[]{:S(2)}) async-start(f32[64,2,256]{2,1,0:T(2,128)} %shard_map.134.summed_ref), calls=%async_computation | async-start | bytes 262144 | tf_op jit(solution)/shard_map/all_to_all | solution.py:668
  25.5 10.0 %copy-start.10 = (s32[64,1,256]{2,1,0:T(1,128)S(1)}, s32[64,1,256]{2,1,0:T(1,128)}, u32[]{:S(2)}) copy-start(s32[64,1,256]{2,1,0:T(1,128)} %cell_ref.5) | copy-start | bytes 196612
  25.5 10.0 %copy-start.11 = (s32[64,1]{0,1:T(1,128)S(1)}, s32[64,1]{0,1:T(1,128)}, u32[]{:S(2)}) copy-start(s32[64,1]{0,1:T(1,128)} %param.23) | copy-start | bytes 772
  26.1 15.3 %collective-permute-start.6 = (f32[2,4,32,128]{3,2,1,0:T(8,128)S(1)}, f32[2,4,32,128]{3,2,1,0:T(8,128)S(1)}, u32[]{:S(2)}, u32[]{:S(2)}) collective-permute-start(f32[2,4,32,128]{3,2,1,0:T(8,128)S(1)} %get-tuple-element.25.after_ref.own_ref.rest_0_), channel_id=1, source_target_pairs={{1,2},{3,4},{5,6},{7,8},{9,10},{11,12},{13,14},{15,16},{17,18},{19... | collective-permute-start | bytes 393224 | tf_op jit(solution)/shard_map/ppermute | solution.py:629
  26.2 15.1 %collective-permute-start.5 = (f32[2,4,32,128]{3,2,1,0:T(8,128)S(1)}, f32[2,4,32,128]{3,2,1,0:T(8,128)S(1)}, u32[]{:S(2)}, u32[]{:S(2)}) collective-permute-start(f32[2,4,32,128]{3,2,1,0:T(8,128)S(1)} %get-tuple-element.25.after_ref.own_ref.rest_0_), channel_id=1, source_target_pairs={{0,1},{2,3},{4,5},{6,7},{8,9},{10,11},{12,13},{14,15},{16,17},{18,... | collective-permute-start | bytes 393224 | tf_op jit(solution)/shard_map/ppermute | solution.py:629
  43.2 9.5 %collective-permute-start.8 = (f32[2,4,32,128]{3,2,1,0:T(8,128)S(1)}, f32[2,4,32,128]{3,2,1,0:T(8,128)S(1)}, u32[]{:S(2)}, u32[]{:S(2)}) collective-permute-start(f32[2,4,32,128]{3,2,1,0:T(8,128)S(1)} %get-tuple-element.28.outer_ref), channel_id=1, source_target_pairs={{1,2},{3,4},{5,6},{7,8},{9,10},{11,12},{13,14},{15,16},{17,18},{19... | collective-permute-start | bytes 393224 | tf_op jit(solution)/shard_map/ppermute | solution.py:629
  43.4 9.4 %collective-permute-start.7 = (f32[2,4,32,128]{3,2,1,0:T(8,128)S(1)}, f32[2,4,32,128]{3,2,1,0:T(8,128)S(1)}, u32[]{:S(2)}, u32[]{:S(2)}) collective-permute-start(f32[2,4,32,128]{3,2,1,0:T(8,128)S(1)} %get-tuple-element.28.outer_ref), channel_id=1, source_target_pairs={{0,1},{2,3},{4,5},{6,7},{8,9},{10,11},{12,13},{14,15},{16,17},{18,... | collective-permute-start | bytes 393224 | tf_op jit(solution)/shard_map/ppermute | solution.py:629
  53.3 14.0 %collective-permute-start.10 = (f32[2,4,32,128]{3,2,1,0:T(8,128)S(1)}, f32[2,4,32,128]{3,2,1,0:T(8,128)S(1)}, u32[]{:S(2)}, u32[]{:S(2)}) collective-permute-start(f32[2,4,32,128]{3,2,1,0:T(8,128)S(1)} %get-tuple-element.30.own_ref), channel_id=1, source_target_pairs={{1,2},{3,4},{5,6},{7,8},{9,10},{11,12},{13,14},{15,16},{17,18},{19... | collective-permute-start | bytes 393224 | tf_op jit(solution)/shard_map/ppermute | solution.py:629
  54.9 12.4 %collective-permute-start.9 = (f32[2,4,32,128]{3,2,1,0:T(8,128)S(1)}, f32[2,4,32,128]{3,2,1,0:T(8,128)S(1)}, u32[]{:S(2)}, u32[]{:S(2)}) collective-permute-start(f32[2,4,32,128]{3,2,1,0:T(8,128)S(1)} %get-tuple-element.30.own_ref), channel_id=1, source_target_pairs={{0,1},{2,3},{4,5},{6,7},{8,9},{10,11},{12,13},{14,15},{16,17},{18,... | collective-permute-start | bytes 393224 | tf_op jit(solution)/shard_map/ppermute | solution.py:629
